TPU v7x, 32 devices: a whole 2x2x4 slice. The times are simulated.
32 devices in a mesh: span: 16 (over z, y, x), col: 2 (over core).
Axes of the slice: x: 2, y: 2, z: 4, core: 2. Of those that a mesh axis runs over, the one named last changes fastest.
Arguments:
- adjoint_field: float32 [3, 128, 16, 256], P(None, 'span', None, 'col'), may hold values from -6 to 6
- base_flow: float32 [3, 128, 16, 256], P(None, 'span', None, 'col'), may hold values from -5 to 5
- metric_diag: bfloat16 [3, 128, 16, 256], P(None, 'span', None, 'col'), may hold values from 1 to 2
- metric_cross: bfloat16 [3, 128, 16, 256], P(None, 'span', None, 'col'), may hold values from -0.44921875 to 0.44921875
- jacobian: float32 [128, 16, 256], P('span', None, 'col'), may hold values from 0.5 to 2
Outputs:
- advanced: float32 [3, 128, 16, 256], P(None, 'span', None, 'col')
All inputs are finite; a program needn't handle non-finite values.
Results may differ from a plain program's by a relative error of at most 0.0003.
Values sent between devices are 32-bit elements; how exact they have to be, the bound alone decides.
No kernel may reach another device: no remote copies, remote signals or barrier semaphores. Data moves between devices by JAX's collectives and lax.ppermute only.
A program may use at most 64 MiB of HBM per device.

v0:
```python
import jax
import jax.numpy as jnp
import numpy as np
from jax import lax
from jax.sharding import PartitionSpec as P

HIGH = lax.Precision.HIGHEST
VISCOSITY = 0.05
STEP_SIZE = 0.01
GLL_INNER = [
    -0.8717401485096066,
    -0.5917001814331423,
    -0.2092992179024789,
    0.2092992179024789,
    0.5917001814331423,
    0.8717401485096066,
]
GAUSS_POINTS = [
    -0.9815606342467192,
    -0.9041172563704749,
    -0.7699026741943047,
    -0.5873179542866175,
    -0.3678314989981802,
    -0.1252334085114689,
    0.1252334085114689,
    0.3678314989981802,
    0.5873179542866175,
    0.7699026741943047,
    0.9041172563704749,
    0.9815606342467192,
]
GAUSS_WEIGHTS = [
    0.0471753363865118,
    0.1069393259953184,
    0.1600783285433462,
    0.2031674267230659,
    0.2334925365383548,
    0.2491470458134028,
    0.2491470458134028,
    0.2334925365383548,
    0.2031674267230659,
    0.1600783285433462,
    0.1069393259953184,
    0.0471753363865118,
]


def padded_2(block, sides, width, periodic):
    for axis, dim in sides:
        count = lax.axis_size(axis)
        forward = [(i, i + 1) for i in range(count - 1)]
        if periodic:
            forward.append((count - 1, 0))
        backward = [(target, source) for source, target in forward]
        low = lax.ppermute(
            lax.slice_in_dim(block, block.shape[dim] - width, None, axis=dim), axis, forward
        )
        high = lax.ppermute(lax.slice_in_dim(block, 0, width, axis=dim), axis, backward)
        block = jnp.concatenate([low, block, high], axis=dim)
    return block


def legendre_seven(points):
    previous = points * 0.0 + 1.0
    current = points
    for degree in range(1, 7):
        following = ((2.0 * degree + 1.0) * points * current - degree * previous) / (degree + 1.0)
        previous = current
        current = following
    return current


def node_tables():
    gll_nodes = np.array([-1.0] + GLL_INNER + [1.0])
    values = legendre_seven(gll_nodes)
    node_weights = 2.0 / (56.0 * values * values)
    identity = np.eye(8, dtype=bool)
    spacing = gll_nodes[:, None] - gll_nodes[None, :]
    derivative = np.where(
        identity, 0.0, values[:, None] / (values[None, :] * np.where(identity, 1.0, spacing))
    )
    corner_terms = np.concatenate([np.array([-14.0]), np.zeros(6), np.array([14.0])])
    derivative = derivative + np.eye(8) * corner_terms[None, :]
    gauss_nodes = np.array(GAUSS_POINTS)
    gauss_weights = np.array(GAUSS_WEIGHTS)
    numerators = gauss_nodes[:, None, None] - gll_nodes[None, None, :]
    denominators = np.where(identity, 1.0, spacing)[None]
    ratios = np.where(identity[None], 1.0, numerators / denominators)
    interpolation = ratios.prod(axis=2)
    slope_interp = interpolation @ derivative
    return (derivative, node_weights, interpolation, slope_interp, gauss_weights)


def float_tables():
    return tuple((jnp.asarray(member, jnp.float32) for member in node_tables()))


def along_first(vector, matrix):
    leading, first_len, second_len, third_len = vector.shape
    columns = matrix.shape[1]
    blocks = vector.reshape(leading, first_len // columns, columns, second_len, third_len)
    result = jnp.einsum("pi,laimz->lapmz", matrix, blocks, precision=HIGH)
    return result.reshape(leading, -1, second_len, third_len)


def along_second(vector, matrix):
    leading, first_len, second_len, third_len = vector.shape
    columns = matrix.shape[1]
    blocks = vector.reshape(leading, first_len, second_len // columns, columns, third_len)
    result = jnp.einsum("pi,lxaiz->lxapz", matrix, blocks, precision=HIGH)
    return result.reshape(leading, first_len, -1, third_len)


def along_third(vector, matrix, group_size):
    leading, first_len, second_len, third_len = vector.shape
    columns = matrix.shape[1]
    kron_table = jnp.kron(jnp.eye(group_size, dtype=jnp.float32), matrix.T)
    blocks = vector.reshape(
        leading, first_len, second_len, third_len // (group_size * columns), group_size * columns
    )
    result = jnp.einsum("lxyzk,kq->lxyzq", blocks, kron_table, precision=HIGH)
    return result.reshape(leading, first_len, second_len, -1)


def interpolate(vector, matrix, group_size):
    return along_third(along_second(along_first(vector, matrix), matrix), matrix, group_size)


def weight_grid(weights, extent):
    nodes_per = weights.shape[0]
    first_axis = jnp.tile(weights, extent[0] // nodes_per)
    second_axis = jnp.tile(weights, extent[1] // nodes_per)
    third_axis = jnp.tile(weights, extent[2] // nodes_per)
    return first_axis[:, None, None] * second_axis[None, :, None] * third_axis[None, None, :]


def transposed_operator(vector, velocity_fine, metric_diag, metric_cross, group_size, tables):
    derivative, node_weights, interpolation, slope_interp, gauss_weights = tables
    grad_first = along_first(vector, derivative)
    grad_second = along_second(vector, derivative)
    grad_third = along_third(vector, derivative, group_size)
    scaled = VISCOSITY * weight_grid(node_weights, vector.shape[1:])
    flux_first = scaled * (
        metric_diag[0] * grad_first + metric_cross[0] * grad_second + metric_cross[1] * grad_third
    )
    flux_second = scaled * (
        metric_cross[0] * grad_first + metric_diag[1] * grad_second + metric_cross[2] * grad_third
    )
    flux_third = scaled * (
        metric_cross[1] * grad_first + metric_cross[2] * grad_second + metric_diag[2] * grad_third
    )
    stiffness = (
        along_first(flux_first, derivative.T)
        + along_second(flux_second, derivative.T)
        + along_third(flux_third, derivative.T, group_size)
    )
    fine_field = interpolate(vector, interpolation, group_size)
    weighted = fine_field * weight_grid(gauss_weights, fine_field.shape[1:])
    back_first = along_first(
        along_second(
            along_third(velocity_fine[0] * weighted, interpolation.T, group_size), interpolation.T
        ),
        slope_interp.T,
    )
    back_second = along_first(
        along_second(
            along_third(velocity_fine[1] * weighted, interpolation.T, group_size), slope_interp.T
        ),
        interpolation.T,
    )
    back_third = along_first(
        along_second(
            along_third(velocity_fine[2] * weighted, slope_interp.T, group_size), interpolation.T
        ),
        interpolation.T,
    )
    return stiffness + back_first + back_second + back_third


def add_partners(padded, which_axis):
    nodes_along = padded.shape[which_axis] - 2
    middle_part = lax.slice_in_dim(padded, 1, nodes_along + 1, axis=which_axis)
    next_part = lax.slice_in_dim(padded, 2, nodes_along + 2, axis=which_axis)
    before = lax.slice_in_dim(padded, 0, nodes_along, axis=which_axis)
    position = (jnp.arange(nodes_along) % 8).reshape(
        tuple((nodes_along if dimension == which_axis else 1 for dimension in range(padded.ndim)))
    )
    return (
        middle_part
        + jnp.where(position == 7, next_part, 0.0)
        + jnp.where(position == 0, before, 0.0)
    )


def wrap_second(vector):
    return add_partners(jnp.concatenate([vector[:, :, -1:], vector, vector[:, :, :1]], axis=2), 2)


def assemble(vector):
    streamwise = add_partners(padded_2(vector, (("span", 1),), 1, True), 1)
    summed = add_partners(padded_2(streamwise, (("col", 3),), 1, False), 3)
    return wrap_second(summed)


def local(adjoint_field, base_flow, metric_diag, metric_cross, jacobian):
    tables = float_tables()
    planes = jacobian.shape[2]
    group_size = min(planes // 8, 16)
    velocity_fine = interpolate(base_flow, tables[2], group_size)
    first_term = transposed_operator(
        adjoint_field, velocity_fine, metric_diag, metric_cross, group_size, tables
    )
    mass_terms = jacobian * weight_grid(tables[1], jacobian.shape)
    assembled = assemble(jnp.concatenate([first_term, mass_terms[None]], axis=0))
    inverse_mass = 1.0 / assembled[3]
    total_planes = planes * lax.axis_size("col")
    global_plane = lax.axis_index("col") * planes + jnp.arange(planes)
    interior = ((global_plane > 0) & (global_plane < total_planes - 1)).astype(jnp.float32)
    half_state = interior * (adjoint_field - 0.5 * STEP_SIZE * inverse_mass * assembled[:3])
    second_term = assemble(
        transposed_operator(
            half_state, velocity_fine, metric_diag, metric_cross, group_size, tables
        )
    )
    return interior * (adjoint_field - STEP_SIZE * inverse_mass * second_term)


def solution(mesh):
    in_specs = (
        P(None, "span", None, "col"),
        P(None, "span", None, "col"),
        P(None, "span", None, "col"),
        P(None, "span", None, "col"),
        P("span", None, "col"),
    )
    out_specs = P(None, "span", None, "col")
    return jax.shard_map(local, mesh=mesh, in_specs=in_specs, out_specs=out_specs, check_vma=False)
```

profile of v0, /device:TPU:0, one launch (start us, length us, event | category | flops | bytes accessed | tf_op | source)
XLA Modules:
  0.0 89.3 jit_solution(12474549294954193757)
XLA Ops:
  1.5 1.3 %broadcast_multiply_fusion.12 = f32[12,24]{1,0:T(8,128)} fusion(f32[24]{0:T(128)S(1)} %mul.721, f32[12]{0:T(128)} %constant.82.clone), kind=kLoop, calls=%fused_computation.198 | loop fusion | flops 288 | bytes 1296 | tf_op jit(solution)/shard_map/mul | solution.py:134
  5.2 1.3 %convolution_bitcast_fusion.23 = f32[3,8,16,128]{3,1,2,0:T(8,128)S(1)} fusion(f32[8,8,1,1]{1,0,3,2:T(8,128)} %constant.90, f32[3,8,16,128]{3,2,1,0:T(8,128)} %param.10), kind=kOutput, calls=%fused_computation.35 | convolution fusion | flops 4718592 | bytes 393472 | tf_op jit(solution)/shard_map/pi,laimz->lapmz/dot_general | solution.py:102
  6.5 1.4 %convolution_bitcast_fusion.22 = f32[3,8,2,8,128]{4,3,2,1,0:T(8,128)S(1)} fusion(f32[8,8,1,1,1]{1,0,4,3,2:T(8,128)} %constant.91, f32[3,8,16,128]{3,2,1,0:T(8,128)} %param.10), kind=kOutput, calls=%fused_computation.34 | convolution fusion | flops 4718592 | bytes 393472 | tf_op jit(solution)/shard_map/pi,lxaiz->lxapz/dot_general | solution.py:110
  20.8 1.1 %reshape.478 = f32[192,128,1,1,1]{0,1,2,3,4:T(8,128)} reshape(f32[16,12,16,8]{1,0,3,2:T(8,128)S(1)} %get-tuple-element.36) | data formatting | bytes 196608 | tf_op jit(solution)/shard_map/jit(kron)/mul | solution.py:117
  22.8 3.1 %broadcast_multiply_fusion.6 = (f32[3,12,24,192]{3,2,1,0:T(8,128)S(1)}, f32[3,12,24,192]{3,2,1,0:T(8,128)S(1)}, f32[3,12,24,192]{3,2,1,0:T(8,128)}) fusion(f32[12,24,192]{2,1,0:T(8,128)} %get-tuple-element.11, f32[12,24,192]{2,1,0:T(8,128)} %get-tuple-element.12, f32[12,24,192]{2,1,0:T(8,128)} %get-tuple-element.13, ...), kind=kOutput, calls=%fused_computation.42 | convolution fusion | flops 255467520 | bytes 3416064 | tf_op jit(solution)/shard_map/lxyzk,kq->lxyzq/dot_general | solution.py:121
  26.0 2.0 %fusion.82 = f32[3,12,2,12,128]{4,3,2,1,0:T(8,128)S(1)} fusion(f32[3,12,2,12,192]{4,3,2,1,0:T(8,128)S(1)} %dot_general.184, f32[192,128,1,1,1]{0,1,2,3,4:T(8,128)} %reshape.478), kind=kOutput, calls=%fused_computation.147 | convolution fusion | flops 254803968 | bytes 1204224 | tf_op jit(solution)/shard_map/lxyzk,kq->lxyzq/dot_general | solution.py:121
  28.0 1.2 %convolution_bitcast_fusion.6 = f32[3,12,16,128]{3,2,1,0:T(8,128)} fusion(f32[3,12,2,12,128]{4,3,2,1,0:T(8,128)S(1)} %fusion.82, f32[12,8,1,1,1]{0,1,4,3,2:T(8,128)S(1)} %copy-done.33), kind=kOutput, calls=%fused_computation.8 | convolution fusion | flops 10616832 | bytes 737664 | tf_op jit(solution)/shard_map/pi,lxaiz->lxapz/dot_general | solution.py:110
  29.2 1.3 %dot_general.174 = f32[3,12,2,12,192]{4,3,2,1,0:T(8,128)S(1)} reshape(f32[3,12,24,192]{3,2,1,0:T(8,128)} %get-tuple-element.10) | data formatting | bytes 1327104 | tf_op jit(solution)/shard_map/lxyzk,kq->lxyzq/dot_general | solution.py:121
  31.6 1.3 %fusion.90 = f32[3,12,2,12,128]{4,3,2,1,0:T(8,128)S(1)} fusion(f32[3,12,2,12,192]{4,3,2,1,0:T(8,128)S(1)} %dot_general.174, f32[192,128,1,1,1]{0,1,2,3,4:T(8,128)S(1)} %reshape.475), kind=kOutput, calls=%fused_computation.155 | convolution fusion | flops 254803968 | bytes 1204224 | tf_op jit(solution)/shard_map/lxyzk,kq->lxyzq/dot_general | solution.py:121
  36.5 7.0 %collective-permute-start = (f32[4,1,16,128]{3,1,2,0:T(1,128)S(1)}, f32[4,1,16,128]{3,1,2,0:T(1,128)S(1)}, u32[]{:S(2)}, u32[]{:S(2)}) collective-permute-start(f32[4,1,16,128]{3,1,2,0:T(1,128)S(1)} %get-tuple-element.20), channel_id=1, source_target_pairs={{2,0},{4,2},{6,4},{8,6},{10,8},{12,10},{14,12},{16,14},{18,16},{20... | collective-permute-start | bytes 98312 | tf_op jit(solution)/shard_map/ppermute | solution.py:58
  43.6 1.5 %collective-permute-done = f32[4,1,16,128]{3,1,2,0:T(1,128)S(1)} collective-permute-done((f32[4,1,16,128]{3,1,2,0:T(1,128)S(1)}, f32[4,1,16,128]{3,1,2,0:T(1,128)S(1)}, u32[]{:S(2)}, u32[]{:S(2)}) %collective-permute-start) | collective-permute-done | bytes 32800 | tf_op jit(solution)/shard_map/ppermute | solution.py:58
  45.1 5.9 %collective-permute-done.1 = f32[4,1,16,128]{3,1,2,0:T(1,128)S(1)} collective-permute-done((f32[4,1,16,128]{3,1,2,0:T(1,128)S(1)}, f32[4,1,16,128]{3,1,2,0:T(1,128)S(1)}, u32[]{:S(2)}, u32[]{:S(2)}) %collective-permute-start.1) | collective-permute-done | bytes 32800 | tf_op jit(solution)/shard_map/ppermute | solution.py:55
  51.2 1.3 %collective-permute-start.2 = (f32[4,8,16,1]{3,1,2,0:T(8,128)S(1)}, f32[4,8,16,1]{3,1,2,0:T(8,128)S(1)}, u32[]{:S(2)}, u32[]{:S(2)}) collective-permute-start(f32[4,8,16,1]{3,1,2,0:T(8,128)S(1)} %get-tuple-element.18), channel_id=1, source_target_pairs={{1,0},{3,2},{5,4},{7,6},{9,8},{11,10},{13,12},{15,14},{17,16},{19,... | collective-permute-start | bytes 6152 | tf_op jit(solution)/shard_map/ppermute | solution.py:58
  52.5 3.1 %collective-permute-start.3 = (f32[4,8,16,1]{3,1,2,0:T(8,128)S(1)}, f32[4,8,16,1]{3,1,2,0:T(8,128)S(1)}, u32[]{:S(2)}, u32[]{:S(2)}) collective-permute-start(f32[4,8,16,1]{3,1,2,0:T(8,128)S(1)} %get-tuple-element.19), channel_id=1, source_target_pairs={{0,1},{2,3},{4,5},{6,7},{8,9},{10,11},{12,13},{14,15},{16,17},{18,... | collective-permute-start | bytes 6152 | tf_op jit(solution)/shard_map/ppermute | solution.py:55
  55.6 1.1 %collective-permute-done.3 = f32[4,8,16,1]{3,1,2,0:T(8,128)S(1)} collective-permute-done((f32[4,8,16,1]{3,1,2,0:T(8,128)S(1)}, f32[4,8,16,1]{3,1,2,0:T(8,128)S(1)}, u32[]{:S(2)}, u32[]{:S(2)}) %collective-permute-start.3) | collective-permute-done | bytes 2080 | tf_op jit(solution)/shard_map/ppermute | solution.py:55
  62.8 2.8 %broadcast_multiply_fusion.5 = (f32[3,12,24,192]{3,2,1,0:T(8,128)}, f32[3,12,24,192]{3,2,1,0:T(8,128)S(1)}, f32[3,12,24,192]{3,2,1,0:T(8,128)S(1)}) fusion(f32[12,24,192]{2,1,0:T(8,128)S(1)} %copy-done.6, f32[12,24,192]{2,1,0:T(8,128)S(1)} %copy-done.7, f32[12,24,192]{2,1,0:T(8,128)S(1)} %copy-done.8, f32[12,24,192]{2,1,0:T(8,128)S(1)} %copy-done.10, ...), kind=kOutput, calls=%fused_computation.41 | convolution fusion | flops 255467520 | bytes 3416064 | tf_op jit(solution)/shard_map/lxyzk,kq->lxyzq/dot_general | solution.py:121
  65.6 1.3 %dot_general.211 = f32[3,12,2,12,192]{4,3,2,1,0:T(8,128)S(1)} reshape(f32[3,12,24,192]{3,2,1,0:T(8,128)} %get-tuple-element.5) | data formatting | bytes 1327104 | tf_op jit(solution)/shard_map/lxyzk,kq->lxyzq/dot_general | solution.py:121
  66.9 2.0 %fusion.80 = f32[3,12,2,12,128]{4,3,2,1,0:T(8,128)S(1)} fusion(f32[3,12,2,12,192]{4,3,2,1,0:T(8,128)S(1)} %dot_general.211, f32[192,128,1,1,1]{0,1,2,3,4:T(8,128)} %reshape.478), kind=kOutput, calls=%fused_computation.145 | convolution fusion | flops 254803968 | bytes 1204224 | tf_op jit(solution)/shard_map/lxyzk,kq->lxyzq/dot_general | solution.py:121
  68.9 1.2 %convolution_bitcast_fusion.3 = f32[3,12,16,128]{3,2,1,0:T(8,128)} fusion(f32[3,12,2,12,128]{4,3,2,1,0:T(8,128)S(1)} %fusion.80, f32[12,8,1,1,1]{0,1,4,3,2:T(8,128)S(1)} %copy-done.33), kind=kOutput, calls=%fused_computation.5 | convolution fusion | flops 10616832 | bytes 737664 | tf_op jit(solution)/shard_map/pi,lxaiz->lxapz/dot_general | solution.py:110
  75.1 2.0 %collective-permute-start.5 = (f32[3,1,16,128]{3,1,2,0:T(1,128)S(1)}, f32[3,1,16,128]{3,1,2,0:T(1,128)S(1)}, u32[]{:S(2)}, u32[]{:S(2)}) collective-permute-start(f32[3,1,16,128]{3,1,2,0:T(1,128)S(1)} %get-tuple-element.27), channel_id=1, source_target_pairs={{0,2},{2,4},{4,6},{6,8},{8,10},{10,12},{12,14},{14,16},{16,18},{18... | collective-permute-start | bytes 73736 | tf_op jit(solution)/shard_map/ppermute | solution.py:55
  77.1 1.8 %collective-permute-done.4 = f32[3,1,16,128]{3,1,2,0:T(1,128)S(1)} collective-permute-done((f32[3,1,16,128]{3,1,2,0:T(1,128)S(1)}, f32[3,1,16,128]{3,1,2,0:T(1,128)S(1)}, u32[]{:S(2)}, u32[]{:S(2)}) %collective-permute-start.4) | collective-permute-done | bytes 24608 | tf_op jit(solution)/shard_map/ppermute | solution.py:58
  78.9 3.7 %collective-permute-done.5 = f32[3,1,16,128]{3,1,2,0:T(1,128)S(1)} collective-permute-done((f32[3,1,16,128]{3,1,2,0:T(1,128)S(1)}, f32[3,1,16,128]{3,1,2,0:T(1,128)S(1)}, u32[]{:S(2)}, u32[]{:S(2)}) %collective-permute-start.5) | collective-permute-done | bytes 24608 | tf_op jit(solution)/shard_map/ppermute | solution.py:55
  82.8 1.3 %collective-permute-start.6 = (f32[3,8,16,1]{3,1,2,0:T(8,128)S(1)}, f32[3,8,16,1]{3,1,2,0:T(8,128)S(1)}, u32[]{:S(2)}, u32[]{:S(2)}) collective-permute-start(f32[3,8,16,1]{3,1,2,0:T(8,128)S(1)} %get-tuple-element.24), channel_id=1, source_target_pairs={{1,0},{3,2},{5,4},{7,6},{9,8},{11,10},{13,12},{15,14},{17,16},{19,... | collective-permute-start | bytes 4616 | tf_op jit(solution)/shard_map/ppermute | solution.py:58
  84.1 3.0 %collective-permute-start.7 = (f32[3,8,16,1]{3,1,2,0:T(8,128)S(1)}, f32[3,8,16,1]{3,1,2,0:T(8,128)S(1)}, u32[]{:S(2)}, u32[]{:S(2)}) collective-permute-start(f32[3,8,16,1]{3,1,2,0:T(8,128)S(1)} %get-tuple-element.25), channel_id=1, source_target_pairs={{0,1},{2,3},{4,5},{6,7},{8,9},{10,11},{12,13},{14,15},{16,17},{18,... | collective-permute-start | bytes 4616 | tf_op jit(solution)/shard_map/ppermute | solution.py:55
  (218 shorter events, 35.4 us)
Async XLA Ops:
  0.0 10.6 %copy-start = (f32[3,8,16,128]{3,2,1,0:T(8,128)S(1)}, f32[3,8,16,128]{3,2,1,0:T(8,128)}, u32[]{:S(2)}) copy-start(f32[3,8,16,128]{3,2,1,0:T(8,128)} %param.11) | copy-start | bytes 589828
  0.0 9.3 %copy-start.35 = (bf16[3,8,16,128]{3,2,1,0:T(8,128)(2,1)S(1)}, bf16[3,8,16,128]{3,2,1,0:T(8,128)(2,1)}, u32[]{:S(2)}) copy-start(bf16[3,8,16,128]{3,2,1,0:T(8,128)(2,1)} %param.13) | copy-start | bytes 294916
  6.4 12.0 %copy-start.2 = (f32[3,8,16,128]{3,1,2,0:T(8,128)}, f32[3,8,16,128]{3,1,2,0:T(8,128)S(1)}, u32[]{:S(2)}) copy-start(f32[3,8,16,128]{3,1,2,0:T(8,128)S(1)} %convolution_bitcast_fusion.23) | copy-start | bytes 589828
  7.9 10.5 %copy-start.4 = (f32[3,8,2,8,128]{4,1,3,2,0:T(8,128)}, f32[3,8,2,8,128]{4,1,3,2,0:T(8,128)S(1)}, u32[]{:S(2)}) copy-start(f32[3,8,2,8,128]{4,1,3,2,0:T(8,128)S(1)} %copy.60) | copy-start | bytes 589828
  9.3 9.1 %copy-start.29 = (f32[8,16,128]{2,0,1:T(8,128)}, f32[8,16,128]{2,0,1:T(8,128)S(1)}, u32[]{:S(2)}) copy-start(f32[8,16,128]{2,0,1:T(8,128)S(1)} %copy.65) | copy-start | bytes 196612
  36.5 8.6 %collective-permute-start = (f32[4,1,16,128]{3,1,2,0:T(1,128)S(1)}, f32[4,1,16,128]{3,1,2,0:T(1,128)S(1)}, u32[]{:S(2)}, u32[]{:S(2)}) collective-permute-start(f32[4,1,16,128]{3,1,2,0:T(1,128)S(1)} %get-tuple-element.20), channel_id=1, source_target_pairs={{2,0},{4,2},{6,4},{8,6},{10,8},{12,10},{14,12},{16,14},{18,16},{20... | collective-permute-start | bytes 98312 | tf_op jit(solution)/shard_map/ppermute | solution.py:58
  43.5 7.5 %collective-permute-start.1 = (f32[4,1,16,128]{3,1,2,0:T(1,128)S(1)}, f32[4,1,16,128]{3,1,2,0:T(1,128)S(1)}, u32[]{:S(2)}, u32[]{:S(2)}) collective-permute-start(f32[4,1,16,128]{3,1,2,0:T(1,128)S(1)} %get-tuple-element.21), channel_id=1, source_target_pairs={{0,2},{2,4},{4,6},{6,8},{8,10},{10,12},{12,14},{14,16},{16,18},{18... | collective-permute-start | bytes 98312 | tf_op jit(solution)/shard_map/ppermute | solution.py:55
  43.5 13.5 %copy-start.48 = (pred[128]{0:T(512)(128)(4,1)}, pred[128]{0:T(512)(128)(4,1)S(1)}, u32[]{:S(2)}) copy-start(pred[128]{0:T(512)(128)(4,1)S(1)} %get-tuple-element.46) | copy-start | bytes 388
  43.5 13.5 %copy-start.50 = (pred[128]{0:T(512)(128)(4,1)}, pred[128]{0:T(512)(128)(4,1)S(1)}, u32[]{:S(2)}) copy-start(pred[128]{0:T(512)(128)(4,1)S(1)} %get-tuple-element.47) | copy-start | bytes 388
  43.5 13.5 %copy-start.56 = (pred[16]{0:T(512)(128)(4,1)}, pred[16]{0:T(512)(128)(4,1)S(1)}, u32[]{:S(2)}) copy-start(pred[16]{0:T(512)(128)(4,1)S(1)} %get-tuple-element.48) | copy-start | bytes 52
  43.5 13.5 %copy-start.58 = (pred[16]{0:T(512)(128)(4,1)}, pred[16]{0:T(512)(128)(4,1)S(1)}, u32[]{:S(2)}) copy-start(pred[16]{0:T(512)(128)(4,1)S(1)} %get-tuple-element.49) | copy-start | bytes 52
  51.2 4.4 %collective-permute-start.2 = (f32[4,8,16,1]{3,1,2,0:T(8,128)S(1)}, f32[4,8,16,1]{3,1,2,0:T(8,128)S(1)}, u32[]{:S(2)}, u32[]{:S(2)}) collective-permute-start(f32[4,8,16,1]{3,1,2,0:T(8,128)S(1)} %get-tuple-element.18), channel_id=1, source_target_pairs={{1,0},{3,2},{5,4},{7,6},{9,8},{11,10},{13,12},{15,14},{17,16},{19,... | collective-permute-start | bytes 6152 | tf_op jit(solution)/shard_map/ppermute | solution.py:58
  52.5 4.2 %collective-permute-start.3 = (f32[4,8,16,1]{3,1,2,0:T(8,128)S(1)}, f32[4,8,16,1]{3,1,2,0:T(8,128)S(1)}, u32[]{:S(2)}, u32[]{:S(2)}) collective-permute-start(f32[4,8,16,1]{3,1,2,0:T(8,128)S(1)} %get-tuple-element.19), channel_id=1, source_target_pairs={{0,1},{2,3},{4,5},{6,7},{8,9},{10,11},{12,13},{14,15},{16,17},{18,... | collective-permute-start | bytes 6152 | tf_op jit(solution)/shard_map/ppermute | solution.py:55
  73.5 9.1 %copy-start.53 = (pred[8]{0:T(512)(128)(4,1)S(1)}, pred[8]{0:T(512)(128)(4,1)}, u32[]{:S(2)}) copy-start(pred[8]{0:T(512)(128)(4,1)} %copy-done.52) | copy-start | bytes 28
  74.4 13.8 %copy-start.49 = (pred[128]{0:T(512)(128)(4,1)S(1)}, pred[128]{0:T(512)(128)(4,1)}, u32[]{:S(2)}) copy-start(pred[128]{0:T(512)(128)(4,1)} %copy-done.48) | copy-start | bytes 388
  74.4 13.8 %copy-start.51 = (pred[128]{0:T(512)(128)(4,1)S(1)}, pred[128]{0:T(512)(128)(4,1)}, u32[]{:S(2)}) copy-start(pred[128]{0:T(512)(128)(4,1)} %copy-done.50) | copy-start | bytes 388
  74.9 13.5 %copy-start.31 = (f32[8,16,128]{2,0,1:T(8,128)S(1)}, f32[8,16,128]{2,0,1:T(8,128)}, u32[]{:S(2)}) copy-start(f32[8,16,128]{2,0,1:T(8,128)} %get-tuple-element.14) | copy-start | bytes 196612
  74.9 13.5 %copy-start.57 = (pred[16]{0:T(512)(128)(4,1)S(1)}, pred[16]{0:T(512)(128)(4,1)}, u32[]{:S(2)}) copy-start(pred[16]{0:T(512)(128)(4,1)} %copy-done.56) | copy-start | bytes 52
  74.9 13.5 %copy-start.59 = (pred[16]{0:T(512)(128)(4,1)S(1)}, pred[16]{0:T(512)(128)(4,1)}, u32[]{:S(2)}) copy-start(pred[16]{0:T(512)(128)(4,1)} %copy-done.58) | copy-start | bytes 52
  74.9 13.5 %copy-start.61 = (f32[128]{0:T(128)S(1)}, f32[128]{0:T(128)}, u32[]{:S(2)}) copy-start(f32[128]{0:T(128)} %copy-done.60) | copy-start | bytes 1540
  75.0 3.9 %collective-permute-start.4 = (f32[3,1,16,128]{3,1,2,0:T(1,128)S(1)}, f32[3,1,16,128]{3,1,2,0:T(1,128)S(1)}, u32[]{:S(2)}, u32[]{:S(2)}) collective-permute-start(f32[3,1,16,128]{3,1,2,0:T(1,128)S(1)} %get-tuple-element.26), channel_id=1, source_target_pairs={{2,0},{4,2},{6,4},{8,6},{10,8},{12,10},{14,12},{16,14},{18,16},{20... | collective-permute-start | bytes 73736 | tf_op jit(solution)/shard_map/ppermute | solution.py:58
  75.1 7.5 %collective-permute-start.5 = (f32[3,1,16,128]{3,1,2,0:T(1,128)S(1)}, f32[3,1,16,128]{3,1,2,0:T(1,128)S(1)}, u32[]{:S(2)}, u32[]{:S(2)}) collective-permute-start(f32[3,1,16,128]{3,1,2,0:T(1,128)S(1)} %get-tuple-element.27), channel_id=1, source_target_pairs={{0,2},{2,4},{4,6},{6,8},{8,10},{10,12},{12,14},{14,16},{16,18},{18... | collective-permute-start | bytes 73736 | tf_op jit(solution)/shard_map/ppermute | solution.py:55
  82.8 4.4 %collective-permute-start.6 = (f32[3,8,16,1]{3,1,2,0:T(8,128)S(1)}, f32[3,8,16,1]{3,1,2,0:T(8,128)S(1)}, u32[]{:S(2)}, u32[]{:S(2)}) collective-permute-start(f32[3,8,16,1]{3,1,2,0:T(8,128)S(1)} %get-tuple-element.24), channel_id=1, source_target_pairs={{1,0},{3,2},{5,4},{7,6},{9,8},{11,10},{13,12},{15,14},{17,16},{19,... | collective-permute-start | bytes 4616 | tf_op jit(solution)/shard_map/ppermute | solution.py:58
  84.1 4.1 %collective-permute-start.7 = (f32[3,8,16,1]{3,1,2,0:T(8,128)S(1)}, f32[3,8,16,1]{3,1,2,0:T(8,128)S(1)}, u32[]{:S(2)}, u32[]{:S(2)}) collective-permute-start(f32[3,8,16,1]{3,1,2,0:T(8,128)S(1)} %get-tuple-element.25), channel_id=1, source_target_pairs={{0,1},{2,3},{4,5},{6,7},{8,9},{10,11},{12,13},{14,15},{16,17},{18,... | collective-permute-start | bytes 4616 | tf_op jit(solution)/shard_map/ppermute | solution.py:55
  (46 other events, 113.5 us)
where the time goes:
time: 89.8 us; the launch traced here: 89.3 us
  matrix products  33.1 us (37%)
  starting transfers between devices  17.8 us (20%)
  local copies, waits for them, and re-layouts  17 us (19%)
  waiting for transfers between devices  15 us (17%)
  other arithmetic  5.19 us (6%)
  between operations  1.21 us (1%)
    dot_general x13, matrix products, along_third(): result = jnp.einsum('lxyzk,kq->lxyzq', blocks, kron_table, precision=HIGH)  17.9 us
    ppermute x4, waiting for transfers between devices, padded_2(): lax.ppermute(lax.slice_in_dim(block, block.shape[dim] - width, None, axis...  11.7 us
    ppermute x4, starting transfers between devices, padded_2(): lax.ppermute(lax.slice_in_dim(block, 0, width, axis=dim), axis, backward)  9.66 us
    dot_general x13, matrix products, along_second(): result = jnp.einsum('pi,lxaiz->lxapz', matrix, blocks, precision=HIGH)  8.56 us
    ppermute x4, starting transfers between devices, padded_2(): lax.ppermute(lax.slice_in_dim(block, block.shape[dim] - width, None, axis...  8.12 us
    dot_general x13, matrix products, along_first(): result = jnp.einsum('pi,laimz->lapmz', matrix, blocks, precision=HIGH)  6.66 us
    mul x5, local copies, waits for them, and re-layouts, along_third(): kron_table = jnp.kron(jnp.eye(group_size, dtype=jnp.float32), matrix.T)  3.68 us
    ppermute x4, waiting for transfers between devices, padded_2(): lax.ppermute(lax.slice_in_dim(block, 0, width, axis=dim), axis, backward)  3.31 us
  transfers between devices with their start and end apart: 8, of which 6 were waited for; matrix products, arithmetic and copies ran while one was open for 0% of the time, Pallas kernels for 0%

commit v1 on v0

v1 whole, which is shorter than its diff:
```python
import functools

import jax
import jax.numpy as jnp
import numpy as np
from jax import lax
from jax.experimental import pallas as pl
from jax.experimental.pallas import tpu as pltpu
from jax.sharding import PartitionSpec as P

VISCOSITY = 0.05
STEP_SIZE = 0.01
GLL_INNER = [
    -0.8717401485096066,
    -0.5917001814331423,
    -0.2092992179024789,
    0.2092992179024789,
    0.5917001814331423,
    0.8717401485096066,
]
GAUSS_POINTS = [
    -0.9815606342467192,
    -0.9041172563704749,
    -0.7699026741943047,
    -0.5873179542866175,
    -0.3678314989981802,
    -0.1252334085114689,
    0.1252334085114689,
    0.3678314989981802,
    0.5873179542866175,
    0.7699026741943047,
    0.9041172563704749,
    0.9815606342467192,
]
GAUSS_WEIGHTS = [
    0.0471753363865118,
    0.1069393259953184,
    0.1600783285433462,
    0.2031674267230659,
    0.2334925365383548,
    0.2491470458134028,
    0.2491470458134028,
    0.2334925365383548,
    0.2031674267230659,
    0.1600783285433462,
    0.1069393259953184,
    0.0471753363865118,
]
F32 = jnp.float32
BF16 = jnp.bfloat16
XY = 64
QQ = 144
LANES = 128


def legendre_seven(points):
    previous = points * 0.0 + 1.0
    current = points
    for degree in range(1, 7):
        following = ((2.0 * degree + 1.0) * points * current - degree * previous) / (degree + 1.0)
        previous = current
        current = following
    return current


def node_tables():
    gll_nodes = np.array([-1.0] + GLL_INNER + [1.0])
    values = legendre_seven(gll_nodes)
    node_weights = 2.0 / (56.0 * values * values)
    identity = np.eye(8, dtype=bool)
    spacing = gll_nodes[:, None] - gll_nodes[None, :]
    derivative = np.where(
        identity, 0.0, values[:, None] / (values[None, :] * np.where(identity, 1.0, spacing))
    )
    corner_terms = np.concatenate([np.array([-14.0]), np.zeros(6), np.array([14.0])])
    derivative = derivative + np.eye(8) * corner_terms[None, :]
    gauss_nodes = np.array(GAUSS_POINTS)
    gauss_weights = np.array(GAUSS_WEIGHTS)
    numerators = gauss_nodes[:, None, None] - gll_nodes[None, None, :]
    denominators = np.where(identity, 1.0, spacing)[None]
    ratios = np.where(identity[None], 1.0, numerators / denominators)
    interpolation = ratios.prod(axis=2)
    slope_interp = interpolation @ derivative
    return (derivative, node_weights, interpolation, slope_interp, gauss_weights)


def halves(matrix):
    high = np.asarray(matrix, np.float32).astype(jnp.bfloat16)
    low = (np.asarray(matrix, np.float64) - high.astype(np.float64)).astype(jnp.bfloat16)
    return high, low


def constants():
    dm, rho, jm, dj, sigma = node_tables()
    def forward_block(matrix):
        high, low = halves(matrix)
        return np.block([[high, low], [high, np.zeros_like(low)]])

    dz = np.kron(np.eye(16), dm.T)
    jz = np.kron(np.eye(16), jm.T)
    last = np.concatenate([jz[:, LANES:], np.zeros((LANES, 64))], axis=1)
    z_forward = np.concatenate(
        [forward_block(dz), forward_block(jz[:, :LANES]), forward_block(last)], axis=1
    )
    def three(matrix):
        high, low = halves(matrix)
        return np.concatenate([high, high, low], axis=1)

    jj = three(np.kron(jm, jm))
    eye = np.eye(8)
    grads = three(np.concatenate([np.kron(dm, eye), np.kron(eye, dm)], axis=0))
    js, ds = sigma[:, None] * jm, sigma[:, None] * dj

    def stacked(matrix):
        high, low = halves(matrix)
        return np.concatenate(
            [
                np.concatenate([high, high], axis=1),
                np.concatenate([low, np.zeros_like(low)], axis=1),
            ],
            axis=0,
        )

    back_12 = stacked(np.concatenate([np.kron(ds, js).T, np.kron(js, ds).T], axis=1))
    back_3 = stacked(np.kron(js, js).T)
    div = np.concatenate([np.kron(dm.T, eye), np.kron(eye, dm.T)], axis=1)
    div_high, div_low = halves(div)
    div = np.concatenate([div_high, div_high, div_low], axis=1)
    def back_block(matrix):
        padded = np.concatenate([matrix, np.zeros((64, LANES))], axis=0)
        high, low = halves(padded)
        return [
            np.concatenate([high, low], axis=1),
            np.concatenate([high, np.zeros_like(low)], axis=1),
        ]

    jz_back = np.kron(np.eye(16), js)
    dz_back = np.kron(np.eye(16), ds)
    z_back = np.concatenate(
        back_block(jz_back) + back_block(dz_back) + [forward_block(np.kron(np.eye(16), dm))], axis=0
    )
    weights = np.einsum("x,y,z->xyz", rho, rho, np.tile(rho, 16)).reshape(XY, LANES)
    return (
        [z_forward, jj, grads, back_12, back_3, div, z_back],
        np.asarray(weights, np.float32),
    )


def split(values):
    high = values.astype(BF16)
    low = (values - high.astype(F32)).astype(BF16)
    return high, low


def dot(left, right):
    return jnp.dot(left, right, preferred_element_type=F32)


def fold(values):
    return values[:, :LANES] + values[:, LANES : 2 * LANES]


def section_rows(block, e):
    return block.reshape(8, 2, 8, LANES)[:, e].reshape(XY, LANES)


def interpolate_wall(js_ref, first, last):
    for c in range(3):
        rows = slice(c * XY, (c + 1) * XY)
        tiles = [first[0][rows], first[1][rows]]
        tiles.append(last[0][rows] + pltpu.roll(last[1][rows], 64, 1))
        for t, tile in enumerate(tiles):
            lanes = slice((3 * c + t) * LANES, (3 * c + t + 1) * LANES)
            high, low = split(tile)
            js_ref[0:XY, lanes] = high
            js_ref[XY : 2 * XY, lanes] = low
            js_ref[2 * XY : 3 * XY, lanes] = high


def fine_flow(base_ref, tables, scratch, u_ref):
    z_forward, jj = tables[0], tables[1]
    xhl, js = scratch["xhl"], scratch["js"]
    first, last = [], []
    for e in range(2):
        for c in range(3):
            high, low = split(section_rows(base_ref[c], e))
            xhl[e, c * XY : (c + 1) * XY, :LANES] = high
            xhl[e, c * XY : (c + 1) * XY, LANES:] = low
        out = dot(xhl[e], z_forward[:, 2 * LANES :])
        first.append(fold(out[:, : 2 * LANES]))
        last.append(fold(out[:, 2 * LANES :]))
    interpolate_wall(js, first, last)
    for d in range(3):
        lanes = slice(d * 3 * LANES, (d + 1) * 3 * LANES)
        u_ref[:, lanes] = dot(jj[...], js[:, lanes])


def operator(rows_of, u_ref, metric, tables, scratch):
    z_forward, jj, grads, back_12, back_3, div, z_back = tables
    xhl, js, vs, bz, ts, hs = (scratch[k] for k in ("xhl", "js", "vs", "bz", "ts", "hs"))
    gz, first, last = [], [], []
    for e in range(2):
        for c in range(3):
            high, low = split(rows_of(c, e))
            xhl[e, c * XY : (c + 1) * XY, :LANES] = high
            xhl[e, c * XY : (c + 1) * XY, LANES:] = low
            lanes = slice((2 * c + e) * LANES, (2 * c + e + 1) * LANES)
            vs[0:XY, lanes] = high
            vs[XY : 2 * XY, lanes] = low
            vs[2 * XY : 3 * XY, lanes] = high
        out = dot(xhl[e], z_forward[...])
        gz.append(fold(out[:, : 2 * LANES]))
        first.append(fold(out[:, 2 * LANES : 4 * LANES]))
        last.append(fold(out[:, 4 * LANES :]))
    interpolate_wall(js, first, last)
    for c in range(3):
        rows = slice(c * XY, (c + 1) * XY)
        pair = slice(2 * c * LANES, 2 * (c + 1) * LANES)
        gxy = dot(grads[...], vs[:, pair])
        for e in range(2):
            lanes = slice(e * LANES, (e + 1) * LANES)
            g1, g2, g3 = gxy[:XY, lanes], gxy[XY:, lanes], gz[e][rows]
            m11, m22, m33, m12, m13, m23 = (metric[k, e] for k in range(6))
            h1 = m11 * g1 + m12 * g2 + m13 * g3
            h2 = m12 * g1 + m22 * g2 + m23 * g3
            h3 = m13 * g1 + m23 * g2 + m33 * g3
            h1h, h1l = split(h1)
            h2h, h2l = split(h2)
            h3h, h3l = split(h3)
            lanes = slice((2 * c + e) * LANES, (2 * c + e + 1) * LANES)
            for k, part in enumerate((h1h, h2h, h1l, h2l, h1h, h2h)):
                hs[k * XY : (k + 1) * XY, lanes] = part
            bz[e, rows, 8 * LANES : 9 * LANES] = h3h
            bz[e, rows, 9 * LANES :] = h3l
    for c in range(3):
        rows = slice(c * XY, (c + 1) * XY)
        fine = dot(jj[...], js[:, 3 * c * LANES : 3 * (c + 1) * LANES])
        for d in range(3):
            high, low = split(u_ref[:, 3 * d * LANES : 3 * (d + 1) * LANES] * fine)
            start = (0, QQ, 4 * QQ)[d]
            gap = (2 * QQ, 2 * QQ, QQ)[d]
            ts[start : start + QQ, :] = high
            ts[start + gap : start + gap + QQ, :] = low
        for k, (table, where) in enumerate(
            ((back_12, slice(0, 4 * QQ)), (back_3, slice(4 * QQ, 6 * QQ)))
        ):
            both = dot(table[...], ts[where, :])
            both = both[:XY] + both[XY:]
            mixed = both[:, 2 * LANES :]
            for e in range(2):
                near = both[:, e * LANES : (e + 1) * LANES]
                far = mixed if e == 0 else pltpu.roll(mixed, 64, 1)
                for t, tile in enumerate((near, far)):
                    high, low = split(tile)
                    at = (4 * k + t) * LANES
                    bz[e, rows, at : at + LANES] = high
                    bz[e, rows, at + 2 * LANES : at + 3 * LANES] = low
    spread = dot(div[...], hs[...])
    result = [[None, None] for _ in range(3)]
    for e in range(2):
        out = fold(dot(bz[e], z_back[...]))
        for c in range(3):
            lanes = slice((2 * c + e) * LANES, (2 * c + e + 1) * LANES)
            result[c][e] = out[c * XY : (c + 1) * XY] + spread[:, lanes]
    return result


def sum_local(pair, out_ref, slot):
    row = lax.broadcasted_iota(jnp.int32, (8, 8, LANES), 1)
    lane = lax.broadcasted_iota(jnp.int32, (8, 8, LANES), 2)
    inner = lane % 8
    for e in range(2):
        mine = pair[e].reshape(8, 8, LANES)
        other = pair[1 - e].reshape(8, 8, LANES)
        total = mine + jnp.where(row == 7, pltpu.roll(other, 7, 1), 0.0)
        total = total + jnp.where(row == 0, pltpu.roll(other, 1, 1), 0.0)
        after = pltpu.roll(total, LANES - 1, 2)
        before = pltpu.roll(total, 1, 2)
        total = (
            total
            + jnp.where((inner == 7) & (lane < LANES - 1), after, 0.0)
            + jnp.where((inner == 0) & (lane > 0), before, 0.0)
        )
        out_ref[slot, :, 8 * e : 8 * (e + 1), :] = total


def positions():
    s, c = lax.axis_index("span"), lax.axis_index("col")
    return s % 2, c % 2, c == 0, c == lax.axis_size("col") - 1


def send_parts(fields, sum_ref, so_ref, se_ref, edge_ref):
    odd, _, _, _ = positions()
    for slot in range(fields):
        so_ref[slot] = sum_ref[slot, 7 * odd]
        se_ref[slot] = sum_ref[slot, 7 - 7 * odd]
    lane = lax.broadcasted_iota(jnp.int32, (8, LANES), 1)
    packed = jnp.zeros((8, LANES), F32)
    for slot in range(fields):
        for x in range(8):
            for e in range(2):
                at = slot * 16 + x * 2 + e
                tile = sum_ref[slot, x, 8 * e : 8 * (e + 1), :]
                packed = jnp.where(lane == at, pltpu.roll(tile, (at + 1) % LANES, 1), packed)
                packed = jnp.where(lane == 64 + at, pltpu.roll(tile, 64 + at, 1), packed)
    edge_ref[...] = packed


def receive(fields, sum_ref, so_ref, se_ref, edge_refs):
    odd, col_odd, _, _ = positions()
    x_so, x_se = 7 * odd, 7 - 7 * odd
    for slot in range(fields):
        sum_ref[slot, x_so] += so_ref[slot]
        sum_ref[slot, x_se] += se_ref[slot]
    lane = lax.broadcasted_iota(jnp.int32, (8, LANES), 1)
    x_of = (lane % 16) // 2

    def moved(tile, target):
        shifted = jnp.where(target == 7, pltpu.roll(tile, 14, 1), pltpu.roll(tile, LANES - 14, 1))
        return jnp.where(x_of == target, shifted, 0.0)

    total = jnp.zeros((8, LANES), F32)
    for k in range(len(edge_refs) // 3):
        straight, by_so, by_se = (ref[...] for ref in edge_refs[3 * k : 3 * k + 3])
        sent = straight + moved(by_so, x_so) + moved(by_se, x_se)
        sent = pltpu.roll(sent, 64, 1)
        high = (col_odd == 0) if k == 0 else (col_odd == 1)
        total = total + jnp.where((lane < 64) == high, sent, 0.0)
    for slot in range(fields):
        for x in range(8):
            for e in range(2):
                at = slot * 16 + x * 2 + e
                add = jnp.where(lane == LANES - 1, pltpu.roll(total, LANES - 1 - at, 1), 0.0)
                add = jnp.where(lane == 0, pltpu.roll(total, (64 - at) % LANES, 1), add)
                sum_ref[slot, x, 8 * e : 8 * (e + 1), :] += add


def interior_mask():
    _, _, first, last = positions()
    lane = lax.broadcasted_iota(jnp.int32, (1, 1, LANES), 2)
    outer = ((lane == 0) & first) | ((lane == LANES - 1) & last)
    return jnp.where(outer, 0.0, 1.0)


def scale_metric(diag_ref, cross_ref, weights, metric):
    for k in range(6):
        ref = diag_ref if k < 3 else cross_ref
        block = ref[k % 3].astype(F32)
        for e in range(2):
            metric[k, e] = section_rows(block, e) * weights[...] * VISCOSITY


def first_kernel(*refs):
    sources, (v, *tables, u, metric, total, so, se, edge) = refs[:13], refs[13:27]
    local_refs, sems = refs[27:32], refs[32]
    scratch = dict(zip(SCRATCH_NAMES, refs[33:]))
    b, gd, gc, jac, w = local_refs
    targets = [b, tables[0], tables[1], v, gd, gc, w, jac] + tables[2:]
    copies = [
        pltpu.make_async_copy(source, target, sems.at[k])
        for k, (source, target) in enumerate(zip(sources, targets))
    ]
    for copy in copies:
        copy.start()
    for copy in copies[:3]:
        copy.wait()
    fine_flow(b, tables, scratch, u)
    for copy in copies[3:]:
        copy.wait()
    scale_metric(gd, gc, w, metric)
    result = operator(lambda c, e: section_rows(v[c], e), u, metric, tables, scratch)
    for c in range(3):
        sum_local(result[c], total, c)
    sum_local([section_rows(jac[...], e) * w[...] for e in range(2)], total, 3)
    send_parts(4, total, so, se, edge)


def second_kernel(edges, *refs):
    v, *tables = refs[:8]
    u, metric, summed, so_in, se_in = refs[8:13]
    edge_in = refs[13 : 13 + edges]
    inverse, total, so, se, edge = refs[13 + edges : 18 + edges]
    scratch = dict(zip(SCRATCH_NAMES + ["held", "half"], refs[18 + edges :]))
    held, half = scratch["held"], scratch["half"]
    held[...] = summed[...]
    receive(4, held, so_in, se_in, edge_in)
    inner = interior_mask()
    inv = 1.0 / held[3]
    inverse[...] = inv
    for c in range(3):
        half[c] = inner * (v[c] - (0.5 * STEP_SIZE) * inv * held[c])
    result = operator(lambda c, e: section_rows(half[c], e), u, metric, tables, scratch)
    for c in range(3):
        sum_local(result[c], total, c)
    send_parts(3, total, so, se, edge)


def third_kernel(edges, *refs):
    v, inverse, summed, so_in, se_in = refs[:5]
    edge_in = refs[5 : 5 + edges]
    out, held, sems = refs[5 + edges :]
    held[...] = summed[...]
    receive(3, held, so_in, se_in, edge_in)
    inner = interior_mask()
    copies = []
    for c in range(3):
        held[c] = inner * (v[c] - STEP_SIZE * inverse[...] * held[c])
        copies.append(pltpu.make_async_copy(held.at[c], out.at[c], sems.at[c]))
        copies[-1].start()
    for copy in copies:
        copy.wait()


SCRATCH_NAMES = ["xhl", "js", "vs", "bz", "ts", "hs"]


def scratch_shapes():
    return [
        pltpu.VMEM((2, 3 * XY, 2 * LANES), BF16),
        pltpu.VMEM((3 * XY, 9 * LANES), BF16),
        pltpu.VMEM((3 * XY, 6 * LANES), BF16),
        pltpu.VMEM((2, 3 * XY, 10 * LANES), BF16),
        pltpu.VMEM((6 * QQ, 3 * LANES), BF16),
        pltpu.VMEM((6 * XY, 6 * LANES), BF16),
    ]


def call(kernel, name, ins, outs, scratch, in_space=pltpu.VMEM, out_space=pltpu.VMEM):
    ins = [pltpu.with_memory_space_constraint(array, in_space) for array in ins]
    return pl.pallas_call(
        kernel,
        name=name,
        out_shape=[out_space(shape, dtype) for shape, dtype in outs],
        in_specs=[pl.BlockSpec(memory_space=in_space)] * len(ins),
        out_specs=[pl.BlockSpec(memory_space=out_space)] * len(outs),
        scratch_shapes=scratch,
        compiler_params=pltpu.CompilerParams(vmem_limit_bytes=24 * 1024 * 1024),
    )(*ins)


def pairings(count, periodic):
    even = [(i, i + 1) for i in range(0, count - 1, 2)]
    odd = [(i, i + 1) for i in range(1, count - 1, 2)]
    if periodic:
        odd.append((count - 1, 0))
    return [pairs + [(b, a) for a, b in pairs] for pairs in (odd, even)]


def exchange(so, se, edge):
    spans, cols = lax.axis_size("span"), lax.axis_size("col")
    span_odd, span_even = pairings(spans, True)
    col_odd, col_even = pairings(cols, False)
    so_in = lax.ppermute(so, "span", span_odd)
    se_in = lax.ppermute(se, "span", span_even)
    edges = []
    for col_pairs in (col_even, col_odd):
        if not col_pairs:
            continue
        edges.append(lax.ppermute(edge, "col", col_pairs))
        for span_pairs in (span_odd, span_even):
            both = [
                (s * cols + c, t * cols + d) for s, t in span_pairs for c, d in col_pairs
            ]
            edges.append(lax.ppermute(edge, ("span", "col"), both))
    return so_in, se_in, edges


def local(adjoint_field, base_flow, metric_diag, metric_cross, jacobian):
    tables, weights = constants()
    tables = [jnp.asarray(table, BF16) for table in tables]
    weights = jnp.asarray(weights)
    block = adjoint_field.shape[1:]
    plane = block[1:]
    ins = [base_flow, tables[0], tables[1], adjoint_field, metric_diag, metric_cross]
    ins += [weights, jacobian] + tables[2:]
    field = ((3,) + block, F32)
    v, *rest = call(
        first_kernel,
        "first_operator",
        ins,
        [field]
        + [(table.shape, BF16) for table in tables]
        + [((QQ, 9 * LANES), F32), ((6, 2, XY, LANES), F32), ((4,) + block, F32)]
        + [((4,) + plane, F32)] * 2
        + [((8, LANES), F32)],
        [
            pltpu.VMEM((3,) + block, F32),
            pltpu.VMEM((3,) + block, BF16),
            pltpu.VMEM((3,) + block, BF16),
            pltpu.VMEM(block, F32),
            pltpu.VMEM(weights.shape, F32),
            pltpu.SemaphoreType.DMA((len(ins),)),
        ]
        + scratch_shapes(),
        in_space=pltpu.HBM,
    )
    *state, so, se, edge = rest
    so, se, edges = exchange(so, se, edge)
    inverse, total, so, se, edge = call(
        functools.partial(second_kernel, len(edges)),
        "second_operator",
        [v] + state + [so, se] + edges,
        [(block, F32), field] + [((3,) + plane, F32)] * 2 + [((8, LANES), F32)],
        scratch_shapes() + [pltpu.VMEM((4,) + block, F32), pltpu.VMEM((3,) + block, F32)],
    )
    so, se, edges = exchange(so, se, edge)
    (out,) = call(
        functools.partial(third_kernel, len(edges)),
        "advance",
        [v, inverse, total, so, se] + edges,
        [field],
        [pltpu.VMEM((3,) + block, F32), pltpu.SemaphoreType.DMA((3,))],
        out_space=pltpu.HBM,
    )
    return out


def solution(mesh):
    in_specs = (
        P(None, "span", None, "col"),
        P(None, "span", None, "col"),
        P(None, "span", None, "col"),
        P(None, "span", None, "col"),
        P("span", None, "col"),
    )
    out_specs = P(None, "span", None, "col")
    return jax.shard_map(local, mesh=mesh, in_specs=in_specs, out_specs=out_specs, check_vma=False)
```

time: 89.8 us -> 32.1 us (0.36)
  matrix products: 33.1 us -> 0 us
  local copies, waits for them, and re-layouts: 17 us -> 0 us
  waiting for transfers between devices: 15 us -> 6.65 us
  Pallas kernels: 0 us -> 7.87 us
  other arithmetic: 5.19 us -> 0 us
  between operations: 1.21 us -> 0.03 us
    dot_general x39 -> x0, matrix products: 33.1 us -> none  [the longest x13 17.9 us: along_third(): result = jnp.einsum('lxyzk,kq->lxyzq', blocks, kron_table, precision=HIGH)]
    ppermute x8 -> x10, waiting for transfers between devices: 15 us -> 6.65 us  [the longest x4 6.64 us: exchange(): edges.append(lax.ppermute(edge, ('span', 'col'), both))]
    pallas_call x0 -> x3, Pallas kernels: none -> 7.87 us  [call(): pl.pallas_call(kernel, name=name, out_shape=[out_space(shape, dtype) for...]
    mul x17 -> x0, local copies, waits for them, and re-layouts: 7.72 us -> none  [the longest x5 3.68 us: along_third(): kron_table = jnp.kron(jnp.eye(group_size, dtype=jnp.float32), matrix.T)]
    another operation x7 -> x0, local copies, waits for them, and re-layouts: 4.33 us -> none
    mul x12 -> x0, other arithmetic: 4.28 us -> none  [the longest x3 2.14 us: weight_grid(): first_axis[:, None, None] * second_axis[None, :, None]]
    dot_general x6 -> x0, local copies, waits for them, and re-layouts: 2.91 us -> none  [along_third(): result = jnp.einsum('lxyzk,kq->lxyzq', blocks, kron_table, precision=HIGH)]
    transpose x4 -> x0, local copies, waits for them, and re-layouts: 0.94 us -> none  [along_second(): result = jnp.einsum('pi,lxaiz->lxapz', matrix, blocks, precision=HIGH)]
  transfers between devices with their start and end apart: 8 -> 10, of which waited for: 6 -> 3; matrix products, arithmetic and copies ran while one was open for 0% -> 0% of each run, Pallas kernels for 0% -> 0%
where the time goes in v1:
time: 32.1 us; the launch traced here: 31.8 us
  starting transfers between devices  17.2 us (54%)
  Pallas kernels  7.87 us (25%)
  waiting for transfers between devices  6.65 us (21%)
    ppermute x2, starting transfers between devices, exchange(): so_in = lax.ppermute(so, 'span', span_odd)  8.21 us
    ppermute x4, starting transfers between devices, exchange(): edges.append(lax.ppermute(edge, ('span', 'col'), both))  8.03 us
    pallas_call x3, Pallas kernels, call(): pl.pallas_call(kernel, name=name, out_shape=[out_space(shape, dtype) for...  7.87 us
    ppermute x4, waiting for transfers between devices, exchange(): edges.append(lax.ppermute(edge, ('span', 'col'), both))  6.64 us
    ppermute x2, starting transfers between devices, exchange(): edges.append(lax.ppermute(edge, 'col', col_pairs))  0.99 us
  transfers between devices with their start and end apart: 10, of which 3 were waited for; matrix products, arithmetic and copies ran while one was open for 0% of the time, Pallas kernels for 0%

profile of v1, /device:TPU:0, one launch (start us, length us, event | category | flops | bytes accessed | tf_op | source)
XLA Modules:
  0.0 31.8 jit_solution(6891386119140157270)
XLA Ops:
  0.0 4.2 %first_operator.1 = (f32[3,8,16,128]{3,2,1,0:T(8,128)S(1)}, bf16[256,768]{1,0:T(8,128)(2,1)S(1)}, bf16[144,192]{1,0:T(8,128)(2,1)S(1)}, bf16[128,192]{1,0:T(8,12...) custom-call(f32[3,8,16,128]{3,2,1,0:T(8,128)} %refs_0_.1, ...), custom_call_target="tpu_custom_call" | custom-call | tf_op jit(solution)/shard_map/first_operator/pallas_call | solution.py:430
  4.2 7.0 %collective-permute-start = (f32[4,16,128]{2,1,0:T(8,128)S(1)}, f32[4,16,128]{2,1,0:T(8,128)S(1)}, u32[]{:S(2)}, u32[]{:S(2)}) collective-permute-start(f32[4,16,128]{2,1,0:T(8,128)S(1)} %get-tuple-element.35), channel_id=1, source_target_pairs={{2,4},{6,8},{10,12},{14,16},{18,20},{22,24},{26,28},{30,0},{4,2},{... | collective-permute-start | bytes 98312 | tf_op jit(solution)/shard_map/ppermute | solution.py:453
  11.2 0.0 collective-permute-start.1
  11.2 0.9 %collective-permute-start.4 = (f32[8,128]{1,0:T(8,128)S(1)}, f32[8,128]{1,0:T(8,128)S(1)}, u32[]{:S(2)}, u32[]{:S(2)}) collective-permute-start(f32[8,128]{1,0:T(8,128)S(1)} %get-tuple-element.37), channel_id=1, source_target_pairs={{0,3},{1,2},{4,7},{5,6},{8,11},{9,10},{12,15},{13,14},{16,19},{17,... | collective-permute-start | bytes 12296 | tf_op jit(solution)/shard_map/ppermute | solution.py:464
  12.1 0.9 %collective-permute-start.3 = (f32[8,128]{1,0:T(8,128)S(1)}, f32[8,128]{1,0:T(8,128)S(1)}, u32[]{:S(2)}, u32[]{:S(2)}) collective-permute-start(f32[8,128]{1,0:T(8,128)S(1)} %get-tuple-element.37), channel_id=1, source_target_pairs={{2,5},{3,4},{6,9},{7,8},{10,13},{11,12},{14,17},{15,16},{18,21},{1... | collective-permute-start | bytes 12296 | tf_op jit(solution)/shard_map/ppermute | solution.py:464
  13.0 0.3 %collective-permute-start.2 = (f32[8,128]{1,0:T(8,128)S(1)}, f32[8,128]{1,0:T(8,128)S(1)}, u32[]{:S(2)}, u32[]{:S(2)}) collective-permute-start(f32[8,128]{1,0:T(8,128)S(1)} %get-tuple-element.37), channel_id=1, source_target_pairs={{0,1},{1,0},{2,3},{3,2},{4,5},{5,4},{6,7},{7,6},{8,9},{9,8},{10,11... | collective-permute-start | bytes 12296 | tf_op jit(solution)/shard_map/ppermute | solution.py:459
  13.3 0.9 %collective-permute-done.4.refs_15_ = f32[8,128]{1,0:T(8,128)S(1)} collective-permute-done((f32[8,128]{1,0:T(8,128)S(1)}, f32[8,128]{1,0:T(8,128)S(1)}, u32[]{:S(2)}, u32[]{:S(2)}) %collective-permute-start.4) | collective-permute-done | bytes 4128 | tf_op jit(solution)/shard_map/ppermute | solution.py:464
  14.3 4.5 %collective-permute-done.3.refs_14_ = f32[8,128]{1,0:T(8,128)S(1)} collective-permute-done((f32[8,128]{1,0:T(8,128)S(1)}, f32[8,128]{1,0:T(8,128)S(1)}, u32[]{:S(2)}, u32[]{:S(2)}) %collective-permute-start.3) | collective-permute-done | bytes 4128 | tf_op jit(solution)/shard_map/ppermute | solution.py:464
  18.7 0.0 collective-permute-done.2.refs_13_
  18.7 0.0 collective-permute-done.refs_11_
  18.7 0.0 collective-permute-done.1.refs_12_
  18.7 2.7 %second_operator.1 = (f32[8,16,128]{2,1,0:T(8,128)S(1)}, f32[3,8,16,128]{3,2,1,0:T(8,128)S(1)}, f32[3,16,128]{2,1,0:T(8,128)S(1)}, f32[3,16,128]{2,1,0:T(8,128)S(1)}, f32[8,128]{1,0:T(8,128)S(1)}) custom-call(f32[3,8,16,128]{3,2,1,0:T(8,128)S(1)} %get-tuple-element.24.refs_0_, bf16[256,768]{1,0:T(8,128)(2,1)S(1)} %get-tuple-element.25.refs_1_, ...), custom_call_target="tpu_custom_call" | custom-call | tf_op jit(solution)/shard_map/second_operator/pallas_call | solution.py:430
  21.4 1.2 %collective-permute-start.5 = (f32[3,16,128]{2,1,0:T(8,128)S(1)}, f32[3,16,128]{2,1,0:T(8,128)S(1)}, u32[]{:S(2)}, u32[]{:S(2)}) collective-permute-start(f32[3,16,128]{2,1,0:T(8,128)S(1)} %get-tuple-element.40), channel_id=1, source_target_pairs={{2,4},{6,8},{10,12},{14,16},{18,20},{22,24},{26,28},{30,0},{4,2},{... | collective-permute-start | bytes 73736 | tf_op jit(solution)/shard_map/ppermute | solution.py:453
  22.6 0.0 collective-permute-start.6
  22.6 1.5 %collective-permute-start.9 = (f32[8,128]{1,0:T(8,128)S(1)}, f32[8,128]{1,0:T(8,128)S(1)}, u32[]{:S(2)}, u32[]{:S(2)}) collective-permute-start(f32[8,128]{1,0:T(8,128)S(1)} %get-tuple-element.42), channel_id=1, source_target_pairs={{0,3},{1,2},{4,7},{5,6},{8,11},{9,10},{12,15},{13,14},{16,19},{17,... | collective-permute-start | bytes 12296 | tf_op jit(solution)/shard_map/ppermute | solution.py:464
  24.1 4.7 %collective-permute-start.8 = (f32[8,128]{1,0:T(8,128)S(1)}, f32[8,128]{1,0:T(8,128)S(1)}, u32[]{:S(2)}, u32[]{:S(2)}) collective-permute-start(f32[8,128]{1,0:T(8,128)S(1)} %get-tuple-element.42), channel_id=1, source_target_pairs={{2,5},{3,4},{6,9},{7,8},{10,13},{11,12},{14,17},{15,16},{18,21},{1... | collective-permute-start | bytes 12296 | tf_op jit(solution)/shard_map/ppermute | solution.py:464
  28.8 0.7 %collective-permute-start.7 = (f32[8,128]{1,0:T(8,128)S(1)}, f32[8,128]{1,0:T(8,128)S(1)}, u32[]{:S(2)}, u32[]{:S(2)}) collective-permute-start(f32[8,128]{1,0:T(8,128)S(1)} %get-tuple-element.42), channel_id=1, source_target_pairs={{0,1},{1,0},{2,3},{3,2},{4,5},{5,4},{6,7},{7,6},{8,9},{9,8},{10,11... | collective-permute-start | bytes 12296 | tf_op jit(solution)/shard_map/ppermute | solution.py:459
  29.5 0.0 collective-permute-done.9.refs_7_
  29.5 1.2 %collective-permute-done.8.refs_6_ = f32[8,128]{1,0:T(8,128)S(1)} collective-permute-done((f32[8,128]{1,0:T(8,128)S(1)}, f32[8,128]{1,0:T(8,128)S(1)}, u32[]{:S(2)}, u32[]{:S(2)}) %collective-permute-start.8) | collective-permute-done | bytes 4128 | tf_op jit(solution)/shard_map/ppermute | solution.py:464
  30.8 0.0 collective-permute-done.7.refs_5_
  30.8 0.0 collective-permute-done.5.refs_3_
  30.8 0.0 collective-permute-done.6.refs_4_
  30.8 1.0 %advance.1 = f32[3,8,16,128]{3,2,1,0:T(8,128)} custom-call(f32[3,8,16,128]{3,2,1,0:T(8,128)S(1)} %get-tuple-element.24.refs_0_, f32[8,16,128]{2,1,0:T(8,128)S(1)} %get-tuple-element.38.refs_1_, f32[3,8,16,128]{3,2,1,0:T(8,128)S(1)} %get-tuple-element.39.refs_2_, f32[3,16,128]{2,1,0:T(8,128)S(1)} %collective-permute-done.5.refs_3_, ...), custom_call_target="tpu_custom_call" | custom-call | tf_op jit(solution)/shard_map/advance/pallas_call | solution.py:430
Async XLA Ops:
  4.2 14.5 %collective-permute-start = (f32[4,16,128]{2,1,0:T(8,128)S(1)}, f32[4,16,128]{2,1,0:T(8,128)S(1)}, u32[]{:S(2)}, u32[]{:S(2)}) collective-permute-start(f32[4,16,128]{2,1,0:T(8,128)S(1)} %get-tuple-element.35), channel_id=1, source_target_pairs={{2,4},{6,8},{10,12},{14,16},{18,20},{22,24},{26,28},{30,0},{4,2},{... | collective-permute-start | bytes 98312 | tf_op jit(solution)/shard_map/ppermute | solution.py:453
  11.2 7.5 %collective-permute-start.1 = (f32[4,16,128]{2,1,0:T(8,128)S(1)}, f32[4,16,128]{2,1,0:T(8,128)S(1)}, u32[]{:S(2)}, u32[]{:S(2)}) collective-permute-start(f32[4,16,128]{2,1,0:T(8,128)S(1)} %get-tuple-element.36), channel_id=1, source_target_pairs={{0,2},{4,6},{8,10},{12,14},{16,18},{20,22},{24,26},{28,30},{2,0},{... | collective-permute-start | bytes 98312 | tf_op jit(solution)/shard_map/ppermute | solution.py:454
  11.2 3.1 %collective-permute-start.4 = (f32[8,128]{1,0:T(8,128)S(1)}, f32[8,128]{1,0:T(8,128)S(1)}, u32[]{:S(2)}, u32[]{:S(2)}) collective-permute-start(f32[8,128]{1,0:T(8,128)S(1)} %get-tuple-element.37), channel_id=1, source_target_pairs={{0,3},{1,2},{4,7},{5,6},{8,11},{9,10},{12,15},{13,14},{16,19},{17,... | collective-permute-start | bytes 12296 | tf_op jit(solution)/shard_map/ppermute | solution.py:464
  12.1 6.6 %collective-permute-start.3 = (f32[8,128]{1,0:T(8,128)S(1)}, f32[8,128]{1,0:T(8,128)S(1)}, u32[]{:S(2)}, u32[]{:S(2)}) collective-permute-start(f32[8,128]{1,0:T(8,128)S(1)} %get-tuple-element.37), channel_id=1, source_target_pairs={{2,5},{3,4},{6,9},{7,8},{10,13},{11,12},{14,17},{15,16},{18,21},{1... | collective-permute-start | bytes 12296 | tf_op jit(solution)/shard_map/ppermute | solution.py:464
  13.0 5.7 %collective-permute-start.2 = (f32[8,128]{1,0:T(8,128)S(1)}, f32[8,128]{1,0:T(8,128)S(1)}, u32[]{:S(2)}, u32[]{:S(2)}) collective-permute-start(f32[8,128]{1,0:T(8,128)S(1)} %get-tuple-element.37), channel_id=1, source_target_pairs={{0,1},{1,0},{2,3},{3,2},{4,5},{5,4},{6,7},{7,6},{8,9},{9,8},{10,11... | collective-permute-start | bytes 12296 | tf_op jit(solution)/shard_map/ppermute | solution.py:459
  21.4 9.4 %collective-permute-start.5 = (f32[3,16,128]{2,1,0:T(8,128)S(1)}, f32[3,16,128]{2,1,0:T(8,128)S(1)}, u32[]{:S(2)}, u32[]{:S(2)}) collective-permute-start(f32[3,16,128]{2,1,0:T(8,128)S(1)} %get-tuple-element.40), channel_id=1, source_target_pairs={{2,4},{6,8},{10,12},{14,16},{18,20},{22,24},{26,28},{30,0},{4,2},{... | collective-permute-start | bytes 73736 | tf_op jit(solution)/shard_map/ppermute | solution.py:453
  22.6 8.1 %collective-permute-start.6 = (f32[3,16,128]{2,1,0:T(8,128)S(1)}, f32[3,16,128]{2,1,0:T(8,128)S(1)}, u32[]{:S(2)}, u32[]{:S(2)}) collective-permute-start(f32[3,16,128]{2,1,0:T(8,128)S(1)} %get-tuple-element.41), channel_id=1, source_target_pairs={{0,2},{4,6},{8,10},{12,14},{16,18},{20,22},{24,26},{28,30},{2,0},{... | collective-permute-start | bytes 73736 | tf_op jit(solution)/shard_map/ppermute | solution.py:454
  22.6 6.9 %collective-permute-start.9 = (f32[8,128]{1,0:T(8,128)S(1)}, f32[8,128]{1,0:T(8,128)S(1)}, u32[]{:S(2)}, u32[]{:S(2)}) collective-permute-start(f32[8,128]{1,0:T(8,128)S(1)} %get-tuple-element.42), channel_id=1, source_target_pairs={{0,3},{1,2},{4,7},{5,6},{8,11},{9,10},{12,15},{13,14},{16,19},{17,... | collective-permute-start | bytes 12296 | tf_op jit(solution)/shard_map/ppermute | solution.py:464
  24.1 6.6 %collective-permute-start.8 = (f32[8,128]{1,0:T(8,128)S(1)}, f32[8,128]{1,0:T(8,128)S(1)}, u32[]{:S(2)}, u32[]{:S(2)}) collective-permute-start(f32[8,128]{1,0:T(8,128)S(1)} %get-tuple-element.42), channel_id=1, source_target_pairs={{2,5},{3,4},{6,9},{7,8},{10,13},{11,12},{14,17},{15,16},{18,21},{1... | collective-permute-start | bytes 12296 | tf_op jit(solution)/shard_map/ppermute | solution.py:464
  28.8 1.9 %collective-permute-start.7 = (f32[8,128]{1,0:T(8,128)S(1)}, f32[8,128]{1,0:T(8,128)S(1)}, u32[]{:S(2)}, u32[]{:S(2)}) collective-permute-start(f32[8,128]{1,0:T(8,128)S(1)} %get-tuple-element.42), channel_id=1, source_target_pairs={{0,1},{1,0},{2,3},{3,2},{4,5},{5,4},{6,7},{7,6},{8,9},{9,8},{10,11... | collective-permute-start | bytes 12296 | tf_op jit(solution)/shard_map/ppermute | solution.py:459

commit v2 on v1

--- a/solution.py
+++ b/solution.py
@@ -285,15 +285,11 @@
 
 
 def positions():
-    s, c = lax.axis_index("span"), lax.axis_index("col")
-    return s % 2, c % 2, c == 0, c == lax.axis_size("col") - 1
-
-
-def send_parts(fields, sum_ref, so_ref, se_ref, edge_ref):
-    odd, _, _, _ = positions()
-    for slot in range(fields):
-        so_ref[slot] = sum_ref[slot, 7 * odd]
-        se_ref[slot] = sum_ref[slot, 7 - 7 * odd]
+    c = lax.axis_index("col")
+    return c % 2, c == 0, c == lax.axis_size("col") - 1
+
+
+def pack_edges(fields, sum_ref, edge_ref):
     lane = lax.broadcasted_iota(jnp.int32, (8, LANES), 1)
     packed = jnp.zeros((8, LANES), F32)
     for slot in range(fields):
@@ -306,37 +302,49 @@
     edge_ref[...] = packed
 
 
-def receive(fields, sum_ref, so_ref, se_ref, edge_refs):
-    odd, col_odd, _, _ = positions()
-    x_so, x_se = 7 * odd, 7 - 7 * odd
-    for slot in range(fields):
-        sum_ref[slot, x_so] += so_ref[slot]
-        sum_ref[slot, x_se] += se_ref[slot]
+def received_edges(edge_refs):
+    col_odd, _, _ = positions()
     lane = lax.broadcasted_iota(jnp.int32, (8, LANES), 1)
-    x_of = (lane % 16) // 2
-
-    def moved(tile, target):
-        shifted = jnp.where(target == 7, pltpu.roll(tile, 14, 1), pltpu.roll(tile, LANES - 14, 1))
-        return jnp.where(x_of == target, shifted, 0.0)
-
     total = jnp.zeros((8, LANES), F32)
-    for k in range(len(edge_refs) // 3):
-        straight, by_so, by_se = (ref[...] for ref in edge_refs[3 * k : 3 * k + 3])
-        sent = straight + moved(by_so, x_so) + moved(by_se, x_se)
-        sent = pltpu.roll(sent, 64, 1)
+    for k, ref in enumerate(edge_refs):
         high = (col_odd == 0) if k == 0 else (col_odd == 1)
-        total = total + jnp.where((lane < 64) == high, sent, 0.0)
+        total = total + jnp.where((lane < 64) == high, pltpu.roll(ref[...], 64, 1), 0.0)
+    return total
+
+
+def with_edges(tile, edges, at):
+    lane = lax.broadcasted_iota(jnp.int32, (8, LANES), 1)
+    add = jnp.where(lane == LANES - 1, pltpu.roll(edges, LANES - 1 - at, 1), 0.0)
+    return tile + jnp.where(lane == 0, pltpu.roll(edges, (64 - at) % LANES, 1), add)
+
+
+def planes_kernel(fields, count, *refs):
+    summed, edge_refs, (up, down) = refs[0], refs[1 : 1 + count], refs[1 + count :]
+    edges = received_edges(edge_refs)
+    for x, plane in ((7, up), (0, down)):
+        for slot in range(fields):
+            for e in range(2):
+                rows = slice(8 * e, 8 * (e + 1))
+                at = slot * 16 + x * 2 + e
+                plane[slot, rows, :] = with_edges(summed[slot, x, rows, :], edges, at)
+
+
+def receive(fields, sum_ref, up_ref, down_ref, edge_refs):
+    edges = received_edges(edge_refs)
     for slot in range(fields):
         for x in range(8):
             for e in range(2):
-                at = slot * 16 + x * 2 + e
-                add = jnp.where(lane == LANES - 1, pltpu.roll(total, LANES - 1 - at, 1), 0.0)
-                add = jnp.where(lane == 0, pltpu.roll(total, (64 - at) % LANES, 1), add)
-                sum_ref[slot, x, 8 * e : 8 * (e + 1), :] += add
+                rows = slice(8 * e, 8 * (e + 1))
+                tile = with_edges(sum_ref[slot, x, rows, :], edges, slot * 16 + x * 2 + e)
+                if x == 0:
+                    tile += up_ref[slot, rows, :]
+                if x == 7:
+                    tile += down_ref[slot, rows, :]
+                sum_ref[slot, x, rows, :] = tile
 
 
 def interior_mask():
-    _, _, first, last = positions()
+    _, first, last = positions()
     lane = lax.broadcasted_iota(jnp.int32, (1, 1, LANES), 2)
     outer = ((lane == 0) & first) | ((lane == LANES - 1) & last)
     return jnp.where(outer, 0.0, 1.0)
@@ -351,9 +359,9 @@
 
 
 def first_kernel(*refs):
-    sources, (v, *tables, u, metric, total, so, se, edge) = refs[:13], refs[13:27]
-    local_refs, sems = refs[27:32], refs[32]
-    scratch = dict(zip(SCRATCH_NAMES, refs[33:]))
+    sources, (v, *tables, u, metric, total, edge) = refs[:13], refs[13:25]
+    local_refs, sems = refs[25:30], refs[30]
+    scratch = dict(zip(SCRATCH_NAMES, refs[31:]))
     b, gd, gc, jac, w = local_refs
     targets = [b, tables[0], tables[1], v, gd, gc, w, jac] + tables[2:]
     copies = [
@@ -372,18 +380,18 @@
     for c in range(3):
         sum_local(result[c], total, c)
     sum_local([section_rows(jac[...], e) * w[...] for e in range(2)], total, 3)
-    send_parts(4, total, so, se, edge)
+    pack_edges(4, total, edge)
 
 
 def second_kernel(edges, *refs):
     v, *tables = refs[:8]
-    u, metric, summed, so_in, se_in = refs[8:13]
+    u, metric, summed, up_in, down_in = refs[8:13]
     edge_in = refs[13 : 13 + edges]
-    inverse, total, so, se, edge = refs[13 + edges : 18 + edges]
-    scratch = dict(zip(SCRATCH_NAMES + ["held", "half"], refs[18 + edges :]))
+    inverse, total, edge = refs[13 + edges : 16 + edges]
+    scratch = dict(zip(SCRATCH_NAMES + ["held", "half"], refs[16 + edges :]))
     held, half = scratch["held"], scratch["half"]
     held[...] = summed[...]
-    receive(4, held, so_in, se_in, edge_in)
+    receive(4, held, up_in, down_in, edge_in)
     inner = interior_mask()
     inv = 1.0 / held[3]
     inverse[...] = inv
@@ -392,15 +400,15 @@
     result = operator(lambda c, e: section_rows(half[c], e), u, metric, tables, scratch)
     for c in range(3):
         sum_local(result[c], total, c)
-    send_parts(3, total, so, se, edge)
+    pack_edges(3, total, edge)
 
 
 def third_kernel(edges, *refs):
-    v, inverse, summed, so_in, se_in = refs[:5]
+    v, inverse, summed, up_in, down_in = refs[:5]
     edge_in = refs[5 : 5 + edges]
     out, held, sems = refs[5 + edges :]
     held[...] = summed[...]
-    receive(3, held, so_in, se_in, edge_in)
+    receive(3, held, up_in, down_in, edge_in)
     inner = interior_mask()
     copies = []
     for c in range(3):
@@ -438,31 +446,26 @@
     )(*ins)
 
 
-def pairings(count, periodic):
+def wall_pairings(count):
     even = [(i, i + 1) for i in range(0, count - 1, 2)]
     odd = [(i, i + 1) for i in range(1, count - 1, 2)]
-    if periodic:
-        odd.append((count - 1, 0))
-    return [pairs + [(b, a) for a, b in pairs] for pairs in (odd, even)]
-
-
-def exchange(so, se, edge):
-    spans, cols = lax.axis_size("span"), lax.axis_size("col")
-    span_odd, span_even = pairings(spans, True)
-    col_odd, col_even = pairings(cols, False)
-    so_in = lax.ppermute(so, "span", span_odd)
-    se_in = lax.ppermute(se, "span", span_even)
-    edges = []
-    for col_pairs in (col_even, col_odd):
-        if not col_pairs:
-            continue
-        edges.append(lax.ppermute(edge, "col", col_pairs))
-        for span_pairs in (span_odd, span_even):
-            both = [
-                (s * cols + c, t * cols + d) for s, t in span_pairs for c, d in col_pairs
-            ]
-            edges.append(lax.ppermute(edge, ("span", "col"), both))
-    return so_in, se_in, edges
+    return [pairs + [(b, a) for a, b in pairs] for pairs in (even, odd) if pairs]
+
+
+def exchange(fields, total, edge):
+    spans = lax.axis_size("span")
+    ahead = [(i, (i + 1) % spans) for i in range(spans)]
+    back = [(b, a) for a, b in ahead]
+    edges = [lax.ppermute(edge, "col", way) for way in wall_pairings(lax.axis_size("col"))]
+    plane = ((fields,) + total.shape[2:], F32)
+    up, down = call(
+        functools.partial(planes_kernel, fields, len(edges)),
+        "planes",
+        [total] + edges,
+        [plane] * 2,
+        [],
+    )
+    return lax.ppermute(up, "span", ahead), lax.ppermute(down, "span", back), edges
 
 
 def local(adjoint_field, base_flow, metric_diag, metric_cross, jacobian):
@@ -470,7 +473,6 @@
     tables = [jnp.asarray(table, BF16) for table in tables]
     weights = jnp.asarray(weights)
     block = adjoint_field.shape[1:]
-    plane = block[1:]
     ins = [base_flow, tables[0], tables[1], adjoint_field, metric_diag, metric_cross]
     ins += [weights, jacobian] + tables[2:]
     field = ((3,) + block, F32)
@@ -481,7 +483,6 @@
         [field]
         + [(table.shape, BF16) for table in tables]
         + [((QQ, 9 * LANES), F32), ((6, 2, XY, LANES), F32), ((4,) + block, F32)]
-        + [((4,) + plane, F32)] * 2
         + [((8, LANES), F32)],
         [
             pltpu.VMEM((3,) + block, F32),
@@ -494,20 +495,20 @@
         + scratch_shapes(),
         in_space=pltpu.HBM,
     )
-    *state, so, se, edge = rest
-    so, se, edges = exchange(so, se, edge)
-    inverse, total, so, se, edge = call(
+    *state, edge = rest
+    up, down, edges = exchange(4, state[-1], edge)
+    inverse, total, edge = call(
         functools.partial(second_kernel, len(edges)),
         "second_operator",
-        [v] + state + [so, se] + edges,
-        [(block, F32), field] + [((3,) + plane, F32)] * 2 + [((8, LANES), F32)],
+        [v] + state + [up, down] + edges,
+        [(block, F32), field, ((8, LANES), F32)],
         scratch_shapes() + [pltpu.VMEM((4,) + block, F32), pltpu.VMEM((3,) + block, F32)],
     )
-    so, se, edges = exchange(so, se, edge)
+    up, down, edges = exchange(3, total, edge)
     (out,) = call(
         functools.partial(third_kernel, len(edges)),
         "advance",
-        [v, inverse, total, so, se] + edges,
+        [v, inverse, total, up, down] + edges,
         [field],
         [pltpu.VMEM((3,) + block, F32), pltpu.SemaphoreType.DMA((3,))],
         out_space=pltpu.HBM,

time: 32.1 us -> 27.1 us (0.84)
  starting transfers between devices: 17.2 us -> 13.3 us
  waiting for transfers between devices: 6.65 us -> 5.55 us
    ppermute x10 -> x6, starting transfers between devices: 17.2 us -> 13.3 us  [the longest x2 9.38 us: exchange(): lax.ppermute(down, 'span', back)]
    ppermute x10 -> x6, waiting for transfers between devices: 6.65 us -> 5.55 us  [the longest x2 3.57 us: exchange(): lax.ppermute(up, 'span', ahead)]
    pallas_call x3 -> x5, Pallas kernels: 7.87 us -> 8.02 us  [call(): pl.pallas_call(kernel, name=name, out_shape=[out_space(shape, dtype) for...]
  transfers between devices with their start and end apart: 10 -> 6, of which waited for: 3 -> 4; matrix products, arithmetic and copies ran while one was open for 0% -> 0% of each run, Pallas kernels for 0% -> 0%
where the time goes in v2:
time: 27.1 us; the launch traced here: 26.9 us
  starting transfers between devices  13.3 us (49%)
  Pallas kernels  8.02 us (30%)
  waiting for transfers between devices  5.55 us (20%)
    ppermute x2, starting transfers between devices, exchange(): lax.ppermute(down, 'span', back)  9.38 us
    pallas_call x5, Pallas kernels, call(): pl.pallas_call(kernel, name=name, out_shape=[out_space(shape, dtype) for...  8.02 us
    ppermute x2, waiting for transfers between devices, exchange(): lax.ppermute(up, 'span', ahead)  3.57 us
    ppermute x2, starting transfers between devices, exchange(): lax.ppermute(up, 'span', ahead)  3.34 us
    ppermute x2, waiting for transfers between devices, exchange(): lax.ppermute(edge, 'col', way)  1.98 us
    ppermute x2, starting transfers between devices, exchange(): lax.ppermute(edge, 'col', way)  0.6 us
  transfers between devices with their start and end apart: 6, of which 4 were waited for; matrix products, arithmetic and copies ran while one was open for 0% of the time, Pallas kernels for 0%

profile of v2, /device:TPU:0, one launch (start us, length us, event | category | flops | bytes accessed | tf_op | source)
XLA Modules:
  0.0 26.9 jit_solution(9044005351988218301)
XLA Ops:
  0.0 4.2 %first_operator.1 = (f32[3,8,16,128]{3,2,1,0:T(8,128)S(1)}, bf16[256,768]{1,0:T(8,128)(2,1)S(1)}, bf16[144,192]{1,0:T(8,128)(2,1)S(1)}, bf16[128,192]{1,0:T(8,12...) custom-call(f32[3,8,16,128]{3,2,1,0:T(8,128)} %refs_0_.1, ...), custom_call_target="tpu_custom_call" | custom-call | tf_op jit(solution)/shard_map/first_operator/pallas_call | solution.py:438
  4.2 0.5 %collective-permute-start = (f32[8,128]{1,0:T(8,128)S(1)}, f32[8,128]{1,0:T(8,128)S(1)}, u32[]{:S(2)}, u32[]{:S(2)}) collective-permute-start(f32[8,128]{1,0:T(8,128)S(1)} %get-tuple-element.35), channel_id=1, source_target_pairs={{0,1},{1,0},{2,3},{3,2},{4,5},{5,4},{6,7},{7,6},{8,9},{9,8},{10,11... | collective-permute-start | bytes 12296 | tf_op jit(solution)/shard_map/ppermute | solution.py:459
  4.7 0.8 %collective-permute-done.refs_1_.refs_13_ = f32[8,128]{1,0:T(8,128)S(1)} collective-permute-done((f32[8,128]{1,0:T(8,128)S(1)}, f32[8,128]{1,0:T(8,128)S(1)}, u32[]{:S(2)}, u32[]{:S(2)}) %collective-permute-start) | collective-permute-done | bytes 4128 | tf_op jit(solution)/shard_map/ppermute | solution.py:459
  5.6 0.2 planes.2
  5.7 2.9 %collective-permute-start.1 = (f32[4,16,128]{2,1,0:T(8,128)S(1)}, f32[4,16,128]{2,1,0:T(8,128)S(1)}, u32[]{:S(2)}, u32[]{:S(2)}) collective-permute-start(f32[4,16,128]{2,1,0:T(8,128)S(1)} %get-tuple-element.36), channel_id=1, source_target_pairs={{0,2},{2,4},{4,6},{6,8},{8,10},{10,12},{12,14},{14,16},{16,18},{18... | collective-permute-start | bytes 98312 | tf_op jit(solution)/shard_map/ppermute | solution.py:468
  8.6 4.1 %collective-permute-start.2 = (f32[4,16,128]{2,1,0:T(8,128)S(1)}, f32[4,16,128]{2,1,0:T(8,128)S(1)}, u32[]{:S(2)}, u32[]{:S(2)}) collective-permute-start(f32[4,16,128]{2,1,0:T(8,128)S(1)} %get-tuple-element.37), channel_id=1, source_target_pairs={{2,0},{4,2},{6,4},{8,6},{10,8},{12,10},{14,12},{16,14},{18,16},{20... | collective-permute-start | bytes 98312 | tf_op jit(solution)/shard_map/ppermute | solution.py:468
  12.7 1.8 %collective-permute-done.1.refs_11_ = f32[4,16,128]{2,1,0:T(8,128)S(1)} collective-permute-done((f32[4,16,128]{2,1,0:T(8,128)S(1)}, f32[4,16,128]{2,1,0:T(8,128)S(1)}, u32[]{:S(2)}, u32[]{:S(2)}) %collective-permute-start.1) | collective-permute-done | bytes 32800 | tf_op jit(solution)/shard_map/ppermute | solution.py:468
  14.5 0.0 collective-permute-done.2.refs_12_
  14.5 2.6 %second_operator.1 = (f32[8,16,128]{2,1,0:T(8,128)S(1)}, f32[3,8,16,128]{3,2,1,0:T(8,128)S(1)}, f32[8,128]{1,0:T(8,128)S(1)}) custom-call(f32[3,8,16,128]{3,2,1,0:T(8,128)S(1)} %get-tuple-element.24.refs_0_, bf16[256,768]{1,0:T(8,128)(2,1)S(1)} %get-tuple-element.25.refs_1_, bf16[144,192]{1,0:T(8,128)(2,1)S(1)} %get-tuple-element.26.refs_2_, ...), custom_call_target="tpu_custom_call" | custom-call | tf_op jit(solution)/shard_map/second_operator/pallas_call | solution.py:438
  17.1 0.1 collective-permute-start.3
  17.1 1.2 %collective-permute-done.3.refs_1_.refs_5_ = f32[8,128]{1,0:T(8,128)S(1)} collective-permute-done((f32[8,128]{1,0:T(8,128)S(1)}, f32[8,128]{1,0:T(8,128)S(1)}, u32[]{:S(2)}, u32[]{:S(2)}) %collective-permute-start.3) | collective-permute-done | bytes 4128 | tf_op jit(solution)/shard_map/ppermute | solution.py:459
  18.3 0.2 planes.3
  18.5 0.5 %collective-permute-start.4 = (f32[3,16,128]{2,1,0:T(8,128)S(1)}, f32[3,16,128]{2,1,0:T(8,128)S(1)}, u32[]{:S(2)}, u32[]{:S(2)}) collective-permute-start(f32[3,16,128]{2,1,0:T(8,128)S(1)} %get-tuple-element.41), channel_id=1, source_target_pairs={{0,2},{2,4},{4,6},{6,8},{8,10},{10,12},{12,14},{14,16},{16,18},{18... | collective-permute-start | bytes 73736 | tf_op jit(solution)/shard_map/ppermute | solution.py:468
  18.9 5.3 %collective-permute-start.5 = (f32[3,16,128]{2,1,0:T(8,128)S(1)}, f32[3,16,128]{2,1,0:T(8,128)S(1)}, u32[]{:S(2)}, u32[]{:S(2)}) collective-permute-start(f32[3,16,128]{2,1,0:T(8,128)S(1)} %get-tuple-element.42), channel_id=1, source_target_pairs={{2,0},{4,2},{6,4},{8,6},{10,8},{12,10},{14,12},{16,14},{18,16},{20... | collective-permute-start | bytes 73736 | tf_op jit(solution)/shard_map/ppermute | solution.py:468
  24.3 1.7 %collective-permute-done.4.refs_3_ = f32[3,16,128]{2,1,0:T(8,128)S(1)} collective-permute-done((f32[3,16,128]{2,1,0:T(8,128)S(1)}, f32[3,16,128]{2,1,0:T(8,128)S(1)}, u32[]{:S(2)}, u32[]{:S(2)}) %collective-permute-start.4) | collective-permute-done | bytes 24608 | tf_op jit(solution)/shard_map/ppermute | solution.py:468
  26.0 0.0 collective-permute-done.5.refs_4_
  26.0 0.9 %advance.1 = f32[3,8,16,128]{3,2,1,0:T(8,128)} custom-call(f32[3,8,16,128]{3,2,1,0:T(8,128)S(1)} %get-tuple-element.24.refs_0_, f32[8,16,128]{2,1,0:T(8,128)S(1)} %get-tuple-element.38.refs_1_, f32[3,8,16,128]{3,2,1,0:T(8,128)S(1)} %get-tuple-element.39.refs_0_.refs_2_, f32[3,16,128]{2,1,0:T(8,128)S(1)} %collective-permute-done.4.refs_3_, ...), custom_call_target="tpu_custom_call" | custom-call | tf_op jit(solution)/shard_map/advance/pallas_call | solution.py:438
Async XLA Ops:
  4.2 1.4 %collective-permute-start = (f32[8,128]{1,0:T(8,128)S(1)}, f32[8,128]{1,0:T(8,128)S(1)}, u32[]{:S(2)}, u32[]{:S(2)}) collective-permute-start(f32[8,128]{1,0:T(8,128)S(1)} %get-tuple-element.35), channel_id=1, source_target_pairs={{0,1},{1,0},{2,3},{3,2},{4,5},{5,4},{6,7},{7,6},{8,9},{9,8},{10,11... | collective-permute-start | bytes 12296 | tf_op jit(solution)/shard_map/ppermute | solution.py:459
  5.7 8.8 %collective-permute-start.1 = (f32[4,16,128]{2,1,0:T(8,128)S(1)}, f32[4,16,128]{2,1,0:T(8,128)S(1)}, u32[]{:S(2)}, u32[]{:S(2)}) collective-permute-start(f32[4,16,128]{2,1,0:T(8,128)S(1)} %get-tuple-element.36), channel_id=1, source_target_pairs={{0,2},{2,4},{4,6},{6,8},{8,10},{10,12},{12,14},{14,16},{16,18},{18... | collective-permute-start | bytes 98312 | tf_op jit(solution)/shard_map/ppermute | solution.py:468
  8.6 5.9 %collective-permute-start.2 = (f32[4,16,128]{2,1,0:T(8,128)S(1)}, f32[4,16,128]{2,1,0:T(8,128)S(1)}, u32[]{:S(2)}, u32[]{:S(2)}) collective-permute-start(f32[4,16,128]{2,1,0:T(8,128)S(1)} %get-tuple-element.37), channel_id=1, source_target_pairs={{2,0},{4,2},{6,4},{8,6},{10,8},{12,10},{14,12},{16,14},{18,16},{20... | collective-permute-start | bytes 98312 | tf_op jit(solution)/shard_map/ppermute | solution.py:468
  17.1 1.2 %collective-permute-start.3 = (f32[8,128]{1,0:T(8,128)S(1)}, f32[8,128]{1,0:T(8,128)S(1)}, u32[]{:S(2)}, u32[]{:S(2)}) collective-permute-start(f32[8,128]{1,0:T(8,128)S(1)} %get-tuple-element.40), channel_id=1, source_target_pairs={{0,1},{1,0},{2,3},{3,2},{4,5},{5,4},{6,7},{7,6},{8,9},{9,8},{10,11... | collective-permute-start | bytes 12296 | tf_op jit(solution)/shard_map/ppermute | solution.py:459
  18.5 7.5 %collective-permute-start.4 = (f32[3,16,128]{2,1,0:T(8,128)S(1)}, f32[3,16,128]{2,1,0:T(8,128)S(1)}, u32[]{:S(2)}, u32[]{:S(2)}) collective-permute-start(f32[3,16,128]{2,1,0:T(8,128)S(1)} %get-tuple-element.41), channel_id=1, source_target_pairs={{0,2},{2,4},{4,6},{6,8},{8,10},{10,12},{12,14},{14,16},{16,18},{18... | collective-permute-start | bytes 73736 | tf_op jit(solution)/shard_map/ppermute | solution.py:468
  18.9 7.1 %collective-permute-start.5 = (f32[3,16,128]{2,1,0:T(8,128)S(1)}, f32[3,16,128]{2,1,0:T(8,128)S(1)}, u32[]{:S(2)}, u32[]{:S(2)}) collective-permute-start(f32[3,16,128]{2,1,0:T(8,128)S(1)} %get-tuple-element.42), channel_id=1, source_target_pairs={{2,0},{4,2},{6,4},{8,6},{10,8},{12,10},{14,12},{16,14},{18,16},{20... | collective-permute-start | bytes 73736 | tf_op jit(solution)/shard_map/ppermute | solution.py:468

commit v3 on v2

v3 whole, which is shorter than its diff:
```python
import functools

import jax
import jax.numpy as jnp
import numpy as np
from jax import lax
from jax.experimental import pallas as pl
from jax.experimental.pallas import tpu as pltpu
from jax.sharding import PartitionSpec as P

VISCOSITY = 0.05
STEP_SIZE = 0.01
GLL_INNER = [
    -0.8717401485096066,
    -0.5917001814331423,
    -0.2092992179024789,
    0.2092992179024789,
    0.5917001814331423,
    0.8717401485096066,
]
GAUSS_POINTS = [
    -0.9815606342467192,
    -0.9041172563704749,
    -0.7699026741943047,
    -0.5873179542866175,
    -0.3678314989981802,
    -0.1252334085114689,
    0.1252334085114689,
    0.3678314989981802,
    0.5873179542866175,
    0.7699026741943047,
    0.9041172563704749,
    0.9815606342467192,
]
GAUSS_WEIGHTS = [
    0.0471753363865118,
    0.1069393259953184,
    0.1600783285433462,
    0.2031674267230659,
    0.2334925365383548,
    0.2491470458134028,
    0.2491470458134028,
    0.2334925365383548,
    0.2031674267230659,
    0.1600783285433462,
    0.1069393259953184,
    0.0471753363865118,
]
F32 = jnp.float32
BF16 = jnp.bfloat16
XY = 64
QQ = 144
LANES = 128
PART_PLANES = ([0, 7], [1, 2, 3, 4, 5, 6])
PART_ROWS = [[8 * x + y for x in planes for y in range(8)] for planes in PART_PLANES]
PAIRS = [(0, 1), (2, 3), (4, 5), (6, 7), (8,)]


def legendre_seven(points):
    previous = points * 0.0 + 1.0
    current = points
    for degree in range(1, 7):
        following = ((2.0 * degree + 1.0) * points * current - degree * previous) / (degree + 1.0)
        previous = current
        current = following
    return current


def node_tables():
    gll_nodes = np.array([-1.0] + GLL_INNER + [1.0])
    values = legendre_seven(gll_nodes)
    node_weights = 2.0 / (56.0 * values * values)
    identity = np.eye(8, dtype=bool)
    spacing = gll_nodes[:, None] - gll_nodes[None, :]
    derivative = np.where(
        identity, 0.0, values[:, None] / (values[None, :] * np.where(identity, 1.0, spacing))
    )
    corner_terms = np.concatenate([np.array([-14.0]), np.zeros(6), np.array([14.0])])
    derivative = derivative + np.eye(8) * corner_terms[None, :]
    gauss_nodes = np.array(GAUSS_POINTS)
    gauss_weights = np.array(GAUSS_WEIGHTS)
    numerators = gauss_nodes[:, None, None] - gll_nodes[None, None, :]
    denominators = np.where(identity, 1.0, spacing)[None]
    ratios = np.where(identity[None], 1.0, numerators / denominators)
    interpolation = ratios.prod(axis=2)
    slope_interp = interpolation @ derivative
    return (derivative, node_weights, interpolation, slope_interp, gauss_weights)


def halves(matrix):
    high = np.asarray(matrix, np.float32).astype(jnp.bfloat16)
    low = (np.asarray(matrix, np.float64) - high.astype(np.float64)).astype(jnp.bfloat16)
    return high, low


def lane_tiles(table):
    rows, columns = table.shape
    padded = np.pad(table, ((0, 0), (0, -columns % LANES)))
    return padded.reshape(rows, -1, LANES).transpose(1, 0, 2)


def constants():
    dm, rho, jm, dj, sigma = node_tables()
    def forward_block(matrix):
        high, low = halves(matrix)
        return np.block([[high, low], [high, np.zeros_like(low)]])

    dz = np.kron(np.eye(16), dm.T)
    jz = np.kron(np.eye(16), jm.T)
    last = np.concatenate([jz[:, LANES:], np.zeros((LANES, 64))], axis=1)
    z_forward = np.concatenate(
        [forward_block(dz), forward_block(jz[:, :LANES]), forward_block(last)], axis=1
    )
    def three(matrix):
        high, low = halves(matrix)
        return np.concatenate([high, high, low], axis=1)

    jj = three(np.kron(jm, jm))
    eye = np.eye(8)
    grads = three(np.concatenate([np.kron(dm, eye), np.kron(eye, dm)], axis=0))
    js, ds = sigma[:, None] * jm, sigma[:, None] * dj

    def stacked(matrix):
        high, low = halves(matrix)
        return np.concatenate(
            [
                np.concatenate([high, high], axis=1),
                np.concatenate([low, np.zeros_like(low)], axis=1),
            ],
            axis=0,
        )

    back_12 = np.concatenate([np.kron(ds, js).T, np.kron(js, ds).T], axis=1)
    back_3 = np.kron(js, js).T
    div = np.concatenate([np.kron(dm.T, eye), np.kron(eye, dm.T)], axis=1)
    by_part = []
    for rows in PART_ROWS:
        by_part += [stacked(back_12[rows]), stacked(back_3[rows]), three(div[rows])]
    def back_block(matrix):
        padded = np.concatenate([matrix, np.zeros((64, LANES))], axis=0)
        high, low = halves(padded)
        return [
            np.concatenate([high, low], axis=1),
            np.concatenate([high, np.zeros_like(low)], axis=1),
        ]

    jz_back = np.kron(np.eye(16), js)
    dz_back = np.kron(np.eye(16), ds)
    z_back = np.concatenate(
        back_block(jz_back) + back_block(dz_back) + [forward_block(np.kron(np.eye(16), dm))], axis=0
    )
    weights = np.einsum("x,y,z->xyz", rho, rho, np.tile(rho, 16)).reshape(XY, LANES)
    return (
        [lane_tiles(t) for t in (z_forward, jj, grads, z_back, *by_part)],
        np.asarray(weights, np.float32),
    )


def split(values):
    high = values.astype(BF16)
    low = (values - high.astype(F32)).astype(BF16)
    return high, low


def dot(left, right):
    return jnp.dot(left, right, preferred_element_type=F32)


def wide(tiles, columns=None):
    whole = jnp.concatenate([tiles[k] for k in range(tiles.shape[0])], axis=1)
    return whole if columns is None else whole[:, :columns]


def fold(values):
    return values[:, :LANES] + values[:, LANES : 2 * LANES]


def section_rows(block, e):
    return block.reshape(8, 2, 8, LANES)[:, e].reshape(XY, LANES)


def interpolate_wall(js_ref, first, last):
    for c in range(3):
        rows = slice(c * XY, (c + 1) * XY)
        tiles = [first[0][rows], first[1][rows]]
        tiles.append(last[0][rows] + pltpu.roll(last[1][rows], 64, 1))
        for t, tile in enumerate(tiles):
            high, low = split(tile)
            js_ref[3 * c + t, 0:XY] = high
            js_ref[3 * c + t, XY : 2 * XY] = low
            js_ref[3 * c + t, 2 * XY : 3 * XY] = high


def tiles_at(ref, tiles, rows=slice(None)):
    return jnp.concatenate([ref[k, rows] for k in tiles], axis=1)


def columns(values, count):
    return [values[:, k * LANES : (k + 1) * LANES] for k in range(count)]


def fine_flow(base_ref, tables, scratch, u_ref):
    z_forward, jj = tables[0], tables[1]
    xhl, js = scratch["xhl"], scratch["js"]
    first, last = [], []
    for e in range(2):
        for c in range(3):
            rows = slice(c * XY, (c + 1) * XY)
            xhl[e, 0, rows], xhl[e, 1, rows] = split(section_rows(base_ref[c], e))
        out = dot(wide(xhl.at[e]), wide(z_forward.at[2:]))
        first.append(fold(out[:, : 2 * LANES]))
        last.append(fold(out[:, 2 * LANES :]))
    interpolate_wall(js, first, last)
    for pair in PAIRS:
        out = dot(wide(jj, 3 * XY), tiles_at(js, pair))
        for k, tile in zip(pair, columns(out, len(pair))):
            u_ref[k] = tile


def front(rows_of, u_ref, metric, tables, scratch, kept):
    z_forward, jj, grads = tables[:3]
    xhl, js, vs = (scratch[k] for k in ("xhl", "js", "vs"))
    ts, hs, h3s = kept
    gz, first, last = [], [], []
    for e in range(2):
        for c in range(3):
            rows = slice(c * XY, (c + 1) * XY)
            high, low = split(rows_of(c, e))
            xhl[e, 0, rows], xhl[e, 1, rows] = high, low
            vs[2 * c + e, 0:XY] = high
            vs[2 * c + e, XY : 2 * XY] = low
            vs[2 * c + e, 2 * XY : 3 * XY] = high
        out = dot(wide(xhl.at[e]), wide(z_forward))
        gz.append(fold(out[:, : 2 * LANES]))
        first.append(fold(out[:, 2 * LANES : 4 * LANES]))
        last.append(fold(out[:, 4 * LANES :]))
    interpolate_wall(js, first, last)

    def flux(c):
        rows = slice(c * XY, (c + 1) * XY)
        gxy = dot(wide(grads, 3 * XY), tiles_at(vs, (2 * c, 2 * c + 1)))
        for e in range(2):
            lanes = slice(e * LANES, (e + 1) * LANES)
            g1, g2, g3 = gxy[:XY, lanes], gxy[XY:, lanes], gz[e][rows]
            m11, m22, m33, m12, m13, m23 = (metric[k, e] for k in range(6))
            h1 = m11 * g1 + m12 * g2 + m13 * g3
            h2 = m12 * g1 + m22 * g2 + m23 * g3
            h3 = m13 * g1 + m23 * g2 + m33 * g3
            h1h, h1l = split(h1)
            h2h, h2l = split(h2)
            for k, part in enumerate((h1h, h2h, h1l, h2l, h1h, h2h)):
                hs[2 * c + e, k * XY : (k + 1) * XY] = part
            h3s[2 * c + e] = h3

    def gauss(pair):
        fine = dot(wide(jj, 3 * XY), tiles_at(js, pair))
        for k, tile in zip(pair, columns(fine, len(pair))):
            for d in range(3):
                start = (0, QQ, 4 * QQ)[d]
                gap = (2 * QQ, 2 * QQ, QQ)[d]
                high, low = split(u_ref[3 * d + k % 3] * tile)
                ts[k, start : start + QQ] = high
                ts[k, start + gap : start + gap + QQ] = low

    gauss(PAIRS[0])
    flux(0)
    gauss(PAIRS[1])
    flux(1)
    gauss(PAIRS[2])
    flux(2)
    gauss(PAIRS[3])
    gauss(PAIRS[4])


def back(part, tables, scratch, kept):
    z_back, back_12, back_3, div = tables
    ts, hs, h3s = kept
    bz = scratch["bz"]
    planes = PART_PLANES[part]
    count = 8 * len(planes)
    result = [[None, None] for _ in range(3)]
    sides = [{}, {}]
    for pair in PAIRS:
        for k, (table, depth, where) in enumerate(
            ((back_12, 4 * QQ, slice(0, 4 * QQ)), (back_3, 2 * QQ, slice(4 * QQ, None)))
        ):
            both = dot(wide(table, depth), tiles_at(ts, pair, where))
            both = both[:count] + both[count:]
            for tile, values in zip(pair, columns(both, len(pair))):
                sides[k][tile] = values
    for c in range(3):
        spread = columns(dot(wide(div), tiles_at(hs, (2 * c, 2 * c + 1))), 2)
        for e in range(2):
            result[c][e] = spread[e]
            rows = slice((2 * c + e) * count, (2 * c + e + 1) * count)
            for k in range(2):
                far = sides[k][3 * c + 2]
                far = far if e == 0 else pltpu.roll(far, 64, 1)
                for t, tile in enumerate((sides[k][3 * c + e], far)):
                    bz[4 * k + t, rows], bz[4 * k + t + 2, rows] = split(tile)
            bz[8, rows], bz[9, rows] = split(part_rows(part, h3s[2 * c + e]))
    out = fold(dot(wide(bz), wide(z_back)))
    for c in range(3):
        for e in range(2):
            result[c][e] += out[(2 * c + e) * count : (2 * c + e + 1) * count]
    return result


def part_rows(part, tall):
    return jnp.concatenate([tall[8 * x : 8 * x + 8] for x in PART_PLANES[part]], axis=0)


def sum_local(pair, out_ref, slot):
    shape = (out_ref.shape[1], 8, LANES)
    row = lax.broadcasted_iota(jnp.int32, shape, 1)
    lane = lax.broadcasted_iota(jnp.int32, shape, 2)
    inner = lane % 8
    for e in range(2):
        mine = pair[e].reshape(shape)
        other = pair[1 - e].reshape(shape)
        total = mine + jnp.where(row == 7, pltpu.roll(other, 7, 1), 0.0)
        total = total + jnp.where(row == 0, pltpu.roll(other, 1, 1), 0.0)
        after = pltpu.roll(total, LANES - 1, 2)
        before = pltpu.roll(total, 1, 2)
        total = (
            total
            + jnp.where((inner == 7) & (lane < LANES - 1), after, 0.0)
            + jnp.where((inner == 0) & (lane > 0), before, 0.0)
        )
        out_ref[slot, :, 8 * e : 8 * (e + 1), :] = total


def positions():
    c = lax.axis_index("col")
    return c % 2, c == 0, c == lax.axis_size("col") - 1


def places(ref):
    fields, planes = ref.shape[:2]
    return [
        (slot, x, e, (slot * planes + x) * 2 + e)
        for slot in range(fields)
        for x in range(planes)
        for e in range(2)
    ]


def pack_edges(sum_ref, edge_ref):
    lane = lax.broadcasted_iota(jnp.int32, (8, LANES), 1)
    packed = jnp.zeros((8, LANES), F32)
    for slot, x, e, at in places(sum_ref):
        tile = sum_ref[slot, x, 8 * e : 8 * (e + 1), :]
        packed = jnp.where(lane == at, pltpu.roll(tile, (at + 1) % LANES, 1), packed)
        packed = jnp.where(lane == 64 + at, pltpu.roll(tile, 64 + at, 1), packed)
    edge_ref[...] = packed


def received_edges(edge_refs):
    col_odd, _, _ = positions()
    lane = lax.broadcasted_iota(jnp.int32, (8, LANES), 1)
    total = jnp.zeros((8, LANES), F32)
    for k, ref in enumerate(edge_refs):
        high = (col_odd == 0) if k == 0 else (col_odd == 1)
        total = total + jnp.where((lane < 64) == high, pltpu.roll(ref[...], 64, 1), 0.0)
    return total


def with_edges(sum_ref, edge_refs):
    edges = received_edges(edge_refs)
    lane = lax.broadcasted_iota(jnp.int32, (8, LANES), 1)
    tiles = {}
    for slot, x, e, at in places(sum_ref):
        add = jnp.where(lane == LANES - 1, pltpu.roll(edges, LANES - 1 - at, 1), 0.0)
        add = jnp.where(lane == 0, pltpu.roll(edges, (64 - at) % LANES, 1), add)
        tiles[slot, x, e] = sum_ref[slot, x, 8 * e : 8 * (e + 1), :] + add
    return tiles


def planes_kernel(count, *refs):
    outer, edge_refs, (up, down) = refs[0], refs[1 : 1 + count], refs[-2:]
    for (slot, x, e), tile in with_edges(outer, edge_refs).items():
        (up if x else down)[slot, 8 * e : 8 * (e + 1), :] = tile


def arrived(outer_ref, edge_refs, up_ref, down_ref):
    tiles = with_edges(outer_ref, edge_refs)
    for slot, x, e in tiles:
        tiles[slot, x, e] += (down_ref if x else up_ref)[slot, 8 * e : 8 * (e + 1), :]
    return tiles


def interior_mask():
    _, first, last = positions()
    lane = lax.broadcasted_iota(jnp.int32, (1, LANES), 1)
    outer = ((lane == 0) & first) | ((lane == LANES - 1) & last)
    return jnp.where(outer, 0.0, 1.0)


def scale_metric(diag_ref, cross_ref, weights, metric):
    for k in range(6):
        ref = diag_ref if k < 3 else cross_ref
        block = ref[k % 3].astype(F32)
        for e in range(2):
            metric[k, e] = section_rows(block, e) * weights[...] * VISCOSITY


def finish(part, kept, tables, scratch, total, edge, mass=None):
    result = back(part, tables, scratch, kept)
    for c in range(3):
        sum_local(result[c], total, c)
    if mass is not None:
        jac, w = mass
        rows = [part_rows(part, section_rows(jac[...], e) * w[...]) for e in range(2)]
        sum_local(rows, total, 3)
    pack_edges(total, edge)


def first_kernel(*refs):
    sources, refs = refs[:16], refs[16:]
    v, tables, (jac, w, u, metric, *kept) = refs[0], refs[1:11], refs[11:18]
    total, edge, b, gd, gc, sems = refs[18:24]
    scratch = dict(zip(SCRATCH_NAMES, refs[24:]))
    targets = [b, tables[0], tables[1], v, gd, gc, w, jac, *tables[2:]]
    copies = [
        pltpu.make_async_copy(source, target, sems.at[k])
        for k, (source, target) in enumerate(zip(sources, targets))
    ]
    for copy in copies:
        copy.start()
    for copy in copies[:3]:
        copy.wait()
    fine_flow(b, tables, scratch, u)
    for copy in copies[3:]:
        copy.wait()
    scale_metric(gd, gc, w, metric)
    front(lambda c, e: section_rows(v[c], e), u, metric, tables, scratch, kept)
    finish(0, kept, tables[3:7], scratch, total, edge, (jac, w))


def inner_kernel(has_mass, *refs):
    kept, tables, refs = refs[:3], refs[3:7], refs[7:]
    mass, refs = (refs[:2], refs[2:]) if has_mass else (None, refs)
    total, edge, *rest = refs
    finish(1, kept, tables, dict(zip(SCRATCH_NAMES, rest)), total, edge, mass)


def second_kernel(edges, *refs):
    v, tables, (u, metric) = refs[0], refs[1:8], refs[8:10]
    outer, inner_sum, up_in, down_in = refs[10:14]
    outer_edges, inner_edges, refs = (
        refs[14 : 14 + edges],
        refs[14 + edges : 14 + 2 * edges],
        refs[14 + 2 * edges :],
    )
    inverse, kept, (total, edge) = refs[0], refs[1:4], refs[4:6]
    scratch = dict(zip(SCRATCH_NAMES + ["half"], refs[6:]))
    half = scratch["half"]
    mask = interior_mask()
    for part, tiles in enumerate(
        (arrived(outer, outer_edges, up_in, down_in), with_edges(inner_sum, inner_edges))
    ):
        for k, x in enumerate(PART_PLANES[part]):
            for e in range(2):
                rows = slice(8 * e, 8 * (e + 1))
                inv = 1.0 / tiles[3, k, e]
                inverse[x, rows] = inv
                for c in range(3):
                    step = (0.5 * STEP_SIZE) * inv * tiles[c, k, e]
                    half[c, x, rows] = mask * (v[c, x, rows] - step)
    front(lambda c, e: section_rows(half[c], e), u, metric, tables, scratch, kept)
    finish(0, kept, tables[3:7], scratch, total, edge)


def advance_kernel(edges, *refs):
    v, inverse, outer, inner_sum, up_in, down_in = refs[:6]
    outer_edges, inner_edges = refs[6 : 6 + edges], refs[6 + edges : 6 + 2 * edges]
    out, held, sems = refs[6 + 2 * edges :]
    mask = interior_mask()
    inner, outermost = with_edges(inner_sum, inner_edges), arrived(outer, outer_edges, up_in, down_in)
    copies = []
    for c in range(3):
        for part, tiles in enumerate((outermost, inner)):
            for k, x in enumerate(PART_PLANES[part]):
                for e in range(2):
                    rows = slice(8 * e, 8 * (e + 1))
                    step = STEP_SIZE * inverse[x, rows] * tiles[c, k, e]
                    held[c, x, rows] = mask * (v[c, x, rows] - step)
        copies.append(pltpu.make_async_copy(held.at[c], out.at[c], sems.at[c]))
        copies[-1].start()
    for copy in copies:
        copy.wait()


SCRATCH_NAMES = ["bz", "xhl", "js", "vs"]


def scratch_shapes(part=None):
    bz = pltpu.VMEM((10, 6 * 8 * len(PART_PLANES[part]), LANES), BF16)
    front_scratch = [
        pltpu.VMEM((2, 2, 3 * XY, LANES), BF16),
        pltpu.VMEM((9, 3 * XY, LANES), BF16),
        pltpu.VMEM((6, 3 * XY, LANES), BF16),
    ]
    return [bz] + (front_scratch if part == 0 else [])


def call(kernel, name, ins, outs, scratch, in_space=pltpu.VMEM, out_space=pltpu.VMEM):
    ins = [pltpu.with_memory_space_constraint(array, in_space) for array in ins]
    return pl.pallas_call(
        kernel,
        name=name,
        out_shape=[out_space(shape, dtype) for shape, dtype in outs],
        in_specs=[pl.BlockSpec(memory_space=in_space)] * len(ins),
        out_specs=[pl.BlockSpec(memory_space=out_space)] * len(outs),
        scratch_shapes=scratch,
        compiler_params=pltpu.CompilerParams(vmem_limit_bytes=24 * 1024 * 1024),
    )(*ins)


def wall_pairings(count):
    even = [(i, i + 1) for i in range(0, count - 1, 2)]
    odd = [(i, i + 1) for i in range(1, count - 1, 2)]
    return [pairs + [(b, a) for a, b in pairs] for pairs in (even, odd) if pairs]


def swap_edges(edge):
    return [lax.ppermute(edge, "col", way) for way in wall_pairings(lax.axis_size("col"))]


def local(adjoint_field, base_flow, metric_diag, metric_cross, jacobian):
    tables, weights = constants()
    tables = [jnp.asarray(table, BF16) for table in tables]
    weights = jnp.asarray(weights)
    block = adjoint_field.shape[1:]
    field = ((3,) + block, F32)
    kept_shapes = [
        ((9, 6 * QQ, LANES), BF16),
        ((6, 6 * XY, LANES), BF16),
        ((6, XY, LANES), F32),
    ]
    edge_shape = ((8, LANES), F32)
    spans = lax.axis_size("span")
    ahead = [(i, (i + 1) % spans) for i in range(spans)]
    back_way = [(b, a) for a, b in ahead]

    def sums(fields, part):
        return [((fields, len(PART_PLANES[part])) + block[1:], F32), edge_shape]

    def exchange(fields, outer, outer_edge, kept, late_tables, mass):
        outer_edges = swap_edges(outer_edge)
        inner, inner_edge = call(
            functools.partial(inner_kernel, len(mass) > 0),
            "inner_planes",
            kept + late_tables + mass,
            sums(fields, 1),
            scratch_shapes(1),
        )
        up, down = call(
            functools.partial(planes_kernel, len(outer_edges)),
            "planes",
            [outer] + outer_edges + [inner_edge],
            [((fields,) + block[1:], F32)] * 2,
            [],
        )
        inner_edges = swap_edges(inner_edge)
        up, down = lax.ppermute(up, "span", ahead), lax.ppermute(down, "span", back_way)
        return up, down, outer_edges, inner, inner_edges

    ins = [base_flow, tables[0], tables[1], adjoint_field, metric_diag, metric_cross]
    ins += [weights, jacobian] + tables[2:]
    out = call(
        first_kernel,
        "first_operator",
        ins,
        [field]
        + [(table.shape, BF16) for table in tables]
        + [(block, F32), (weights.shape, F32)]
        + [((9, QQ, LANES), F32), ((6, 2, XY, LANES), F32)]
        + kept_shapes
        + sums(4, 0),
        [
            pltpu.VMEM((3,) + block, F32),
            pltpu.VMEM((3,) + block, BF16),
            pltpu.VMEM((3,) + block, BF16),
            pltpu.SemaphoreType.DMA((len(ins),)),
        ]
        + scratch_shapes(0),
        in_space=pltpu.HBM,
    )
    v, tables, (jac, w, u, metric), kept = out[0], out[1:11], out[11:15], out[15:18]
    tables, kept = list(tables), list(kept)
    outer, outer_edge = out[18:]
    late_tables = [tables[3]] + tables[7:10]
    up, down, outer_edges, inner, inner_edges = exchange(
        4, outer, outer_edge, kept, late_tables, [jac, w]
    )
    inverse, *kept, outer, outer_edge = call(
        functools.partial(second_kernel, len(outer_edges)),
        "second_operator",
        [v] + tables[:7] + [u, metric, outer, inner, up, down] + outer_edges + inner_edges,
        [(block, F32)] + kept_shapes + sums(3, 0),
        scratch_shapes(0) + [pltpu.VMEM((3,) + block, F32)],
    )
    up, down, outer_edges, inner, inner_edges = exchange(
        3, outer, outer_edge, kept, late_tables, []
    )
    (out,) = call(
        functools.partial(advance_kernel, len(outer_edges)),
        "advance",
        [v, inverse, outer, inner, up, down] + outer_edges + inner_edges,
        [field],
        [pltpu.VMEM((3,) + block, F32), pltpu.SemaphoreType.DMA((3,))],
        out_space=pltpu.HBM,
    )
    return out


def solution(mesh):
    in_specs = (
        P(None, "span", None, "col"),
        P(None, "span", None, "col"),
        P(None, "span", None, "col"),
        P(None, "span", None, "col"),
        P("span", None, "col"),
    )
    out_specs = P(None, "span", None, "col")
    return jax.shard_map(local, mesh=mesh, in_specs=in_specs, out_specs=out_specs, check_vma=False)
```

time: 27.1 us -> 25.7 us (0.948)
  waiting for transfers between devices: 5.55 us -> 3.45 us
  Pallas kernels: 8.02 us -> 8.75 us
    ppermute x2, waiting for transfers between devices: 3.57 us -> 1.39 us  [exchange(): lax.ppermute(up, 'span', ahead)]
    pallas_call x5 -> x7, Pallas kernels: 8.02 us -> 8.75 us  [call(): pl.pallas_call(kernel, name=name, out_shape=[out_space(shape, dtype) for...]
    ppermute x2, starting transfers between devices: 3.34 us -> 2.92 us  [exchange(): lax.ppermute(up, 'span', ahead)]
    ppermute x4 -> x6, starting transfers between devices: 9.98 us -> 10.3 us  [the longest x2 9.4 us: exchange(): lax.ppermute(down, 'span', back_way)]
    ppermute x4 -> x6, waiting for transfers between devices: 1.98 us -> 2.06 us  [the longest x4 2.05 us: swap_edges(): lax.ppermute(edge, 'col', way)]
  transfers between devices with their start and end apart: 6 -> 8, of which waited for: 4 -> 5; matrix products, arithmetic and copies ran while one was open for 0% -> 0% of each run, Pallas kernels for 0% -> 9%
where the time goes in v3:
time: 25.7 us; the launch traced here: 25.5 us
  starting transfers between devices  13.3 us (52%)
  Pallas kernels  8.75 us (34%)
  waiting for transfers between devices  3.45 us (13%)
    ppermute x2, starting transfers between devices, exchange(): lax.ppermute(down, 'span', back_way)  9.4 us
    pallas_call x7, Pallas kernels, call(): pl.pallas_call(kernel, name=name, out_shape=[out_space(shape, dtype) for...  8.75 us
    ppermute x2, starting transfers between devices, exchange(): lax.ppermute(up, 'span', ahead)  2.92 us
    ppermute x4, waiting for transfers between devices, swap_edges(): lax.ppermute(edge, 'col', way)  2.05 us
    ppermute x2, waiting for transfers between devices, exchange(): lax.ppermute(up, 'span', ahead)  1.39 us
    ppermute x4, starting transfers between devices, swap_edges(): lax.ppermute(edge, 'col', way)  0.94 us
  transfers between devices with their start and end apart: 8, of which 5 were waited for; matrix products, arithmetic and copies ran while one was open for 0% of the time, Pallas kernels for 9%

profile of v3, /device:TPU:0, one launch (start us, length us, event | category | flops | bytes accessed | tf_op | source)
XLA Modules:
  0.0 25.5 jit_solution(5953493252861587267)
XLA Ops:
  0.0 3.5 %first_operator.1 = (f32[3,8,16,128]{3,2,1,0:T(8,128)S(1)}, bf16[6,256,128]{2,1,0:T(8,128)(2,1)S(1)}, bf16[2,144,128]{2,1,0:T(8,128)(2,1)S(1)}, bf16[2,128,128]{...) custom-call(f32[3,8,16,128]{3,2,1,0:T(8,128)} %refs_0_.1, ...), custom_call_target="tpu_custom_call" | custom-call | tf_op jit(solution)/shard_map/first_operator/pallas_call | solution.py:509
  3.5 0.5 %collective-permute-start = (f32[8,128]{1,0:T(8,128)S(1)}, f32[8,128]{1,0:T(8,128)S(1)}, u32[]{:S(2)}, u32[]{:S(2)}) collective-permute-start(f32[8,128]{1,0:T(8,128)S(1)} %get-tuple-element.59), channel_id=1, source_target_pairs={{0,1},{1,0},{2,3},{3,2},{4,5},{5,4},{6,7},{7,6},{8,9},{9,8},{10,11... | collective-permute-start | bytes 12296 | tf_op jit(solution)/shard_map/ppermute | solution.py:527
  4.0 1.1 %inner_planes.2 = (f32[4,6,16,128]{3,2,1,0:T(8,128)S(1)}, f32[8,128]{1,0:T(8,128)S(1)}) custom-call(bf16[9,864,128]{2,1,0:T(8,128)(2,1)S(1)} %get-tuple-element.50.refs_0_, bf16[6,384,128]{2,1,0:T(8,128)(2,1)S(1)} %get-tuple-element.51.refs_1_, f32[6,64,128]{2,1,0:T(8,128)S(1)} %get-tuple-element.52.refs_2_, ...), custom_call_target="tpu_custom_call" | custom-call | tf_op jit(solution)/shard_map/inner_planes/pallas_call | solution.py:509
  5.1 0.0 collective-permute-done.refs_1_.refs_14_
  5.1 0.2 planes.2
  5.3 2.6 %collective-permute-start.1 = (f32[4,16,128]{2,1,0:T(8,128)S(1)}, f32[4,16,128]{2,1,0:T(8,128)S(1)}, u32[]{:S(2)}, u32[]{:S(2)}) collective-permute-start(f32[4,16,128]{2,1,0:T(8,128)S(1)} %get-tuple-element.61), channel_id=1, source_target_pairs={{0,2},{2,4},{4,6},{6,8},{8,10},{10,12},{12,14},{14,16},{16,18},{18... | collective-permute-start | bytes 98312 | tf_op jit(solution)/shard_map/ppermute | solution.py:566
  7.9 4.1 %collective-permute-start.2 = (f32[4,16,128]{2,1,0:T(8,128)S(1)}, f32[4,16,128]{2,1,0:T(8,128)S(1)}, u32[]{:S(2)}, u32[]{:S(2)}) collective-permute-start(f32[4,16,128]{2,1,0:T(8,128)S(1)} %get-tuple-element.62), channel_id=1, source_target_pairs={{2,0},{4,2},{6,4},{8,6},{10,8},{12,10},{14,12},{16,14},{18,16},{20... | collective-permute-start | bytes 98312 | tf_op jit(solution)/shard_map/ppermute | solution.py:566
  11.9 0.2 collective-permute-start.3
  12.1 1.0 %collective-permute-done.3.refs_15_ = f32[8,128]{1,0:T(8,128)S(1)} collective-permute-done((f32[8,128]{1,0:T(8,128)S(1)}, f32[8,128]{1,0:T(8,128)S(1)}, u32[]{:S(2)}, u32[]{:S(2)}) %collective-permute-start.3) | collective-permute-done | bytes 4128 | tf_op jit(solution)/shard_map/ppermute | solution.py:527
  13.1 0.8 %collective-permute-done.1.refs_12_ = f32[4,16,128]{2,1,0:T(8,128)S(1)} collective-permute-done((f32[4,16,128]{2,1,0:T(8,128)S(1)}, f32[4,16,128]{2,1,0:T(8,128)S(1)}, u32[]{:S(2)}, u32[]{:S(2)}) %collective-permute-start.1) | collective-permute-done | bytes 32800 | tf_op jit(solution)/shard_map/ppermute | solution.py:566
  13.9 0.0 collective-permute-done.2.refs_13_
  13.9 1.9 %second_operator.1 = (f32[8,16,128]{2,1,0:T(8,128)S(1)}, bf16[9,864,128]{2,1,0:T(8,128)(2,1)S(1)}, bf16[6,384,128]{2,1,0:T(8,128)(2,1)S(1)}, f32[6,64,128]{2,1,0...) custom-call(f32[3,8,16,128]{3,2,1,0:T(8,128)S(1)} %get-tuple-element.39.refs_0_, ...), custom_call_target="tpu_custom_call" | custom-call | tf_op jit(solution)/shard_map/second_operator/pallas_call | solution.py:509
  15.7 0.1 collective-permute-start.4
  15.8 1.1 %inner_planes.3 = (f32[3,6,16,128]{3,2,1,0:T(8,128)S(1)}, f32[8,128]{1,0:T(8,128)S(1)}) custom-call(bf16[9,864,128]{2,1,0:T(8,128)(2,1)S(1)} %get-tuple-element.65.refs_0_, bf16[6,384,128]{2,1,0:T(8,128)(2,1)S(1)} %get-tuple-element.66.refs_1_, f32[6,64,128]{2,1,0:T(8,128)S(1)} %get-tuple-element.67.refs_2_, ...), custom_call_target="tpu_custom_call" | custom-call | tf_op jit(solution)/shard_map/inner_planes/pallas_call | solution.py:509
  16.9 0.1 collective-permute-done.4.refs_1_.refs_6_
  17.0 0.2 planes.3
  17.1 0.3 %collective-permute-start.5 = (f32[3,16,128]{2,1,0:T(8,128)S(1)}, f32[3,16,128]{2,1,0:T(8,128)S(1)}, u32[]{:S(2)}, u32[]{:S(2)}) collective-permute-start(f32[3,16,128]{2,1,0:T(8,128)S(1)} %get-tuple-element.71), channel_id=1, source_target_pairs={{0,2},{2,4},{4,6},{6,8},{8,10},{10,12},{12,14},{14,16},{16,18},{18... | collective-permute-start | bytes 73736 | tf_op jit(solution)/shard_map/ppermute | solution.py:566
  17.5 5.3 %collective-permute-start.6 = (f32[3,16,128]{2,1,0:T(8,128)S(1)}, f32[3,16,128]{2,1,0:T(8,128)S(1)}, u32[]{:S(2)}, u32[]{:S(2)}) collective-permute-start(f32[3,16,128]{2,1,0:T(8,128)S(1)} %get-tuple-element.72), channel_id=1, source_target_pairs={{2,0},{4,2},{6,4},{8,6},{10,8},{12,10},{14,12},{16,14},{18,16},{20... | collective-permute-start | bytes 73736 | tf_op jit(solution)/shard_map/ppermute | solution.py:566
  22.8 0.2 collective-permute-start.7
  23.0 1.0 %collective-permute-done.7.refs_7_ = f32[8,128]{1,0:T(8,128)S(1)} collective-permute-done((f32[8,128]{1,0:T(8,128)S(1)}, f32[8,128]{1,0:T(8,128)S(1)}, u32[]{:S(2)}, u32[]{:S(2)}) %collective-permute-start.7) | collective-permute-done | bytes 4128 | tf_op jit(solution)/shard_map/ppermute | solution.py:527
  24.0 0.6 %collective-permute-done.5.refs_4_ = f32[3,16,128]{2,1,0:T(8,128)S(1)} collective-permute-done((f32[3,16,128]{2,1,0:T(8,128)S(1)}, f32[3,16,128]{2,1,0:T(8,128)S(1)}, u32[]{:S(2)}, u32[]{:S(2)}) %collective-permute-start.5) | collective-permute-done | bytes 24608 | tf_op jit(solution)/shard_map/ppermute | solution.py:566
  24.6 0.0 collective-permute-done.6.refs_5_
  24.6 0.9 %advance.1 = f32[3,8,16,128]{3,2,1,0:T(8,128)} custom-call(f32[3,8,16,128]{3,2,1,0:T(8,128)S(1)} %get-tuple-element.39.refs_0_, f32[8,16,128]{2,1,0:T(8,128)S(1)} %get-tuple-element.63.refs_1_, f32[3,2,16,128]{3,2,1,0:T(8,128)S(1)} %get-tuple-element.64.refs_0_.refs_2_, f32[3,6,16,128]{3,2,1,0:T(8,128)S(1)} %get-tuple-element.68.refs_3_, ...), custom_call_target="tpu_custom_call" | custom-call | tf_op jit(solution)/shard_map/advance/pallas_call | solution.py:509
Async XLA Ops:
  3.5 1.6 %collective-permute-start = (f32[8,128]{1,0:T(8,128)S(1)}, f32[8,128]{1,0:T(8,128)S(1)}, u32[]{:S(2)}, u32[]{:S(2)}) collective-permute-start(f32[8,128]{1,0:T(8,128)S(1)} %get-tuple-element.59), channel_id=1, source_target_pairs={{0,1},{1,0},{2,3},{3,2},{4,5},{5,4},{6,7},{7,6},{8,9},{9,8},{10,11... | collective-permute-start | bytes 12296 | tf_op jit(solution)/shard_map/ppermute | solution.py:527
  5.3 8.6 %collective-permute-start.1 = (f32[4,16,128]{2,1,0:T(8,128)S(1)}, f32[4,16,128]{2,1,0:T(8,128)S(1)}, u32[]{:S(2)}, u32[]{:S(2)}) collective-permute-start(f32[4,16,128]{2,1,0:T(8,128)S(1)} %get-tuple-element.61), channel_id=1, source_target_pairs={{0,2},{2,4},{4,6},{6,8},{8,10},{10,12},{12,14},{14,16},{16,18},{18... | collective-permute-start | bytes 98312 | tf_op jit(solution)/shard_map/ppermute | solution.py:566
  7.9 6.0 %collective-permute-start.2 = (f32[4,16,128]{2,1,0:T(8,128)S(1)}, f32[4,16,128]{2,1,0:T(8,128)S(1)}, u32[]{:S(2)}, u32[]{:S(2)}) collective-permute-start(f32[4,16,128]{2,1,0:T(8,128)S(1)} %get-tuple-element.62), channel_id=1, source_target_pairs={{2,0},{4,2},{6,4},{8,6},{10,8},{12,10},{14,12},{16,14},{18,16},{20... | collective-permute-start | bytes 98312 | tf_op jit(solution)/shard_map/ppermute | solution.py:566
  11.9 1.2 %collective-permute-start.3 = (f32[8,128]{1,0:T(8,128)S(1)}, f32[8,128]{1,0:T(8,128)S(1)}, u32[]{:S(2)}, u32[]{:S(2)}) collective-permute-start(f32[8,128]{1,0:T(8,128)S(1)} %get-tuple-element.60.refs_2_), channel_id=1, source_target_pairs={{0,1},{1,0},{2,3},{3,2},{4,5},{5,4},{6,7},{7,6},{8,9},{9,8},{10,11... | collective-permute-start | bytes 12296 | tf_op jit(solution)/shard_map/ppermute | solution.py:527
  15.7 1.2 %collective-permute-start.4 = (f32[8,128]{1,0:T(8,128)S(1)}, f32[8,128]{1,0:T(8,128)S(1)}, u32[]{:S(2)}, u32[]{:S(2)}) collective-permute-start(f32[8,128]{1,0:T(8,128)S(1)} %get-tuple-element.69), channel_id=1, source_target_pairs={{0,1},{1,0},{2,3},{3,2},{4,5},{5,4},{6,7},{7,6},{8,9},{9,8},{10,11... | collective-permute-start | bytes 12296 | tf_op jit(solution)/shard_map/ppermute | solution.py:527
  17.1 7.5 %collective-permute-start.5 = (f32[3,16,128]{2,1,0:T(8,128)S(1)}, f32[3,16,128]{2,1,0:T(8,128)S(1)}, u32[]{:S(2)}, u32[]{:S(2)}) collective-permute-start(f32[3,16,128]{2,1,0:T(8,128)S(1)} %get-tuple-element.71), channel_id=1, source_target_pairs={{0,2},{2,4},{4,6},{6,8},{8,10},{10,12},{12,14},{14,16},{16,18},{18... | collective-permute-start | bytes 73736 | tf_op jit(solution)/shard_map/ppermute | solution.py:566
  17.5 7.1 %collective-permute-start.6 = (f32[3,16,128]{2,1,0:T(8,128)S(1)}, f32[3,16,128]{2,1,0:T(8,128)S(1)}, u32[]{:S(2)}, u32[]{:S(2)}) collective-permute-start(f32[3,16,128]{2,1,0:T(8,128)S(1)} %get-tuple-element.72), channel_id=1, source_target_pairs={{2,0},{4,2},{6,4},{8,6},{10,8},{12,10},{14,12},{16,14},{18,16},{20... | collective-permute-start | bytes 73736 | tf_op jit(solution)/shard_map/ppermute | solution.py:566
  22.8 1.2 %collective-permute-start.7 = (f32[8,128]{1,0:T(8,128)S(1)}, f32[8,128]{1,0:T(8,128)S(1)}, u32[]{:S(2)}, u32[]{:S(2)}) collective-permute-start(f32[8,128]{1,0:T(8,128)S(1)} %get-tuple-element.70.refs_2_), channel_id=1, source_target_pairs={{0,1},{1,0},{2,3},{3,2},{4,5},{5,4},{6,7},{7,6},{8,9},{9,8},{10,11... | collective-permute-start | bytes 12296 | tf_op jit(solution)/shard_map/ppermute | solution.py:527

commit v4 on v3

v4 whole, which is shorter than its diff:
```python
import functools

import jax
import jax.numpy as jnp
import numpy as np
from jax import lax
from jax.experimental import pallas as pl
from jax.experimental.pallas import tpu as pltpu
from jax.sharding import PartitionSpec as P

VISCOSITY = 0.05
STEP_SIZE = 0.01
GLL_INNER = [
    -0.8717401485096066,
    -0.5917001814331423,
    -0.2092992179024789,
    0.2092992179024789,
    0.5917001814331423,
    0.8717401485096066,
]
GAUSS_POINTS = [
    -0.9815606342467192,
    -0.9041172563704749,
    -0.7699026741943047,
    -0.5873179542866175,
    -0.3678314989981802,
    -0.1252334085114689,
    0.1252334085114689,
    0.3678314989981802,
    0.5873179542866175,
    0.7699026741943047,
    0.9041172563704749,
    0.9815606342467192,
]
GAUSS_WEIGHTS = [
    0.0471753363865118,
    0.1069393259953184,
    0.1600783285433462,
    0.2031674267230659,
    0.2334925365383548,
    0.2491470458134028,
    0.2491470458134028,
    0.2334925365383548,
    0.2031674267230659,
    0.1600783285433462,
    0.1069393259953184,
    0.0471753363865118,
]
F32 = jnp.float32
BF16 = jnp.bfloat16
XY = 64
QQ = 144
LANES = 128
PART_PLANES = ([0, 7], [1, 2, 3, 4, 5, 6])
PART_ROWS = [[8 * x + y for x in planes for y in range(8)] for planes in PART_PLANES]
PAIRS = [(0, 1), (2, 3), (4, 5), (6, 7), (8,)]


def legendre_seven(points):
    previous = points * 0.0 + 1.0
    current = points
    for degree in range(1, 7):
        following = ((2.0 * degree + 1.0) * points * current - degree * previous) / (degree + 1.0)
        previous = current
        current = following
    return current


def node_tables():
    gll_nodes = np.array([-1.0] + GLL_INNER + [1.0])
    values = legendre_seven(gll_nodes)
    node_weights = 2.0 / (56.0 * values * values)
    identity = np.eye(8, dtype=bool)
    spacing = gll_nodes[:, None] - gll_nodes[None, :]
    derivative = np.where(
        identity, 0.0, values[:, None] / (values[None, :] * np.where(identity, 1.0, spacing))
    )
    corner_terms = np.concatenate([np.array([-14.0]), np.zeros(6), np.array([14.0])])
    derivative = derivative + np.eye(8) * corner_terms[None, :]
    gauss_nodes = np.array(GAUSS_POINTS)
    gauss_weights = np.array(GAUSS_WEIGHTS)
    numerators = gauss_nodes[:, None, None] - gll_nodes[None, None, :]
    denominators = np.where(identity, 1.0, spacing)[None]
    ratios = np.where(identity[None], 1.0, numerators / denominators)
    interpolation = ratios.prod(axis=2)
    slope_interp = interpolation @ derivative
    return (derivative, node_weights, interpolation, slope_interp, gauss_weights)


def halves(matrix):
    high = np.asarray(matrix, np.float32).astype(jnp.bfloat16)
    low = (np.asarray(matrix, np.float64) - high.astype(np.float64)).astype(jnp.bfloat16)
    return high, low


def lane_tiles(table):
    rows, columns = table.shape
    padded = np.pad(table, ((0, 0), (0, -columns % LANES)))
    return padded.reshape(rows, -1, LANES).transpose(1, 0, 2)


def three(matrix):
    high, low = halves(matrix)
    return np.concatenate([high, high, low], axis=1)


def stacked(matrix):
    high, low = halves(matrix)
    upper = np.concatenate([high, high], axis=1)
    return np.concatenate([upper, np.concatenate([low, np.zeros_like(low)], axis=1)], axis=0)


def section_tables():
    dm, _, jm, dj, sigma = node_tables()
    eye = np.eye(8)
    values = np.kron(jm, jm)
    slopes = np.concatenate([np.kron(dm, eye), np.kron(eye, dm)], axis=0)
    js, ds = sigma[:, None] * jm, sigma[:, None] * dj
    back_12 = np.concatenate([np.kron(ds, js).T, np.kron(js, ds).T], axis=1)
    back_3 = np.kron(js, js).T
    div = np.concatenate([np.kron(dm.T, eye), np.kron(eye, dm.T)], axis=1)
    tables = {"values": three(values), "slopes": three(slopes)}
    for part, rows in enumerate(PART_ROWS):
        tables["back_12", part] = stacked(back_12[rows])
        tables["back_3", part] = stacked(back_3[rows])
        tables["div", part] = three(div[rows])
        tables["values", part] = three(values[:, rows])
        tables["slopes", part] = three(slopes[:, rows])
    return {name: lane_tiles(table) for name, table in tables.items()}


EARLY = ["values", "slopes", ("back_12", 0), ("back_3", 0), ("div", 0)]
LATE = [("back_12", 1), ("back_3", 1), ("div", 1)]
LATE += [(kind, part) for part in range(2) for kind in ("values", "slopes")]


class Packed:
    def __init__(self, names):
        tables = section_tables()
        self.array = np.concatenate([tables[name].reshape(-1, LANES) for name in names])
        self.places, start = {}, 0
        for name in names:
            self.places[name] = (start, tables[name].shape)
            start += tables[name].shape[0] * tables[name].shape[1]

    def get(self, ref, name):
        start, (tiles, rows, _) = self.places[name]
        return [ref[start + k * rows : start + (k + 1) * rows] for k in range(tiles)]


def wall_bases():
    dm, rho, jm, dj, sigma = node_tables()
    lane = np.arange(LANES)
    gauss = np.arange(24)
    forward_lanes = [lane % 12, (lane + LANES) % 12]
    blocks = [dm.T[:, lane % 8]]
    blocks += [jm.T[:, lanes] for lanes in forward_lanes]
    blocks[2] = np.where(lane < 64, blocks[2], 0.0)
    blocks += [(sigma[:, None] * matrix)[gauss % 12][:, lane % 8] for matrix in (jm, dj)]
    blocks += [dm[:, lane % 8]]
    rows = [np.asarray(part, np.float32) for block in blocks for part in halves(block)]
    rows.append(np.asarray(rho[:, None] * rho[None, lane % 8], np.float32))
    return np.concatenate(rows), [float(weight) for weight in rho]


def build_wall_tables(bases, z_forward, z_back, w, rho):
    row = lax.broadcasted_iota(jnp.int32, (8, LANES), 0)
    lane = lax.broadcasted_iota(jnp.int32, (8, LANES), 1)
    zero = jnp.zeros((8, LANES), F32)
    nothing = jnp.zeros((LANES, LANES), BF16)
    for t in range(6):
        kind, low = t // 2, t % 2
        element = (lane // 8, lane // 12, (lane + LANES) // 12)[kind]
        base = bases[8 * t : 8 * t + 8]
        table = [jnp.where(element == a, base, zero) for a in range(16)]
        table = jnp.concatenate(table, axis=0).astype(BF16)
        z_forward[t, :LANES] = table
        z_forward[t, LANES:] = nothing if low else table
    for kind in range(2):
        for low in range(2):
            start = 48 + 24 * (2 * kind + low)
            table = []
            for block in range(24):
                inside = row + 8 * block - 12 * (lane // 8)
                base = bases[start + 8 * (block % 3) : start + 8 * (block % 3) + 8]
                table.append(jnp.where((inside >= 0) & (inside < 12), base, zero))
            table = jnp.concatenate(table + [zero] * 8, axis=0).astype(BF16)
            z_back[low, 512 * kind : 512 * kind + 256] = table
            z_back[low, 512 * kind + 256 : 512 * (kind + 1)] = (
                jnp.zeros((256, LANES), BF16) if low else table
            )
    for low in range(2):
        base = bases[144 + 8 * low : 152 + 8 * low]
        table = [jnp.where(lane // 8 == a, base, zero) for a in range(16)]
        table = jnp.concatenate(table, axis=0).astype(BF16)
        z_back[low, 1024:1152] = table
        z_back[low, 1152:] = nothing if low else table
    for x in range(8):
        w[8 * x : 8 * x + 8] = bases[160:168] * rho[x]


def split(values):
    high = values.astype(BF16)
    low = (values - high.astype(F32)).astype(BF16)
    return high, low


def dot(left, right):
    return jnp.dot(left, right, preferred_element_type=F32)


def wide(tiles, columns=None):
    count = len(tiles) if isinstance(tiles, list) else tiles.shape[0]
    whole = jnp.concatenate([tiles[k] for k in range(count)], axis=1)
    return whole if columns is None else whole[:, :columns]


def fold(values):
    return values[:, :LANES] + values[:, LANES : 2 * LANES]


def section_rows(block, e):
    return block.reshape(8, 2, 8, LANES)[:, e].reshape(XY, LANES)


def tiles_at(ref, tiles, rows=slice(None)):
    return jnp.concatenate([ref[k, rows] for k in tiles], axis=1)


def columns(values, count):
    return [values[:, k * LANES : (k + 1) * LANES] for k in range(count)]


def wall_stage(rows_of, z_forward, xhl, js, vs=None):
    count = js.shape[1] // 3
    skip = 2 if vs is None else 0
    outs = []
    for e in range(2):
        for c in range(3):
            rows = slice(c * count, (c + 1) * count)
            high, low = split(rows_of(c, e))
            xhl[e, 0, rows], xhl[e, 1, rows] = high, low
            if vs is not None:
                for k, part in enumerate((high, low, high)):
                    vs[2 * c + e, k * count : (k + 1) * count] = part
        outs.append(dot(wide(xhl.at[e]), wide(z_forward.at[skip:])))
    skip = (2 - skip) * LANES
    for c in range(3):
        rows = slice(c * count, (c + 1) * count)
        first = [fold(out[rows, skip : skip + 2 * LANES]) for out in outs]
        last = [fold(out[rows, skip + 2 * LANES :]) for out in outs]
        tiles = first + [last[0] + pltpu.roll(last[1], 64, 1)]
        for t, tile in enumerate(tiles):
            high, low = split(tile)
            for k, part in enumerate((high, low, high)):
                js[3 * c + t, k * count : (k + 1) * count] = part
    if vs is None:
        return None
    return {
        (c, e): fold(outs[e][c * count : (c + 1) * count, : 2 * LANES])
        for c in range(3)
        for e in range(2)
    }


def at_gauss(jj, js, pair):
    depth = js.shape[1]
    return columns(dot(wide(jj, depth), tiles_at(js, pair)), len(pair))


def section_slopes(grads, vs, c):
    return columns(dot(wide(grads, vs.shape[1]), tiles_at(vs, (2 * c, 2 * c + 1))), 2)


def fine_flow(jj, js, u_ref):
    for pair in PAIRS:
        for k, tile in zip(pair, at_gauss(jj, js, pair)):
            u_ref[k] = tile


def front(slopes, jj, grads, js, vs, u_ref, metric, kept, partial=None):
    ts, hs, h3s = kept

    def flux(c):
        for e, both in enumerate(section_slopes(grads, vs, c)):
            if partial is not None:
                both = both + partial[1][2 * c + e]
            g1, g2, g3 = both[:XY], both[XY:], slopes[c, e]
            m11, m22, m33, m12, m13, m23 = (metric[k, e] for k in range(6))
            h1 = m11 * g1 + m12 * g2 + m13 * g3
            h2 = m12 * g1 + m22 * g2 + m23 * g3
            h3 = m13 * g1 + m23 * g2 + m33 * g3
            h1h, h1l = split(h1)
            h2h, h2l = split(h2)
            for k, part in enumerate((h1h, h2h, h1l, h2l, h1h, h2h)):
                hs[2 * c + e, k * XY : (k + 1) * XY] = part
            h3s[2 * c + e] = h3

    def gauss(pair):
        for k, tile in zip(pair, at_gauss(jj, js, pair)):
            if partial is not None:
                tile = tile + partial[0][k]
            for d in range(3):
                start = (0, QQ, 4 * QQ)[d]
                gap = (2 * QQ, 2 * QQ, QQ)[d]
                high, low = split(u_ref[3 * d + k % 3] * tile)
                ts[k, start : start + QQ] = high
                ts[k, start + gap : start + gap + QQ] = low

    gauss(PAIRS[0])
    flux(0)
    gauss(PAIRS[1])
    flux(1)
    gauss(PAIRS[2])
    flux(2)
    gauss(PAIRS[3])
    gauss(PAIRS[4])


def back(part, tables, scratch, kept):
    z_back, back_12, back_3, div = tables
    ts, hs, h3s = kept
    bz = scratch["bz"]
    planes = PART_PLANES[part]
    count = 8 * len(planes)
    result = [[None, None] for _ in range(3)]
    sides = [{}, {}]
    for pair in PAIRS:
        for k, (table, depth, where) in enumerate(
            ((back_12, 4 * QQ, slice(0, 4 * QQ)), (back_3, 2 * QQ, slice(4 * QQ, None)))
        ):
            both = dot(wide(table, depth), tiles_at(ts, pair, where))
            both = both[:count] + both[count:]
            for tile, values in zip(pair, columns(both, len(pair))):
                sides[k][tile] = values
    for c in range(3):
        spread = columns(dot(wide(div), tiles_at(hs, (2 * c, 2 * c + 1))), 2)
        for e in range(2):
            result[c][e] = spread[e]
            rows = slice((2 * c + e) * count, (2 * c + e + 1) * count)
            for k in range(2):
                far = sides[k][3 * c + 2]
                far = far if e == 0 else pltpu.roll(far, 64, 1)
                for t, tile in enumerate((sides[k][3 * c + e], far)):
                    bz[4 * k + t, rows], bz[4 * k + t + 2, rows] = split(tile)
            bz[8, rows], bz[9, rows] = split(part_rows(part, h3s[2 * c + e]))
    out = fold(dot(wide(bz), wide(z_back)))
    for c in range(3):
        for e in range(2):
            result[c][e] += out[(2 * c + e) * count : (2 * c + e + 1) * count]
    return result


def part_rows(part, tall):
    return jnp.concatenate([tall[8 * x : 8 * x + 8] for x in PART_PLANES[part]], axis=0)


def sum_local(pair, out_ref, slot):
    shape = (out_ref.shape[1], 8, LANES)
    row = lax.broadcasted_iota(jnp.int32, shape, 1)
    lane = lax.broadcasted_iota(jnp.int32, shape, 2)
    inner = lane % 8
    for e in range(2):
        mine = pair[e].reshape(shape)
        other = pair[1 - e].reshape(shape)
        total = mine + jnp.where(row == 7, pltpu.roll(other, 7, 1), 0.0)
        total = total + jnp.where(row == 0, pltpu.roll(other, 1, 1), 0.0)
        after = pltpu.roll(total, LANES - 1, 2)
        before = pltpu.roll(total, 1, 2)
        total = (
            total
            + jnp.where((inner == 7) & (lane < LANES - 1), after, 0.0)
            + jnp.where((inner == 0) & (lane > 0), before, 0.0)
        )
        out_ref[slot, :, 8 * e : 8 * (e + 1), :] = total


def positions():
    c = lax.axis_index("col")
    return c % 2, c == 0, c == lax.axis_size("col") - 1


def places(ref):
    fields, planes = ref.shape[:2]
    return [
        (slot, x, e, (slot * planes + x) * 2 + e)
        for slot in range(fields)
        for x in range(planes)
        for e in range(2)
    ]


def pack_edges(sum_ref, edge_ref):
    lane = lax.broadcasted_iota(jnp.int32, (8, LANES), 1)
    packed = jnp.zeros((8, LANES), F32)
    for slot, x, e, at in places(sum_ref):
        tile = sum_ref[slot, x, 8 * e : 8 * (e + 1), :]
        packed = jnp.where(lane == 2 * at, pltpu.roll(tile, 2 * at, 1) if at else tile, packed)
        packed = jnp.where(lane == 2 * at + 1, pltpu.roll(tile, (2 * at + 2) % LANES, 1), packed)
    edge_ref[...] = packed


def with_edges(sum_ref, edge_refs):
    col_odd, _, _ = positions()
    lane = lax.broadcasted_iota(jnp.int32, (8, LANES), 1)
    edges = jnp.zeros((8, LANES), F32)
    for k, ref in enumerate(edge_refs):
        edges = edges + jnp.where(lane % 2 == (col_odd + k) % 2, ref[...], 0.0)
    meets = (lane == LANES - 1) | (lane == 0)
    return {
        (slot, x, e): sum_ref[slot, x, 8 * e : 8 * (e + 1), :]
        + jnp.where(meets, pltpu.roll(edges, LANES - 1 - 2 * at, 1), 0.0)
        for slot, x, e, at in places(sum_ref)
    }


def planes_kernel(count, *refs):
    outer, edge_refs, (up, down) = refs[0], refs[1 : 1 + count], refs[-2:]
    for (slot, x, e), tile in with_edges(outer, edge_refs).items():
        (up if x else down)[slot, 8 * e : 8 * (e + 1), :] = tile


def arrived(own_refs, up_ref, down_ref):
    up, down = own_refs
    return {
        (slot, x, e): (up if x else down)[slot, 8 * e : 8 * (e + 1), :]
        + (down_ref if x else up_ref)[slot, 8 * e : 8 * (e + 1), :]
        for slot, x, e, _ in places(jax.ShapeDtypeStruct((up.shape[0], 2, 16, LANES), F32))
    }


def interior_mask():
    _, first, last = positions()
    lane = lax.broadcasted_iota(jnp.int32, (1, LANES), 1)
    outer = ((lane == 0) & first) | ((lane == LANES - 1) & last)
    return jnp.where(outer, 0.0, 1.0)


def scale_metric(diag_ref, cross_ref, weights, metric):
    for k in range(6):
        ref = diag_ref if k < 3 else cross_ref
        block = ref[k % 3].astype(F32)
        for e in range(2):
            metric[k, e] = section_rows(block, e) * weights[...] * VISCOSITY


def finish(part, kept, tables, scratch, total, edge, mass=None):
    result = back(part, tables, scratch, kept)
    for c in range(3):
        sum_local(result[c], total, c)
    if mass is not None:
        jac, w = mass
        rows = [part_rows(part, section_rows(jac[...], e) * w[...]) for e in range(2)]
        sum_local(rows, total, 3)
    pack_edges(total, edge)


def back_tables(z_back, packed, ref, part):
    return [z_back] + [packed.get(ref, (kind, part)) for kind in ("back_12", "back_3", "div")]


def first_kernel(early_pack, rho, *refs):
    sources, refs = refs[:8], refs[8:]
    v, early, late, z_forward, z_back, jac, w, u, metric, *kept = refs[:12]
    total, edge, bases, b, gd, gc, sems = refs[12:19]
    bz, xhl, js, vs, flow_xhl, flow_js = refs[19:]
    targets = [bases, b, early, v, gd, gc, jac, late]
    copies = [
        pltpu.make_async_copy(source, target, sems.at[k])
        for k, (source, target) in enumerate(zip(sources, targets))
    ]
    for copy in copies:
        copy.start()
    copies[0].wait()
    build_wall_tables(bases, z_forward, z_back, w, rho)
    for copy in copies[1:7]:
        copy.wait()
    values, slopes = early_pack.get(early, "values"), early_pack.get(early, "slopes")
    wall_stage(lambda c, e: section_rows(b[c], e), z_forward, flow_xhl, flow_js)
    by_wall = wall_stage(lambda c, e: section_rows(v[c], e), z_forward, xhl, js, vs)
    fine_flow(values, flow_js, u)
    scale_metric(gd, gc, w, metric)
    front(by_wall, values, slopes, js, vs, u, metric, kept)
    tables = back_tables(z_back, early_pack, early, 0)
    finish(0, kept, tables, {"bz": bz}, total, edge, (jac, w))
    copies[7].wait()


def inner_kernel(has_mass, late_pack, *refs):
    kept, (z_back, late), refs = refs[:3], refs[3:5], refs[5:]
    mass, refs = (refs[:2], refs[2:]) if has_mass else (None, refs)
    total, edge, bz = refs
    tables = back_tables(z_back, late_pack, late, 1)
    finish(1, kept, tables, {"bz": bz}, total, edge, mass)


def half_step(part, tiles, v, inverse, half):
    mask = interior_mask()
    for k, x in enumerate(PART_PLANES[part]):
        for e in range(2):
            rows = slice(8 * e, 8 * (e + 1))
            inv = 1.0 / tiles[3, k, e]
            inverse[k, rows] = inv
            for c in range(3):
                step = (0.5 * STEP_SIZE) * inv * tiles[c, k, e]
                half[c, e, 8 * k : 8 * (k + 1)] = mask * (v[c, x, rows] - step)


def prepare_kernel(edges, late_pack, *refs):
    v, z_forward, late, summed = refs[:4]
    inverse, values, slopes, wall_slopes, half, xhl, js, vs = refs[4 + edges :]
    jj, grads = late_pack.get(late, ("values", 1)), late_pack.get(late, ("slopes", 1))
    half_step(1, with_edges(summed, refs[4 : 4 + edges]), v, inverse, half)
    by_wall = wall_stage(lambda c, e: half[c, e], z_forward, xhl, js, vs)
    for pair in PAIRS:
        for k, tile in zip(pair, at_gauss(jj, js, pair)):
            values[k] = tile
    for c in range(3):
        for e, both in enumerate(section_slopes(grads, vs, c)):
            slopes[2 * c + e] = both
            wall_slopes[2 * c + e] = by_wall[c, e]


def second_kernel(early_pack, late_pack, *refs):
    v, z_forward, z_back, early, late, u, metric = refs[:7]
    values, slopes, wall_slopes, up, down, up_in, down_in = refs[7:14]
    inverse, kept, (total, edge) = refs[14], refs[15:18], refs[18:20]
    bz, xhl, js, vs, half = refs[20:]
    jj, grads = late_pack.get(late, ("values", 0)), late_pack.get(late, ("slopes", 0))
    half_step(0, arrived((up, down), up_in, down_in), v, inverse, half)
    by_wall = wall_stage(lambda c, e: half[c, e], z_forward, xhl, js, vs)
    for (c, e), outer in by_wall.items():
        inner = wall_slopes[2 * c + e]
        by_wall[c, e] = jnp.concatenate([outer[:8], inner, outer[8:]], axis=0)
    front(by_wall, jj, grads, js, vs, u, metric, kept, (values, slopes))
    tables = back_tables(z_back, early_pack, early, 0)
    finish(0, kept, tables, {"bz": bz}, total, edge)


def advance(part, tiles, v, inverse, held):
    mask = interior_mask()
    planes = PART_PLANES[part]
    for c in range(3):
        for k, x in enumerate(planes):
            for e in range(2):
                rows = slice(8 * e, 8 * (e + 1))
                step = STEP_SIZE * inverse[k, rows] * tiles[c, k, e]
                held[c, k, rows] = mask * (v[c, x, rows] - step)


def advance_inner_kernel(edges, *refs):
    v, inverse, summed = refs[:3]
    advance(1, with_edges(summed, refs[3 : 3 + edges]), v, inverse, refs[-1])


def advance_kernel(*refs):
    v, inverse, inner, up, down, up_in, down_in, out, held, sems = refs
    copies = [pltpu.make_async_copy(inner, out.at[:, 1:7], sems.at[0])]
    copies[0].start()
    advance(0, arrived((up, down), up_in, down_in), v, inverse, held)
    for k, x in enumerate(PART_PLANES[0]):
        copies.append(pltpu.make_async_copy(held.at[:, k], out.at[:, x], sems.at[1 + k]))
        copies[-1].start()
    for copy in copies:
        copy.wait()


def back_scratch(part):
    return [pltpu.VMEM((10, 6 * 8 * len(PART_PLANES[part]), LANES), BF16)]


def front_scratch(count, with_field=True):
    shapes = [(2, 2, 3 * count, LANES), (9, 3 * count, LANES), (6, 3 * count, LANES)]
    return [pltpu.VMEM(shape, BF16) for shape in shapes[: 3 if with_field else 2]]


def call(kernel, name, ins, outs, scratch, in_space=pltpu.VMEM, out_space=pltpu.VMEM):
    ins = [pltpu.with_memory_space_constraint(array, in_space) for array in ins]
    return pl.pallas_call(
        kernel,
        name=name,
        out_shape=[out_space(shape, dtype) for shape, dtype in outs],
        in_specs=[pl.BlockSpec(memory_space=in_space)] * len(ins),
        out_specs=[pl.BlockSpec(memory_space=out_space)] * len(outs),
        scratch_shapes=scratch,
        compiler_params=pltpu.CompilerParams(vmem_limit_bytes=24 * 1024 * 1024),
    )(*ins)


def wall_pairings(count):
    even = [(i, i + 1) for i in range(0, count - 1, 2)]
    odd = [(i, i + 1) for i in range(1, count - 1, 2)]
    return [pairs + [(b, a) for a, b in pairs] for pairs in (even, odd) if pairs]


def swap_edges(edge):
    return [lax.ppermute(edge, "col", way) for way in wall_pairings(lax.axis_size("col"))]


def local(adjoint_field, base_flow, metric_diag, metric_cross, jacobian):
    early_pack, late_pack = Packed(EARLY), Packed(LATE)
    bases, rho = wall_bases()
    block = adjoint_field.shape[1:]
    field = ((3,) + block, F32)
    kept_shapes = [
        ((9, 6 * QQ, LANES), BF16),
        ((6, 6 * XY, LANES), BF16),
        ((6, XY, LANES), F32),
    ]
    edge_shape = ((8, LANES), F32)
    spans = lax.axis_size("span")
    ahead = [(i, (i + 1) % spans) for i in range(spans)]
    back_way = [(b, a) for a, b in ahead]

    def sums(fields, part):
        return [((fields, len(PART_PLANES[part])) + block[1:], F32), edge_shape]

    def exchange(fields, outer, outer_edge, operands):
        outer_edges = swap_edges(outer_edge)
        inner, inner_edge = call(
            functools.partial(inner_kernel, len(operands) > 5, late_pack),
            "inner_planes",
            operands,
            sums(fields, 1),
            back_scratch(1),
        )
        up, down = call(
            functools.partial(planes_kernel, len(outer_edges)),
            "planes",
            [outer] + outer_edges + [inner_edge],
            [((fields,) + block[1:], F32)] * 2,
            [],
        )
        inner_edges = swap_edges(inner_edge)
        up_in, down_in = lax.ppermute(up, "span", ahead), lax.ppermute(down, "span", back_way)
        return [up, down, up_in, down_in], inner, inner_edges

    early, late = (jnp.asarray(pack.array, BF16) for pack in (early_pack, late_pack))
    ins = [jnp.asarray(bases), base_flow, early, adjoint_field]
    ins += [metric_diag, metric_cross, jacobian, late]
    v, early, late, z_forward, z_back, jac, w, u, metric, *kept, outer, outer_edge = call(
        functools.partial(first_kernel, early_pack, rho),
        "first_operator",
        ins,
        [field, (early.shape, BF16), (late.shape, BF16)]
        + [((6, 2 * LANES, LANES), BF16), ((2, 1280, LANES), BF16)]
        + [(block, F32), ((XY, LANES), F32)]
        + [((9, QQ, LANES), F32), ((6, 2, XY, LANES), F32)]
        + kept_shapes
        + sums(4, 0),
        [
            pltpu.VMEM(bases.shape, F32),
            pltpu.VMEM((3,) + block, F32),
            pltpu.VMEM((3,) + block, BF16),
            pltpu.VMEM((3,) + block, BF16),
            pltpu.SemaphoreType.DMA((len(ins),)),
        ]
        + back_scratch(0)
        + front_scratch(XY)
        + front_scratch(XY, False),
        in_space=pltpu.HBM,
    )
    planes, inner, inner_edges = exchange(4, outer, outer_edge, kept + [z_back, late, jac, w])
    half = [pltpu.VMEM((3, 2, 8 * len(planes), LANES), F32) for planes in PART_PLANES]
    inner_inverse, *partial = call(
        functools.partial(prepare_kernel, len(inner_edges), late_pack),
        "prepare",
        [v, z_forward, late, inner] + inner_edges,
        [
            ((6,) + block[1:], F32),
            ((9, QQ, LANES), F32),
            ((6, 2 * XY, LANES), F32),
            ((6, 48, LANES), F32),
        ],
        [half[1]] + front_scratch(48),
    )
    inverse, *kept, outer, outer_edge = call(
        functools.partial(second_kernel, early_pack, late_pack),
        "second_operator",
        [v, z_forward, z_back, early, late, u, metric] + partial + planes,
        [((2,) + block[1:], F32)] + kept_shapes + sums(3, 0),
        back_scratch(0) + front_scratch(16) + [half[0]],
    )
    planes, inner, inner_edges = exchange(3, outer, outer_edge, kept + [z_back, late])
    (done,) = call(
        functools.partial(advance_inner_kernel, len(inner_edges)),
        "advance_inner",
        [v, inner_inverse, inner] + inner_edges,
        [((3, 6) + block[1:], F32)],
        [],
    )
    (out,) = call(
        advance_kernel,
        "advance",
        [v, inverse, done] + planes,
        [field],
        [pltpu.VMEM((3, 2) + block[1:], F32), pltpu.SemaphoreType.DMA((3,))],
        out_space=pltpu.HBM,
    )
    return out


def solution(mesh):
    in_specs = (
        P(None, "span", None, "col"),
        P(None, "span", None, "col"),
        P(None, "span", None, "col"),
        P(None, "span", None, "col"),
        P("span", None, "col"),
    )
    out_specs = P(None, "span", None, "col")
    return jax.shard_map(local, mesh=mesh, in_specs=in_specs, out_specs=out_specs, check_vma=False)
```

time: 25.7 us -> 25 us (0.973)
  waiting for transfers between devices: 3.45 us -> 2.66 us
    ppermute x2, waiting for transfers between devices: 1.39 us -> 0.57 us  [exchange(): lax.ppermute(up, 'span', ahead)]
    pallas_call x7 -> x9, Pallas kernels: 8.75 us -> 8.79 us  [call(): pl.pallas_call(kernel, name=name, out_shape=[out_space(shape, dtype) for...]
  transfers between devices with their start and end apart: 8 -> 8, of which waited for: 5 -> 4; matrix products, arithmetic and copies ran while one was open for 0% -> 0% of each run, Pallas kernels for 9% -> 12%
where the time goes in v4:
time: 25 us; the launch traced here: 24.8 us
  starting transfers between devices  13.3 us (53%)
  Pallas kernels  8.79 us (35%)
  waiting for transfers between devices  2.66 us (11%)
    ppermute x2, starting transfers between devices, exchange(): lax.ppermute(down, 'span', back_way)  9.5 us
    pallas_call x9, Pallas kernels, call(): pl.pallas_call(kernel, name=name, out_shape=[out_space(shape, dtype) for...  8.79 us
    ppermute x2, starting transfers between devices, exchange(): lax.ppermute(up, 'span', ahead)  2.85 us
    ppermute x4, waiting for transfers between devices, swap_edges(): lax.ppermute(edge, 'col', way)  2.09 us
    ppermute x4, starting transfers between devices, swap_edges(): lax.ppermute(edge, 'col', way)  0.96 us
    ppermute x2, waiting for transfers between devices, exchange(): lax.ppermute(up, 'span', ahead)  0.57 us
  transfers between devices with their start and end apart: 8, of which 4 were waited for; matrix products, arithmetic and copies ran while one was open for 0% of the time, Pallas kernels for 12%

profile of v4, /device:TPU:0, one launch (start us, length us, event | category | flops | bytes accessed | tf_op | source)
XLA Modules:
  0.0 24.8 jit_solution(15201074290347774434)
XLA Ops:
  0.0 3.3 %first_operator.1 = (f32[3,8,16,128]{3,2,1,0:T(8,128)S(1)}, bf16[848,128]{1,0:T(8,128)(2,1)S(1)}, bf16[1728,128]{1,0:T(8,128)(2,1)S(1)}, bf16[6,256,128]{2,1,0:T...) custom-call(f32[168,128]{1,0:T(8,128)} %constant.8.clone.refs_0_, ...), custom_call_target="tpu_custom_call" | custom-call | tf_op jit(solution)/shard_map/first_operator/pallas_call | solution.py:579
  3.3 0.5 %collective-permute-start.1 = (f32[8,128]{1,0:T(8,128)S(1)}, f32[8,128]{1,0:T(8,128)S(1)}, u32[]{:S(2)}, u32[]{:S(2)}) collective-permute-start(f32[8,128]{1,0:T(8,128)S(1)} %get-tuple-element.55), channel_id=1, source_target_pairs={{0,1},{1,0},{2,3},{3,2},{4,5},{5,4},{6,7},{7,6},{8,9},{9,8},{10,11... | collective-permute-start | bytes 12296 | tf_op jit(solution)/shard_map/ppermute | solution.py:597
  3.8 1.1 %inner_planes.2 = (f32[4,6,16,128]{3,2,1,0:T(8,128)S(1)}, f32[8,128]{1,0:T(8,128)S(1)}) custom-call(bf16[9,864,128]{2,1,0:T(8,128)(2,1)S(1)} %get-tuple-element.44.refs_0_, bf16[6,384,128]{2,1,0:T(8,128)(2,1)S(1)} %get-tuple-element.45.refs_1_, f32[6,64,128]{2,1,0:T(8,128)S(1)} %get-tuple-element.46.refs_2_, ...), custom_call_target="tpu_custom_call" | custom-call | tf_op jit(solution)/shard_map/inner_planes/pallas_call | solution.py:579
  4.9 0.0 collective-permute-done.1.refs_1_
  4.9 0.1 planes.2
  5.0 2.6 %collective-permute-start.2 = (f32[4,16,128]{2,1,0:T(8,128)S(1)}, f32[4,16,128]{2,1,0:T(8,128)S(1)}, u32[]{:S(2)}, u32[]{:S(2)}) collective-permute-start(f32[4,16,128]{2,1,0:T(8,128)S(1)} %get-tuple-element.56.refs_10_), channel_id=1, source_target_pairs={{0,2},{2,4},{4,6},{6,8},{8,10},{10,12},{12,14},{14,16},{16,18},{18... | collective-permute-start | bytes 98312 | tf_op jit(solution)/shard_map/ppermute | solution.py:635
  7.6 4.1 %collective-permute-start.3 = (f32[4,16,128]{2,1,0:T(8,128)S(1)}, f32[4,16,128]{2,1,0:T(8,128)S(1)}, u32[]{:S(2)}, u32[]{:S(2)}) collective-permute-start(f32[4,16,128]{2,1,0:T(8,128)S(1)} %get-tuple-element.57.refs_11_), channel_id=1, source_target_pairs={{2,0},{4,2},{6,4},{8,6},{10,8},{12,10},{14,12},{16,14},{18,16},{20... | collective-permute-start | bytes 98312 | tf_op jit(solution)/shard_map/ppermute | solution.py:635
  11.7 0.2 collective-permute-start
  11.9 1.0 %collective-permute-done.refs_4_ = f32[8,128]{1,0:T(8,128)S(1)} collective-permute-done((f32[8,128]{1,0:T(8,128)S(1)}, f32[8,128]{1,0:T(8,128)S(1)}, u32[]{:S(2)}, u32[]{:S(2)}) %collective-permute-start) | collective-permute-done | bytes 4128 | tf_op jit(solution)/shard_map/ppermute | solution.py:597
  12.8 0.7 %prepare.1 = (f32[6,16,128]{2,1,0:T(8,128)S(1)}, f32[9,144,128]{2,1,0:T(8,128)S(1)}, f32[6,128,128]{2,1,0:T(8,128)S(1)}, f32[6,48,128]{2,1,0:T(8,128)S(1)}) custom-call(f32[3,8,16,128]{3,2,1,0:T(8,128)S(1)} %get-tuple-element.37.refs_0_, bf16[6,256,128]{2,1,0:T(8,128)(2,1)S(1)} %get-tuple-element.38.refs_1_, ...), custom_call_target="tpu_custom_call" | custom-call | tf_op jit(solution)/shard_map/prepare/pallas_call | solution.py:579
  13.6 0.1 collective-permute-done.2.refs_12_
  13.6 0.0 collective-permute-done.3.refs_13_
  13.6 1.6 %second_operator.1 = (f32[2,16,128]{2,1,0:T(8,128)S(1)}, bf16[9,864,128]{2,1,0:T(8,128)(2,1)S(1)}, bf16[6,384,128]{2,1,0:T(8,128)(2,1)S(1)}, f32[6,64,128]{2,1,0...) custom-call(f32[3,8,16,128]{3,2,1,0:T(8,128)S(1)} %get-tuple-element.37.refs_0_, ...), custom_call_target="tpu_custom_call" | custom-call | tf_op jit(solution)/shard_map/second_operator/pallas_call | solution.py:579
  15.3 0.2 collective-permute-start.5
  15.5 1.1 %inner_planes.3 = (f32[3,6,16,128]{3,2,1,0:T(8,128)S(1)}, f32[8,128]{1,0:T(8,128)S(1)}) custom-call(bf16[9,864,128]{2,1,0:T(8,128)(2,1)S(1)} %get-tuple-element.60.refs_0_, bf16[6,384,128]{2,1,0:T(8,128)(2,1)S(1)} %get-tuple-element.61.refs_1_, f32[6,64,128]{2,1,0:T(8,128)S(1)} %get-tuple-element.62.refs_2_, ...), custom_call_target="tpu_custom_call" | custom-call | tf_op jit(solution)/shard_map/inner_planes/pallas_call | solution.py:579
  16.6 0.1 planes.3
  16.7 0.3 %collective-permute-start.6 = (f32[3,16,128]{2,1,0:T(8,128)S(1)}, f32[3,16,128]{2,1,0:T(8,128)S(1)}, u32[]{:S(2)}, u32[]{:S(2)}) collective-permute-start(f32[3,16,128]{2,1,0:T(8,128)S(1)} %get-tuple-element.67.refs_3_), channel_id=1, source_target_pairs={{0,2},{2,4},{4,6},{6,8},{8,10},{10,12},{12,14},{14,16},{16,18},{18... | collective-permute-start | bytes 73736 | tf_op jit(solution)/shard_map/ppermute | solution.py:635
  16.9 5.4 %collective-permute-start.7 = (f32[3,16,128]{2,1,0:T(8,128)S(1)}, f32[3,16,128]{2,1,0:T(8,128)S(1)}, u32[]{:S(2)}, u32[]{:S(2)}) collective-permute-start(f32[3,16,128]{2,1,0:T(8,128)S(1)} %get-tuple-element.68.refs_4_), channel_id=1, source_target_pairs={{2,0},{4,2},{6,4},{8,6},{10,8},{12,10},{14,12},{16,14},{18,16},{20... | collective-permute-start | bytes 73736 | tf_op jit(solution)/shard_map/ppermute | solution.py:635
  22.4 0.1 collective-permute-start.4
  22.4 1.1 %collective-permute-done.4.refs_3_ = f32[8,128]{1,0:T(8,128)S(1)} collective-permute-done((f32[8,128]{1,0:T(8,128)S(1)}, f32[8,128]{1,0:T(8,128)S(1)}, u32[]{:S(2)}, u32[]{:S(2)}) %collective-permute-start.4) | collective-permute-done | bytes 4128 | tf_op jit(solution)/shard_map/ppermute | solution.py:597
  23.5 0.1 advance_inner.1.refs_2_
  23.7 0.5 %collective-permute-done.6.refs_5_ = f32[3,16,128]{2,1,0:T(8,128)S(1)} collective-permute-done((f32[3,16,128]{2,1,0:T(8,128)S(1)}, f32[3,16,128]{2,1,0:T(8,128)S(1)}, u32[]{:S(2)}, u32[]{:S(2)}) %collective-permute-start.6) | collective-permute-done | bytes 24608 | tf_op jit(solution)/shard_map/ppermute | solution.py:635
  24.2 0.0 collective-permute-done.7.refs_6_
  24.2 0.7 %advance.1 = f32[3,8,16,128]{3,2,1,0:T(8,128)} custom-call(f32[3,8,16,128]{3,2,1,0:T(8,128)S(1)} %get-tuple-element.37.refs_0_, f32[2,16,128]{2,1,0:T(8,128)S(1)} %get-tuple-element.58.refs_1_, f32[3,6,16,128]{3,2,1,0:T(8,128)S(1)} %advance_inner.1.refs_2_, f32[3,16,128]{2,1,0:T(8,128)S(1)} %get-tuple-element.67.refs_3_, ...), custom_call_target="tpu_custom_call" | custom-call | tf_op jit(solution)/shard_map/advance/pallas_call | solution.py:579
  (1 shorter events, 0.0 us)
Async XLA Ops:
  3.3 1.6 %collective-permute-start.1 = (f32[8,128]{1,0:T(8,128)S(1)}, f32[8,128]{1,0:T(8,128)S(1)}, u32[]{:S(2)}, u32[]{:S(2)}) collective-permute-start(f32[8,128]{1,0:T(8,128)S(1)} %get-tuple-element.55), channel_id=1, source_target_pairs={{0,1},{1,0},{2,3},{3,2},{4,5},{5,4},{6,7},{7,6},{8,9},{9,8},{10,11... | collective-permute-start | bytes 12296 | tf_op jit(solution)/shard_map/ppermute | solution.py:597
  5.0 8.6 %collective-permute-start.2 = (f32[4,16,128]{2,1,0:T(8,128)S(1)}, f32[4,16,128]{2,1,0:T(8,128)S(1)}, u32[]{:S(2)}, u32[]{:S(2)}) collective-permute-start(f32[4,16,128]{2,1,0:T(8,128)S(1)} %get-tuple-element.56.refs_10_), channel_id=1, source_target_pairs={{0,2},{2,4},{4,6},{6,8},{8,10},{10,12},{12,14},{14,16},{16,18},{18... | collective-permute-start | bytes 98312 | tf_op jit(solution)/shard_map/ppermute | solution.py:635
  7.6 6.0 %collective-permute-start.3 = (f32[4,16,128]{2,1,0:T(8,128)S(1)}, f32[4,16,128]{2,1,0:T(8,128)S(1)}, u32[]{:S(2)}, u32[]{:S(2)}) collective-permute-start(f32[4,16,128]{2,1,0:T(8,128)S(1)} %get-tuple-element.57.refs_11_), channel_id=1, source_target_pairs={{2,0},{4,2},{6,4},{8,6},{10,8},{12,10},{14,12},{16,14},{18,16},{20... | collective-permute-start | bytes 98312 | tf_op jit(solution)/shard_map/ppermute | solution.py:635
  11.7 1.2 %collective-permute-start = (f32[8,128]{1,0:T(8,128)S(1)}, f32[8,128]{1,0:T(8,128)S(1)}, u32[]{:S(2)}, u32[]{:S(2)}) collective-permute-start(f32[8,128]{1,0:T(8,128)S(1)} %get-tuple-element.50.refs_2_), channel_id=1, source_target_pairs={{0,1},{1,0},{2,3},{3,2},{4,5},{5,4},{6,7},{7,6},{8,9},{9,8},{10,11... | collective-permute-start | bytes 12296 | tf_op jit(solution)/shard_map/ppermute | solution.py:597
  15.3 1.3 %collective-permute-start.5 = (f32[8,128]{1,0:T(8,128)S(1)}, f32[8,128]{1,0:T(8,128)S(1)}, u32[]{:S(2)}, u32[]{:S(2)}) collective-permute-start(f32[8,128]{1,0:T(8,128)S(1)} %get-tuple-element.66), channel_id=1, source_target_pairs={{0,1},{1,0},{2,3},{3,2},{4,5},{5,4},{6,7},{7,6},{8,9},{9,8},{10,11... | collective-permute-start | bytes 12296 | tf_op jit(solution)/shard_map/ppermute | solution.py:597
  16.7 7.5 %collective-permute-start.6 = (f32[3,16,128]{2,1,0:T(8,128)S(1)}, f32[3,16,128]{2,1,0:T(8,128)S(1)}, u32[]{:S(2)}, u32[]{:S(2)}) collective-permute-start(f32[3,16,128]{2,1,0:T(8,128)S(1)} %get-tuple-element.67.refs_3_), channel_id=1, source_target_pairs={{0,2},{2,4},{4,6},{6,8},{8,10},{10,12},{12,14},{14,16},{16,18},{18... | collective-permute-start | bytes 73736 | tf_op jit(solution)/shard_map/ppermute | solution.py:635
  16.9 7.2 %collective-permute-start.7 = (f32[3,16,128]{2,1,0:T(8,128)S(1)}, f32[3,16,128]{2,1,0:T(8,128)S(1)}, u32[]{:S(2)}, u32[]{:S(2)}) collective-permute-start(f32[3,16,128]{2,1,0:T(8,128)S(1)} %get-tuple-element.68.refs_4_), channel_id=1, source_target_pairs={{2,0},{4,2},{6,4},{8,6},{10,8},{12,10},{14,12},{16,14},{18,16},{20... | collective-permute-start | bytes 73736 | tf_op jit(solution)/shard_map/ppermute | solution.py:635
  22.4 1.2 %collective-permute-start.4 = (f32[8,128]{1,0:T(8,128)S(1)}, f32[8,128]{1,0:T(8,128)S(1)}, u32[]{:S(2)}, u32[]{:S(2)}) collective-permute-start(f32[8,128]{1,0:T(8,128)S(1)} %get-tuple-element.64.refs_2_), channel_id=1, source_target_pairs={{0,1},{1,0},{2,3},{3,2},{4,5},{5,4},{6,7},{7,6},{8,9},{9,8},{10,11... | collective-permute-start | bytes 12296 | tf_op jit(solution)/shard_map/ppermute | solution.py:597

commit v5 on v4

--- a/solution.py
+++ b/solution.py
@@ -53,6 +53,7 @@
 LANES = 128
 PART_PLANES = ([0, 7], [1, 2, 3, 4, 5, 6])
 PART_ROWS = [[8 * x + y for x in planes for y in range(8)] for planes in PART_PLANES]
+ROWS = PART_ROWS[0] + PART_ROWS[1]
 PAIRS = [(0, 1), (2, 3), (4, 5), (6, 7), (8,)]
 
 
@@ -99,6 +100,10 @@
     return padded.reshape(rows, -1, LANES).transpose(1, 0, 2)
 
 
+def part_rows(part, tall):
+    return tall[16:] if part else tall[:16]
+
+
 def three(matrix):
     high, low = halves(matrix)
     return np.concatenate([high, high, low], axis=1)
@@ -113,25 +118,23 @@
 def section_tables():
     dm, _, jm, dj, sigma = node_tables()
     eye = np.eye(8)
-    values = np.kron(jm, jm)
-    slopes = np.concatenate([np.kron(dm, eye), np.kron(eye, dm)], axis=0)
+    values = np.kron(jm, jm)[:, ROWS]
+    along = [np.kron(dm, eye)[ROWS][:, ROWS], np.kron(eye, dm)[ROWS][:, ROWS]]
+    slopes = np.concatenate(along, axis=0)
     js, ds = sigma[:, None] * jm, sigma[:, None] * dj
     back_12 = np.concatenate([np.kron(ds, js).T, np.kron(js, ds).T], axis=1)
     back_3 = np.kron(js, js).T
-    div = np.concatenate([np.kron(dm.T, eye), np.kron(eye, dm.T)], axis=1)
+    div = np.concatenate([matrix.T for matrix in along], axis=1)
     tables = {"values": three(values), "slopes": three(slopes)}
     for part, rows in enumerate(PART_ROWS):
         tables["back_12", part] = stacked(back_12[rows])
         tables["back_3", part] = stacked(back_3[rows])
-        tables["div", part] = three(div[rows])
-        tables["values", part] = three(values[:, rows])
-        tables["slopes", part] = three(slopes[:, rows])
+        tables["div", part] = three(part_rows(part, div))
     return {name: lane_tiles(table) for name, table in tables.items()}
 
 
 EARLY = ["values", "slopes", ("back_12", 0), ("back_3", 0), ("div", 0)]
 LATE = [("back_12", 1), ("back_3", 1), ("div", 1)]
-LATE += [(kind, part) for part in range(2) for kind in ("values", "slopes")]
 
 
 class Packed:
@@ -196,7 +199,7 @@
         z_back[low, 1024:1152] = table
         z_back[low, 1152:] = nothing if low else table
     for x in range(8):
-        w[8 * x : 8 * x + 8] = bases[160:168] * rho[x]
+        w[8 * x : 8 * x + 8] = bases[160:168] * rho[ROWS[8 * x] // 8]
 
 
 def split(values):
@@ -220,7 +223,9 @@
 
 
 def section_rows(block, e):
-    return block.reshape(8, 2, 8, LANES)[:, e].reshape(XY, LANES)
+    planes = block.reshape(8, 2, 8, LANES)[:, e]
+    planes = jnp.concatenate([planes[:1], planes[7:], planes[1:7]], axis=0)
+    return planes.reshape(XY, LANES)
 
 
 def tiles_at(ref, tiles, rows=slice(None)):
@@ -234,42 +239,52 @@
 def wall_stage(rows_of, z_forward, xhl, js, vs=None):
     count = js.shape[1] // 3
     skip = 2 if vs is None else 0
-    outs = []
-    for e in range(2):
-        for c in range(3):
-            rows = slice(c * count, (c + 1) * count)
+    batches = [[(c, e) for c in range(3)] for e in range(2)]
+    if count < 32:
+        batches = [batches[0] + batches[1]]
+    pieces = {}
+    for first, batch in enumerate(batches):
+        start = first * 3 * count
+        for k, (c, e) in enumerate(batch):
+            rows = slice(start + k * count, start + (k + 1) * count)
             high, low = split(rows_of(c, e))
-            xhl[e, 0, rows], xhl[e, 1, rows] = high, low
+            xhl[0, rows], xhl[1, rows] = high, low
             if vs is not None:
-                for k, part in enumerate((high, low, high)):
-                    vs[2 * c + e, k * count : (k + 1) * count] = part
-        outs.append(dot(wide(xhl.at[e]), wide(z_forward.at[skip:])))
-    skip = (2 - skip) * LANES
+                for t, part in enumerate((high, low, high)):
+                    vs[2 * c + e, t * count : (t + 1) * count] = part
+        out = dot(wide(xhl.at[:, start : start + len(batch) * count]), wide(z_forward.at[skip:]))
+        for k, (c, e) in enumerate(batch):
+            for kind in range(skip // 2, 3):
+                lanes = slice((2 * kind - skip) * LANES, (2 * kind - skip + 2) * LANES)
+                pieces[kind, c, e] = fold(out[k * count : (k + 1) * count, lanes])
     for c in range(3):
-        rows = slice(c * count, (c + 1) * count)
-        first = [fold(out[rows, skip : skip + 2 * LANES]) for out in outs]
-        last = [fold(out[rows, skip + 2 * LANES :]) for out in outs]
-        tiles = first + [last[0] + pltpu.roll(last[1], 64, 1)]
+        tiles = [pieces[1, c, 0], pieces[1, c, 1]]
+        tiles.append(pieces[2, c, 0] + pltpu.roll(pieces[2, c, 1], 64, 1))
         for t, tile in enumerate(tiles):
             high, low = split(tile)
             for k, part in enumerate((high, low, high)):
                 js[3 * c + t, k * count : (k + 1) * count] = part
-    if vs is None:
-        return None
-    return {
-        (c, e): fold(outs[e][c * count : (c + 1) * count, : 2 * LANES])
-        for c in range(3)
-        for e in range(2)
-    }
+    return {(c, e): pieces[0, c, e] for c in range(3) for e in range(2)} if vs is not None else None
+
+
+def right_side(refs, tiles):
+    whole = []
+    for k in tiles:
+        parts = []
+        for third in range(3):
+            for ref in refs:
+                count = ref.shape[1] // 3
+                parts.append(ref[k, third * count : (third + 1) * count])
+        whole.append(jnp.concatenate(parts, axis=0))
+    return jnp.concatenate(whole, axis=1)
 
 
 def at_gauss(jj, js, pair):
-    depth = js.shape[1]
-    return columns(dot(wide(jj, depth), tiles_at(js, pair)), len(pair))
+    return columns(dot(wide(jj, 3 * XY), right_side(js, pair)), len(pair))
 
 
 def section_slopes(grads, vs, c):
-    return columns(dot(wide(grads, vs.shape[1]), tiles_at(vs, (2 * c, 2 * c + 1))), 2)
+    return columns(dot(wide(grads, 3 * XY), right_side(vs, (2 * c, 2 * c + 1))), 2)
 
 
 def fine_flow(jj, js, u_ref):
@@ -278,13 +293,11 @@
             u_ref[k] = tile
 
 
-def front(slopes, jj, grads, js, vs, u_ref, metric, kept, partial=None):
+def front(slopes, jj, grads, js, vs, u_ref, metric, kept):
     ts, hs, h3s = kept
 
     def flux(c):
         for e, both in enumerate(section_slopes(grads, vs, c)):
-            if partial is not None:
-                both = both + partial[1][2 * c + e]
             g1, g2, g3 = both[:XY], both[XY:], slopes[c, e]
             m11, m22, m33, m12, m13, m23 = (metric[k, e] for k in range(6))
             h1 = m11 * g1 + m12 * g2 + m13 * g3
@@ -298,8 +311,6 @@
 
     def gauss(pair):
         for k, tile in zip(pair, at_gauss(jj, js, pair)):
-            if partial is not None:
-                tile = tile + partial[0][k]
             for d in range(3):
                 start = (0, QQ, 4 * QQ)[d]
                 gap = (2 * QQ, 2 * QQ, QQ)[d]
@@ -307,14 +318,13 @@
                 ts[k, start : start + QQ] = high
                 ts[k, start + gap : start + gap + QQ] = low
 
-    gauss(PAIRS[0])
-    flux(0)
-    gauss(PAIRS[1])
-    flux(1)
-    gauss(PAIRS[2])
-    flux(2)
-    gauss(PAIRS[3])
-    gauss(PAIRS[4])
+    if len(js) == 1:
+        work = [(gauss, pair) for pair in PAIRS] + [(flux, c) for c in range(3)]
+    else:
+        work = [step for c in range(3) for step in ((flux, c), (gauss, PAIRS[c]))]
+        work += [(gauss, pair) for pair in PAIRS[3:]]
+    for step, argument in work:
+        step(argument)
 
 
 def back(part, tables, scratch, kept):
@@ -351,10 +361,6 @@
     return result
 
 
-def part_rows(part, tall):
-    return jnp.concatenate([tall[8 * x : 8 * x + 8] for x in PART_PLANES[part]], axis=0)
-
-
 def sum_local(pair, out_ref, slot):
     shape = (out_ref.shape[1], 8, LANES)
     row = lax.broadcasted_iota(jnp.int32, shape, 1)
@@ -464,7 +470,7 @@
     v, early, late, z_forward, z_back, jac, w, u, metric, *kept = refs[:12]
     total, edge, bases, b, gd, gc, sems = refs[12:19]
     bz, xhl, js, vs, flow_xhl, flow_js = refs[19:]
-    targets = [bases, b, early, v, gd, gc, jac, late]
+    targets = [bases, b, v, early, gd, gc, jac, late]
     copies = [
         pltpu.make_async_copy(source, target, sems.at[k])
         for k, (source, target) in enumerate(zip(sources, targets))
@@ -473,14 +479,18 @@
         copy.start()
     copies[0].wait()
     build_wall_tables(bases, z_forward, z_back, w, rho)
-    for copy in copies[1:7]:
-        copy.wait()
-    values, slopes = early_pack.get(early, "values"), early_pack.get(early, "slopes")
+    copies[1].wait()
+    copies[2].wait()
     wall_stage(lambda c, e: section_rows(b[c], e), z_forward, flow_xhl, flow_js)
     by_wall = wall_stage(lambda c, e: section_rows(v[c], e), z_forward, xhl, js, vs)
-    fine_flow(values, flow_js, u)
+    copies[3].wait()
+    copies[4].wait()
+    copies[5].wait()
+    copies[6].wait()
+    values, slopes = early_pack.get(early, "values"), early_pack.get(early, "slopes")
+    fine_flow(values, [flow_js], u)
     scale_metric(gd, gc, w, metric)
-    front(by_wall, values, slopes, js, vs, u, metric, kept)
+    front(by_wall, values, slopes, [js], [vs], u, metric, kept)
     tables = back_tables(z_back, early_pack, early, 0)
     finish(0, kept, tables, {"bz": bz}, total, edge, (jac, w))
     copies[7].wait()
@@ -506,33 +516,26 @@
                 half[c, e, 8 * k : 8 * (k + 1)] = mask * (v[c, x, rows] - step)
 
 
-def prepare_kernel(edges, late_pack, *refs):
-    v, z_forward, late, summed = refs[:4]
-    inverse, values, slopes, wall_slopes, half, xhl, js, vs = refs[4 + edges :]
-    jj, grads = late_pack.get(late, ("values", 1)), late_pack.get(late, ("slopes", 1))
-    half_step(1, with_edges(summed, refs[4 : 4 + edges]), v, inverse, half)
+def prepare_kernel(edges, *refs):
+    v, z_forward, summed = refs[:3]
+    inverse, js, vs, wall_slopes, half, xhl = refs[3 + edges :]
+    half_step(1, with_edges(summed, refs[3 : 3 + edges]), v, inverse, half)
     by_wall = wall_stage(lambda c, e: half[c, e], z_forward, xhl, js, vs)
-    for pair in PAIRS:
-        for k, tile in zip(pair, at_gauss(jj, js, pair)):
-            values[k] = tile
-    for c in range(3):
-        for e, both in enumerate(section_slopes(grads, vs, c)):
-            slopes[2 * c + e] = both
-            wall_slopes[2 * c + e] = by_wall[c, e]
-
-
-def second_kernel(early_pack, late_pack, *refs):
-    v, z_forward, z_back, early, late, u, metric = refs[:7]
-    values, slopes, wall_slopes, up, down, up_in, down_in = refs[7:14]
-    inverse, kept, (total, edge) = refs[14], refs[15:18], refs[18:20]
-    bz, xhl, js, vs, half = refs[20:]
-    jj, grads = late_pack.get(late, ("values", 0)), late_pack.get(late, ("slopes", 0))
+    for (c, e), slope in by_wall.items():
+        wall_slopes[2 * c + e] = slope
+
+
+def second_kernel(early_pack, *refs):
+    v, z_forward, z_back, early, u, metric = refs[:6]
+    inner_js, inner_vs, wall_slopes, up, down, up_in, down_in = refs[6:13]
+    inverse, kept, (total, edge) = refs[13], refs[14:17], refs[17:19]
+    bz, xhl, js, vs, half = refs[19:]
+    values, slopes = early_pack.get(early, "values"), early_pack.get(early, "slopes")
     half_step(0, arrived((up, down), up_in, down_in), v, inverse, half)
     by_wall = wall_stage(lambda c, e: half[c, e], z_forward, xhl, js, vs)
-    for (c, e), outer in by_wall.items():
-        inner = wall_slopes[2 * c + e]
-        by_wall[c, e] = jnp.concatenate([outer[:8], inner, outer[8:]], axis=0)
-    front(by_wall, jj, grads, js, vs, u, metric, kept, (values, slopes))
+    for c, e in by_wall:
+        by_wall[c, e] = jnp.concatenate([by_wall[c, e], wall_slopes[2 * c + e]], axis=0)
+    front(by_wall, values, slopes, [js, inner_js], [vs, inner_vs], u, metric, kept)
     tables = back_tables(z_back, early_pack, early, 0)
     finish(0, kept, tables, {"bz": bz}, total, edge)
 
@@ -570,7 +573,7 @@
 
 
 def front_scratch(count, with_field=True):
-    shapes = [(2, 2, 3 * count, LANES), (9, 3 * count, LANES), (6, 3 * count, LANES)]
+    shapes = [(2, 6 * count, LANES), (9, 3 * count, LANES), (6, 3 * count, LANES)]
     return [pltpu.VMEM(shape, BF16) for shape in shapes[: 3 if with_field else 2]]
 
 
@@ -636,7 +639,7 @@
         return [up, down, up_in, down_in], inner, inner_edges
 
     early, late = (jnp.asarray(pack.array, BF16) for pack in (early_pack, late_pack))
-    ins = [jnp.asarray(bases), base_flow, early, adjoint_field]
+    ins = [jnp.asarray(bases), base_flow, adjoint_field, early]
     ins += [metric_diag, metric_cross, jacobian, late]
     v, early, late, z_forward, z_back, jac, w, u, metric, *kept, outer, outer_edge = call(
         functools.partial(first_kernel, early_pack, rho),
@@ -662,22 +665,22 @@
     )
     planes, inner, inner_edges = exchange(4, outer, outer_edge, kept + [z_back, late, jac, w])
     half = [pltpu.VMEM((3, 2, 8 * len(planes), LANES), F32) for planes in PART_PLANES]
-    inner_inverse, *partial = call(
-        functools.partial(prepare_kernel, len(inner_edges), late_pack),
+    inner_inverse, *prepared = call(
+        functools.partial(prepare_kernel, len(inner_edges)),
         "prepare",
-        [v, z_forward, late, inner] + inner_edges,
+        [v, z_forward, inner] + inner_edges,
         [
             ((6,) + block[1:], F32),
-            ((9, QQ, LANES), F32),
-            ((6, 2 * XY, LANES), F32),
+            ((9, 144, LANES), BF16),
+            ((6, 144, LANES), BF16),
             ((6, 48, LANES), F32),
         ],
-        [half[1]] + front_scratch(48),
+        [half[1], front_scratch(48)[0]],
     )
     inverse, *kept, outer, outer_edge = call(
-        functools.partial(second_kernel, early_pack, late_pack),
+        functools.partial(second_kernel, early_pack),
         "second_operator",
-        [v, z_forward, z_back, early, late, u, metric] + partial + planes,
+        [v, z_forward, z_back, early, u, metric] + prepared + planes,
         [((2,) + block[1:], F32)] + kept_shapes + sums(3, 0),
         back_scratch(0) + front_scratch(16) + [half[0]],
     )

time: 25 us -> 24.7 us (0.988)
  Pallas kernels: 8.79 us -> 8.37 us
    pallas_call x9, Pallas kernels: 8.79 us -> 8.37 us  [call(): pl.pallas_call(kernel, name=name, out_shape=[out_space(shape, dtype) for...]
    ppermute x2, waiting for transfers between devices: 0.57 us -> 0.88 us  [exchange(): lax.ppermute(up, 'span', ahead)]
  transfers between devices with their start and end apart: 8 -> 8, of which waited for: 4 -> 4; matrix products, arithmetic and copies ran while one was open for 0% -> 0% of each run, Pallas kernels for 12% -> 11%
where the time goes in v5:
time: 24.7 us; the launch traced here: 24.6 us
  starting transfers between devices  13.3 us (54%)
  Pallas kernels  8.37 us (34%)
  waiting for transfers between devices  2.9 us (12%)
    ppermute x2, starting transfers between devices, exchange(): lax.ppermute(down, 'span', back_way)  9.42 us
    pallas_call x9, Pallas kernels, call(): pl.pallas_call(kernel, name=name, out_shape=[out_space(shape, dtype) for...  8.37 us
    ppermute x2, starting transfers between devices, exchange(): lax.ppermute(up, 'span', ahead)  2.87 us
    ppermute x4, waiting for transfers between devices, swap_edges(): lax.ppermute(edge, 'col', way)  2.01 us
    ppermute x4, starting transfers between devices, swap_edges(): lax.ppermute(edge, 'col', way)  0.96 us
    ppermute x2, waiting for transfers between devices, exchange(): lax.ppermute(up, 'span', ahead)  0.88 us
  transfers between devices with their start and end apart: 8, of which 4 were waited for; matrix products, arithmetic and copies ran while one was open for 0% of the time, Pallas kernels for 11%

profile of v5, /device:TPU:0, one launch (start us, length us, event | category | flops | bytes accessed | tf_op | source)
XLA Modules:
  0.0 24.6 jit_solution(1507523065744976178)
XLA Ops:
  0.0 3.2 %first_operator.1 = (f32[3,8,16,128]{3,2,1,0:T(8,128)S(1)}, bf16[848,128]{1,0:T(8,128)(2,1)S(1)}, bf16[912,128]{1,0:T(8,128)(2,1)S(1)}, bf16[6,256,128]{2,1,0:T(...) custom-call(f32[168,128]{1,0:T(8,128)} %constant.8.clone.refs_0_, ...), custom_call_target="tpu_custom_call" | custom-call | tf_op jit(solution)/shard_map/first_operator/pallas_call | solution.py:582
  3.2 0.5 %collective-permute-start.1 = (f32[8,128]{1,0:T(8,128)S(1)}, f32[8,128]{1,0:T(8,128)S(1)}, u32[]{:S(2)}, u32[]{:S(2)}) collective-permute-start(f32[8,128]{1,0:T(8,128)S(1)} %get-tuple-element.55), channel_id=1, source_target_pairs={{0,1},{1,0},{2,3},{3,2},{4,5},{5,4},{6,7},{7,6},{8,9},{9,8},{10,11... | collective-permute-start | bytes 12296 | tf_op jit(solution)/shard_map/ppermute | solution.py:600
  3.7 1.1 %inner_planes.2 = (f32[4,6,16,128]{3,2,1,0:T(8,128)S(1)}, f32[8,128]{1,0:T(8,128)S(1)}) custom-call(bf16[9,864,128]{2,1,0:T(8,128)(2,1)S(1)} %get-tuple-element.43.refs_0_, bf16[6,384,128]{2,1,0:T(8,128)(2,1)S(1)} %get-tuple-element.44.refs_1_, f32[6,64,128]{2,1,0:T(8,128)S(1)} %get-tuple-element.45.refs_2_, ...), custom_call_target="tpu_custom_call" | custom-call | tf_op jit(solution)/shard_map/inner_planes/pallas_call | solution.py:582
  4.8 0.0 collective-permute-done.1.refs_1_
  4.9 0.1 planes.2
  5.0 2.6 %collective-permute-start.2 = (f32[4,16,128]{2,1,0:T(8,128)S(1)}, f32[4,16,128]{2,1,0:T(8,128)S(1)}, u32[]{:S(2)}, u32[]{:S(2)}) collective-permute-start(f32[4,16,128]{2,1,0:T(8,128)S(1)} %get-tuple-element.56.refs_9_), channel_id=1, source_target_pairs={{0,2},{2,4},{4,6},{6,8},{8,10},{10,12},{12,14},{14,16},{16,18},{18... | collective-permute-start | bytes 98312 | tf_op jit(solution)/shard_map/ppermute | solution.py:638
  7.5 4.1 %collective-permute-start.3 = (f32[4,16,128]{2,1,0:T(8,128)S(1)}, f32[4,16,128]{2,1,0:T(8,128)S(1)}, u32[]{:S(2)}, u32[]{:S(2)}) collective-permute-start(f32[4,16,128]{2,1,0:T(8,128)S(1)} %get-tuple-element.57.refs_10_), channel_id=1, source_target_pairs={{2,0},{4,2},{6,4},{8,6},{10,8},{12,10},{14,12},{16,14},{18,16},{20... | collective-permute-start | bytes 98312 | tf_op jit(solution)/shard_map/ppermute | solution.py:638
  11.6 0.2 collective-permute-start
  11.8 1.0 %collective-permute-done.refs_3_ = f32[8,128]{1,0:T(8,128)S(1)} collective-permute-done((f32[8,128]{1,0:T(8,128)S(1)}, f32[8,128]{1,0:T(8,128)S(1)}, u32[]{:S(2)}, u32[]{:S(2)}) %collective-permute-start) | collective-permute-done | bytes 4128 | tf_op jit(solution)/shard_map/ppermute | solution.py:600
  12.7 0.4 %prepare.1 = (f32[6,16,128]{2,1,0:T(8,128)S(1)}, bf16[9,144,128]{2,1,0:T(8,128)(2,1)S(1)}, bf16[6,144,128]{2,1,0:T(8,128)(2,1)S(1)}, f32[6,48,128]{2,1,0:T(8,128)S(1)}) custom-call(f32[3,8,16,128]{3,2,1,0:T(8,128)S(1)} %get-tuple-element.37.refs_0_, bf16[6,256,128]{2,1,0:T(8,128)(2,1)S(1)} %get-tuple-element.38.refs_1_, ...), custom_call_target="tpu_custom_call" | custom-call | tf_op jit(solution)/shard_map/prepare/pallas_call | solution.py:582
  13.2 0.4 %collective-permute-done.2.refs_11_ = f32[4,16,128]{2,1,0:T(8,128)S(1)} collective-permute-done((f32[4,16,128]{2,1,0:T(8,128)S(1)}, f32[4,16,128]{2,1,0:T(8,128)S(1)}, u32[]{:S(2)}, u32[]{:S(2)}) %collective-permute-start.2) | collective-permute-done | bytes 32800 | tf_op jit(solution)/shard_map/ppermute | solution.py:638
  13.6 1.5 %second_operator.1 = (f32[2,16,128]{2,1,0:T(8,128)S(1)}, bf16[9,864,128]{2,1,0:T(8,128)(2,1)S(1)}, bf16[6,384,128]{2,1,0:T(8,128)(2,1)S(1)}, f32[6,64,128]{2,1,0...) custom-call(f32[3,8,16,128]{3,2,1,0:T(8,128)S(1)} %get-tuple-element.37.refs_0_, ...), custom_call_target="tpu_custom_call" | custom-call | tf_op jit(solution)/shard_map/second_operator/pallas_call | solution.py:582
  15.1 0.1 collective-permute-start.5
  15.2 1.1 %inner_planes.3 = (f32[3,6,16,128]{3,2,1,0:T(8,128)S(1)}, f32[8,128]{1,0:T(8,128)S(1)}) custom-call(bf16[9,864,128]{2,1,0:T(8,128)(2,1)S(1)} %get-tuple-element.60.refs_0_, bf16[6,384,128]{2,1,0:T(8,128)(2,1)S(1)} %get-tuple-element.61.refs_1_, f32[6,64,128]{2,1,0:T(8,128)S(1)} %get-tuple-element.62.refs_2_, ...), custom_call_target="tpu_custom_call" | custom-call | tf_op jit(solution)/shard_map/inner_planes/pallas_call | solution.py:582
  16.3 0.0 collective-permute-done.5.refs_1_
  16.3 0.1 planes.3
  16.4 0.3 %collective-permute-start.6 = (f32[3,16,128]{2,1,0:T(8,128)S(1)}, f32[3,16,128]{2,1,0:T(8,128)S(1)}, u32[]{:S(2)}, u32[]{:S(2)}) collective-permute-start(f32[3,16,128]{2,1,0:T(8,128)S(1)} %get-tuple-element.67.refs_3_), channel_id=1, source_target_pairs={{0,2},{2,4},{4,6},{6,8},{8,10},{10,12},{12,14},{14,16},{16,18},{18... | collective-permute-start | bytes 73736 | tf_op jit(solution)/shard_map/ppermute | solution.py:638
  16.7 5.4 %collective-permute-start.7 = (f32[3,16,128]{2,1,0:T(8,128)S(1)}, f32[3,16,128]{2,1,0:T(8,128)S(1)}, u32[]{:S(2)}, u32[]{:S(2)}) collective-permute-start(f32[3,16,128]{2,1,0:T(8,128)S(1)} %get-tuple-element.68.refs_4_), channel_id=1, source_target_pairs={{2,0},{4,2},{6,4},{8,6},{10,8},{12,10},{14,12},{16,14},{18,16},{20... | collective-permute-start | bytes 73736 | tf_op jit(solution)/shard_map/ppermute | solution.py:638
  22.1 0.2 collective-permute-start.4
  22.3 1.0 %collective-permute-done.4.refs_3_ = f32[8,128]{1,0:T(8,128)S(1)} collective-permute-done((f32[8,128]{1,0:T(8,128)S(1)}, f32[8,128]{1,0:T(8,128)S(1)}, u32[]{:S(2)}, u32[]{:S(2)}) %collective-permute-start.4) | collective-permute-done | bytes 4128 | tf_op jit(solution)/shard_map/ppermute | solution.py:600
  23.3 0.1 advance_inner.1.refs_2_
  23.4 0.5 %collective-permute-done.6.refs_5_ = f32[3,16,128]{2,1,0:T(8,128)S(1)} collective-permute-done((f32[3,16,128]{2,1,0:T(8,128)S(1)}, f32[3,16,128]{2,1,0:T(8,128)S(1)}, u32[]{:S(2)}, u32[]{:S(2)}) %collective-permute-start.6) | collective-permute-done | bytes 24608 | tf_op jit(solution)/shard_map/ppermute | solution.py:638
  23.9 0.0 collective-permute-done.7.refs_6_
  23.9 0.7 %advance.1 = f32[3,8,16,128]{3,2,1,0:T(8,128)} custom-call(f32[3,8,16,128]{3,2,1,0:T(8,128)S(1)} %get-tuple-element.37.refs_0_, f32[2,16,128]{2,1,0:T(8,128)S(1)} %get-tuple-element.58.refs_1_, f32[3,6,16,128]{3,2,1,0:T(8,128)S(1)} %advance_inner.1.refs_2_, f32[3,16,128]{2,1,0:T(8,128)S(1)} %get-tuple-element.67.refs_3_, ...), custom_call_target="tpu_custom_call" | custom-call | tf_op jit(solution)/shard_map/advance/pallas_call | solution.py:582
  (1 shorter events, 0.0 us)
Async XLA Ops:
  3.2 1.6 %collective-permute-start.1 = (f32[8,128]{1,0:T(8,128)S(1)}, f32[8,128]{1,0:T(8,128)S(1)}, u32[]{:S(2)}, u32[]{:S(2)}) collective-permute-start(f32[8,128]{1,0:T(8,128)S(1)} %get-tuple-element.55), channel_id=1, source_target_pairs={{0,1},{1,0},{2,3},{3,2},{4,5},{5,4},{6,7},{7,6},{8,9},{9,8},{10,11... | collective-permute-start | bytes 12296 | tf_op jit(solution)/shard_map/ppermute | solution.py:600
  5.0 8.6 %collective-permute-start.2 = (f32[4,16,128]{2,1,0:T(8,128)S(1)}, f32[4,16,128]{2,1,0:T(8,128)S(1)}, u32[]{:S(2)}, u32[]{:S(2)}) collective-permute-start(f32[4,16,128]{2,1,0:T(8,128)S(1)} %get-tuple-element.56.refs_9_), channel_id=1, source_target_pairs={{0,2},{2,4},{4,6},{6,8},{8,10},{10,12},{12,14},{14,16},{16,18},{18... | collective-permute-start | bytes 98312 | tf_op jit(solution)/shard_map/ppermute | solution.py:638
  7.5 6.0 %collective-permute-start.3 = (f32[4,16,128]{2,1,0:T(8,128)S(1)}, f32[4,16,128]{2,1,0:T(8,128)S(1)}, u32[]{:S(2)}, u32[]{:S(2)}) collective-permute-start(f32[4,16,128]{2,1,0:T(8,128)S(1)} %get-tuple-element.57.refs_10_), channel_id=1, source_target_pairs={{2,0},{4,2},{6,4},{8,6},{10,8},{12,10},{14,12},{16,14},{18,16},{20... | collective-permute-start | bytes 98312 | tf_op jit(solution)/shard_map/ppermute | solution.py:638
  11.6 1.2 %collective-permute-start = (f32[8,128]{1,0:T(8,128)S(1)}, f32[8,128]{1,0:T(8,128)S(1)}, u32[]{:S(2)}, u32[]{:S(2)}) collective-permute-start(f32[8,128]{1,0:T(8,128)S(1)} %get-tuple-element.50.refs_2_), channel_id=1, source_target_pairs={{0,1},{1,0},{2,3},{3,2},{4,5},{5,4},{6,7},{7,6},{8,9},{9,8},{10,11... | collective-permute-start | bytes 12296 | tf_op jit(solution)/shard_map/ppermute | solution.py:600
  15.1 1.2 %collective-permute-start.5 = (f32[8,128]{1,0:T(8,128)S(1)}, f32[8,128]{1,0:T(8,128)S(1)}, u32[]{:S(2)}, u32[]{:S(2)}) collective-permute-start(f32[8,128]{1,0:T(8,128)S(1)} %get-tuple-element.66), channel_id=1, source_target_pairs={{0,1},{1,0},{2,3},{3,2},{4,5},{5,4},{6,7},{7,6},{8,9},{9,8},{10,11... | collective-permute-start | bytes 12296 | tf_op jit(solution)/shard_map/ppermute | solution.py:600
  16.4 7.5 %collective-permute-start.6 = (f32[3,16,128]{2,1,0:T(8,128)S(1)}, f32[3,16,128]{2,1,0:T(8,128)S(1)}, u32[]{:S(2)}, u32[]{:S(2)}) collective-permute-start(f32[3,16,128]{2,1,0:T(8,128)S(1)} %get-tuple-element.67.refs_3_), channel_id=1, source_target_pairs={{0,2},{2,4},{4,6},{6,8},{8,10},{10,12},{12,14},{14,16},{16,18},{18... | collective-permute-start | bytes 73736 | tf_op jit(solution)/shard_map/ppermute | solution.py:638
  16.7 7.2 %collective-permute-start.7 = (f32[3,16,128]{2,1,0:T(8,128)S(1)}, f32[3,16,128]{2,1,0:T(8,128)S(1)}, u32[]{:S(2)}, u32[]{:S(2)}) collective-permute-start(f32[3,16,128]{2,1,0:T(8,128)S(1)} %get-tuple-element.68.refs_4_), channel_id=1, source_target_pairs={{2,0},{4,2},{6,4},{8,6},{10,8},{12,10},{14,12},{16,14},{18,16},{20... | collective-permute-start | bytes 73736 | tf_op jit(solution)/shard_map/ppermute | solution.py:638
  22.1 1.2 %collective-permute-start.4 = (f32[8,128]{1,0:T(8,128)S(1)}, f32[8,128]{1,0:T(8,128)S(1)}, u32[]{:S(2)}, u32[]{:S(2)}) collective-permute-start(f32[8,128]{1,0:T(8,128)S(1)} %get-tuple-element.64.refs_2_), channel_id=1, source_target_pairs={{0,1},{1,0},{2,3},{3,2},{4,5},{5,4},{6,7},{7,6},{8,9},{9,8},{10,11... | collective-permute-start | bytes 12296 | tf_op jit(solution)/shard_map/ppermute | solution.py:600

commit v6 on v5

--- a/solution.py
+++ b/solution.py
@@ -129,7 +129,7 @@
     for part, rows in enumerate(PART_ROWS):
         tables["back_12", part] = stacked(back_12[rows])
         tables["back_3", part] = stacked(back_3[rows])
-        tables["div", part] = three(part_rows(part, div))
+        tables["div", part] = stacked(part_rows(part, div))
     return {name: lane_tiles(table) for name, table in tables.items()}
 
 
@@ -187,17 +187,13 @@
                 inside = row + 8 * block - 12 * (lane // 8)
                 base = bases[start + 8 * (block % 3) : start + 8 * (block % 3) + 8]
                 table.append(jnp.where((inside >= 0) & (inside < 12), base, zero))
-            table = jnp.concatenate(table + [zero] * 8, axis=0).astype(BF16)
-            z_back[low, 512 * kind : 512 * kind + 256] = table
-            z_back[low, 512 * kind + 256 : 512 * (kind + 1)] = (
-                jnp.zeros((256, LANES), BF16) if low else table
-            )
+            table = jnp.concatenate(table, axis=0).astype(BF16)
+            z_back[low, LANES * kind : LANES * (kind + 1)] = table[:LANES]
+            z_back[low, 256 + 64 * kind : 320 + 64 * kind] = table[LANES:]
     for low in range(2):
         base = bases[144 + 8 * low : 152 + 8 * low]
         table = [jnp.where(lane // 8 == a, base, zero) for a in range(16)]
-        table = jnp.concatenate(table, axis=0).astype(BF16)
-        z_back[low, 1024:1152] = table
-        z_back[low, 1152:] = nothing if low else table
+        z_back[low, 384:] = jnp.concatenate(table, axis=0).astype(BF16)
     for x in range(8):
         w[8 * x : 8 * x + 8] = bases[160:168] * rho[ROWS[8 * x] // 8]
 
@@ -305,7 +301,7 @@
             h3 = m13 * g1 + m23 * g2 + m33 * g3
             h1h, h1l = split(h1)
             h2h, h2l = split(h2)
-            for k, part in enumerate((h1h, h2h, h1l, h2l, h1h, h2h)):
+            for k, part in enumerate((h1h, h2h, h1l, h2l)):
                 hs[2 * c + e, k * XY : (k + 1) * XY] = part
             h3s[2 * c + e] = h3
 
@@ -321,7 +317,7 @@
     if len(js) == 1:
         work = [(gauss, pair) for pair in PAIRS] + [(flux, c) for c in range(3)]
     else:
-        work = [step for c in range(3) for step in ((flux, c), (gauss, PAIRS[c]))]
+        work = [step for c in range(3) for step in ((gauss, PAIRS[c]), (flux, c))]
         work += [(gauss, pair) for pair in PAIRS[3:]]
     for step, argument in work:
         step(argument)
@@ -343,18 +339,25 @@
             both = both[:count] + both[count:]
             for tile, values in zip(pair, columns(both, len(pair))):
                 sides[k][tile] = values
+    spreads = dot(wide(div), tiles_at(hs, range(6)))
+    spreads = columns(spreads[:count] + spreads[count:], 6)
+    low_lanes = lax.broadcasted_iota(jnp.int32, (count, LANES), 1) < 64
     for c in range(3):
-        spread = columns(dot(wide(div), tiles_at(hs, (2 * c, 2 * c + 1))), 2)
+        spread = spreads[2 * c : 2 * c + 2]
+        far = [sides[k][3 * c + 2] for k in range(2)]
+        turned = [pltpu.roll(tile, 64, 1) for tile in far]
+        far = [
+            jnp.where(low_lanes, far[0], turned[1]),
+            jnp.where(low_lanes, turned[0], far[1]),
+        ]
         for e in range(2):
             result[c][e] = spread[e]
             rows = slice((2 * c + e) * count, (2 * c + e + 1) * count)
-            for k in range(2):
-                far = sides[k][3 * c + 2]
-                far = far if e == 0 else pltpu.roll(far, 64, 1)
-                for t, tile in enumerate((sides[k][3 * c + e], far)):
-                    bz[4 * k + t, rows], bz[4 * k + t + 2, rows] = split(tile)
-            bz[8, rows], bz[9, rows] = split(part_rows(part, h3s[2 * c + e]))
-    out = fold(dot(wide(bz), wide(z_back)))
+            near = [sides[k][3 * c + e] for k in range(2)]
+            tiles = near + [far[e], part_rows(part, h3s[2 * c + e])]
+            for t, tile in enumerate(tiles):
+                bz[t, rows], bz[4 + t, rows] = split(tile)
+    out = fold(dot(wide(bz.at[:4]), wide(z_back))) + dot(wide(bz.at[4:]), z_back[0])
     for c in range(3):
         for e in range(2):
             result[c][e] += out[(2 * c + e) * count : (2 * c + e + 1) * count]
@@ -569,7 +572,7 @@
 
 
 def back_scratch(part):
-    return [pltpu.VMEM((10, 6 * 8 * len(PART_PLANES[part]), LANES), BF16)]
+    return [pltpu.VMEM((8, 6 * 8 * len(PART_PLANES[part]), LANES), BF16)]
 
 
 def front_scratch(count, with_field=True):
@@ -607,7 +610,7 @@
     field = ((3,) + block, F32)
     kept_shapes = [
         ((9, 6 * QQ, LANES), BF16),
-        ((6, 6 * XY, LANES), BF16),
+        ((6, 4 * XY, LANES), BF16),
         ((6, XY, LANES), F32),
     ]
     edge_shape = ((8, LANES), F32)
@@ -646,7 +649,7 @@
         "first_operator",
         ins,
         [field, (early.shape, BF16), (late.shape, BF16)]
-        + [((6, 2 * LANES, LANES), BF16), ((2, 1280, LANES), BF16)]
+        + [((6, 2 * LANES, LANES), BF16), ((2, 512, LANES), BF16)]
         + [(block, F32), ((XY, LANES), F32)]
         + [((9, QQ, LANES), F32), ((6, 2, XY, LANES), F32)]
         + kept_shapes

time: 24.7 us -> 24.2 us (0.980)
  Pallas kernels: 8.37 us -> 7.74 us
    pallas_call x9, Pallas kernels: 8.37 us -> 7.74 us  [call(): pl.pallas_call(kernel, name=name, out_shape=[out_space(shape, dtype) for...]
    ppermute x4, waiting for transfers between devices: 2.01 us -> 2.38 us  [swap_edges(): lax.ppermute(edge, 'col', way)]
    ppermute x2, starting transfers between devices: 2.87 us -> 3.15 us  [exchange(): lax.ppermute(up, 'span', ahead)]
    ppermute x4, starting transfers between devices: 0.96 us -> 0.7 us  [swap_edges(): lax.ppermute(edge, 'col', way)]
  transfers between devices with their start and end apart: 8 -> 8, of which waited for: 4 -> 5; matrix products, arithmetic and copies ran while one was open for 0% -> 0% of each run, Pallas kernels for 11% -> 10%
where the time goes in v6:
time: 24.2 us; the launch traced here: 24.1 us
  starting transfers between devices  13.2 us (55%)
  Pallas kernels  7.74 us (32%)
  waiting for transfers between devices  3.07 us (13%)
    ppermute x2, starting transfers between devices, exchange(): lax.ppermute(down, 'span', back_way)  9.37 us
    pallas_call x9, Pallas kernels, call(): pl.pallas_call(kernel, name=name, out_shape=[out_space(shape, dtype) for...  7.74 us
    ppermute x2, starting transfers between devices, exchange(): lax.ppermute(up, 'span', ahead)  3.15 us
    ppermute x4, waiting for transfers between devices, swap_edges(): lax.ppermute(edge, 'col', way)  2.38 us
    ppermute x4, starting transfers between devices, swap_edges(): lax.ppermute(edge, 'col', way)  0.7 us
    ppermute x2, waiting for transfers between devices, exchange(): lax.ppermute(up, 'span', ahead)  0.69 us
  transfers between devices with their start and end apart: 8, of which 5 were waited for; matrix products, arithmetic and copies ran while one was open for 0% of the time, Pallas kernels for 10%

profile of v6, /device:TPU:0, one launch (start us, length us, event | category | flops | bytes accessed | tf_op | source)
XLA Modules:
  0.0 24.1 jit_solution(4124155546462095411)
XLA Ops:
  0.0 3.0 %first_operator.1 = (f32[3,8,16,128]{3,2,1,0:T(8,128)S(1)}, bf16[864,128]{1,0:T(8,128)(2,1)S(1)}, bf16[960,128]{1,0:T(8,128)(2,1)S(1)}, bf16[6,256,128]{2,1,0:T(...) custom-call(f32[168,128]{1,0:T(8,128)} %constant.8.clone.refs_0_, ...), custom_call_target="tpu_custom_call" | custom-call | tf_op jit(solution)/shard_map/first_operator/pallas_call | solution.py:585
  3.0 0.5 %collective-permute-start.1 = (f32[8,128]{1,0:T(8,128)S(1)}, f32[8,128]{1,0:T(8,128)S(1)}, u32[]{:S(2)}, u32[]{:S(2)}) collective-permute-start(f32[8,128]{1,0:T(8,128)S(1)} %get-tuple-element.55), channel_id=1, source_target_pairs={{0,1},{1,0},{2,3},{3,2},{4,5},{5,4},{6,7},{7,6},{8,9},{9,8},{10,11... | collective-permute-start | bytes 12296 | tf_op jit(solution)/shard_map/ppermute | solution.py:603
  3.5 1.0 %inner_planes.2 = (f32[4,6,16,128]{3,2,1,0:T(8,128)S(1)}, f32[8,128]{1,0:T(8,128)S(1)}) custom-call(bf16[9,864,128]{2,1,0:T(8,128)(2,1)S(1)} %get-tuple-element.43.refs_0_, bf16[6,256,128]{2,1,0:T(8,128)(2,1)S(1)} %get-tuple-element.44.refs_1_, f32[6,64,128]{2,1,0:T(8,128)S(1)} %get-tuple-element.45.refs_2_, ...), custom_call_target="tpu_custom_call" | custom-call | tf_op jit(solution)/shard_map/inner_planes/pallas_call | solution.py:585
  4.5 0.0 collective-permute-done.1.refs_1_
  4.5 0.1 planes.2
  4.6 2.7 %collective-permute-start.2 = (f32[4,16,128]{2,1,0:T(8,128)S(1)}, f32[4,16,128]{2,1,0:T(8,128)S(1)}, u32[]{:S(2)}, u32[]{:S(2)}) collective-permute-start(f32[4,16,128]{2,1,0:T(8,128)S(1)} %get-tuple-element.56.refs_9_), channel_id=1, source_target_pairs={{0,2},{2,4},{4,6},{6,8},{8,10},{10,12},{12,14},{14,16},{16,18},{18... | collective-permute-start | bytes 98312 | tf_op jit(solution)/shard_map/ppermute | solution.py:641
  7.3 4.0 %collective-permute-start.3 = (f32[4,16,128]{2,1,0:T(8,128)S(1)}, f32[4,16,128]{2,1,0:T(8,128)S(1)}, u32[]{:S(2)}, u32[]{:S(2)}) collective-permute-start(f32[4,16,128]{2,1,0:T(8,128)S(1)} %get-tuple-element.57.refs_10_), channel_id=1, source_target_pairs={{2,0},{4,2},{6,4},{8,6},{10,8},{12,10},{14,12},{16,14},{18,16},{20... | collective-permute-start | bytes 98312 | tf_op jit(solution)/shard_map/ppermute | solution.py:641
  11.4 0.1 collective-permute-start
  11.4 1.1 %collective-permute-done.refs_3_ = f32[8,128]{1,0:T(8,128)S(1)} collective-permute-done((f32[8,128]{1,0:T(8,128)S(1)}, f32[8,128]{1,0:T(8,128)S(1)}, u32[]{:S(2)}, u32[]{:S(2)}) %collective-permute-start) | collective-permute-done | bytes 4128 | tf_op jit(solution)/shard_map/ppermute | solution.py:603
  12.5 0.4 %prepare.1 = (f32[6,16,128]{2,1,0:T(8,128)S(1)}, bf16[9,144,128]{2,1,0:T(8,128)(2,1)S(1)}, bf16[6,144,128]{2,1,0:T(8,128)(2,1)S(1)}, f32[6,48,128]{2,1,0:T(8,128)S(1)}) custom-call(f32[3,8,16,128]{3,2,1,0:T(8,128)S(1)} %get-tuple-element.37.refs_0_, bf16[6,256,128]{2,1,0:T(8,128)(2,1)S(1)} %get-tuple-element.38.refs_1_, ...), custom_call_target="tpu_custom_call" | custom-call | tf_op jit(solution)/shard_map/prepare/pallas_call | solution.py:585
  13.0 0.2 collective-permute-done.2.refs_11_
  13.2 0.0 collective-permute-done.3.refs_12_
  13.2 1.4 %second_operator.1 = (f32[2,16,128]{2,1,0:T(8,128)S(1)}, bf16[9,864,128]{2,1,0:T(8,128)(2,1)S(1)}, bf16[6,256,128]{2,1,0:T(8,128)(2,1)S(1)}, f32[6,64,128]{2,1,0...) custom-call(f32[3,8,16,128]{3,2,1,0:T(8,128)S(1)} %get-tuple-element.37.refs_0_, ...), custom_call_target="tpu_custom_call" | custom-call | tf_op jit(solution)/shard_map/second_operator/pallas_call | solution.py:585
  14.6 0.0 collective-permute-start.5
  14.6 1.0 %inner_planes.3 = (f32[3,6,16,128]{3,2,1,0:T(8,128)S(1)}, f32[8,128]{1,0:T(8,128)S(1)}) custom-call(bf16[9,864,128]{2,1,0:T(8,128)(2,1)S(1)} %get-tuple-element.60.refs_0_, bf16[6,256,128]{2,1,0:T(8,128)(2,1)S(1)} %get-tuple-element.61.refs_1_, f32[6,64,128]{2,1,0:T(8,128)S(1)} %get-tuple-element.62.refs_2_, ...), custom_call_target="tpu_custom_call" | custom-call | tf_op jit(solution)/shard_map/inner_planes/pallas_call | solution.py:585
  15.6 0.2 collective-permute-done.5.refs_1_
  15.8 0.1 planes.3
  15.9 0.5 %collective-permute-start.6 = (f32[3,16,128]{2,1,0:T(8,128)S(1)}, f32[3,16,128]{2,1,0:T(8,128)S(1)}, u32[]{:S(2)}, u32[]{:S(2)}) collective-permute-start(f32[3,16,128]{2,1,0:T(8,128)S(1)} %get-tuple-element.67.refs_3_), channel_id=1, source_target_pairs={{0,2},{2,4},{4,6},{6,8},{8,10},{10,12},{12,14},{14,16},{16,18},{18... | collective-permute-start | bytes 73736 | tf_op jit(solution)/shard_map/ppermute | solution.py:641
  16.3 5.3 %collective-permute-start.7 = (f32[3,16,128]{2,1,0:T(8,128)S(1)}, f32[3,16,128]{2,1,0:T(8,128)S(1)}, u32[]{:S(2)}, u32[]{:S(2)}) collective-permute-start(f32[3,16,128]{2,1,0:T(8,128)S(1)} %get-tuple-element.68.refs_4_), channel_id=1, source_target_pairs={{2,0},{4,2},{6,4},{8,6},{10,8},{12,10},{14,12},{16,14},{18,16},{20... | collective-permute-start | bytes 73736 | tf_op jit(solution)/shard_map/ppermute | solution.py:641
  21.7 0.1 collective-permute-start.4
  21.7 1.1 %collective-permute-done.4.refs_3_ = f32[8,128]{1,0:T(8,128)S(1)} collective-permute-done((f32[8,128]{1,0:T(8,128)S(1)}, f32[8,128]{1,0:T(8,128)S(1)}, u32[]{:S(2)}, u32[]{:S(2)}) %collective-permute-start.4) | collective-permute-done | bytes 4128 | tf_op jit(solution)/shard_map/ppermute | solution.py:603
  22.8 0.1 advance_inner.1.refs_2_
  23.0 0.4 %collective-permute-done.6.refs_5_ = f32[3,16,128]{2,1,0:T(8,128)S(1)} collective-permute-done((f32[3,16,128]{2,1,0:T(8,128)S(1)}, f32[3,16,128]{2,1,0:T(8,128)S(1)}, u32[]{:S(2)}, u32[]{:S(2)}) %collective-permute-start.6) | collective-permute-done | bytes 24608 | tf_op jit(solution)/shard_map/ppermute | solution.py:641
  23.4 0.7 %advance.1 = f32[3,8,16,128]{3,2,1,0:T(8,128)} custom-call(f32[3,8,16,128]{3,2,1,0:T(8,128)S(1)} %get-tuple-element.37.refs_0_, f32[2,16,128]{2,1,0:T(8,128)S(1)} %get-tuple-element.58.refs_1_, f32[3,6,16,128]{3,2,1,0:T(8,128)S(1)} %advance_inner.1.refs_2_, f32[3,16,128]{2,1,0:T(8,128)S(1)} %get-tuple-element.67.refs_3_, ...), custom_call_target="tpu_custom_call" | custom-call | tf_op jit(solution)/shard_map/advance/pallas_call | solution.py:585
  (1 shorter events, 0.0 us)
Async XLA Ops:
  3.0 1.5 %collective-permute-start.1 = (f32[8,128]{1,0:T(8,128)S(1)}, f32[8,128]{1,0:T(8,128)S(1)}, u32[]{:S(2)}, u32[]{:S(2)}) collective-permute-start(f32[8,128]{1,0:T(8,128)S(1)} %get-tuple-element.55), channel_id=1, source_target_pairs={{0,1},{1,0},{2,3},{3,2},{4,5},{5,4},{6,7},{7,6},{8,9},{9,8},{10,11... | collective-permute-start | bytes 12296 | tf_op jit(solution)/shard_map/ppermute | solution.py:603
  4.6 8.6 %collective-permute-start.2 = (f32[4,16,128]{2,1,0:T(8,128)S(1)}, f32[4,16,128]{2,1,0:T(8,128)S(1)}, u32[]{:S(2)}, u32[]{:S(2)}) collective-permute-start(f32[4,16,128]{2,1,0:T(8,128)S(1)} %get-tuple-element.56.refs_9_), channel_id=1, source_target_pairs={{0,2},{2,4},{4,6},{6,8},{8,10},{10,12},{12,14},{14,16},{16,18},{18... | collective-permute-start | bytes 98312 | tf_op jit(solution)/shard_map/ppermute | solution.py:641
  7.3 5.9 %collective-permute-start.3 = (f32[4,16,128]{2,1,0:T(8,128)S(1)}, f32[4,16,128]{2,1,0:T(8,128)S(1)}, u32[]{:S(2)}, u32[]{:S(2)}) collective-permute-start(f32[4,16,128]{2,1,0:T(8,128)S(1)} %get-tuple-element.57.refs_10_), channel_id=1, source_target_pairs={{2,0},{4,2},{6,4},{8,6},{10,8},{12,10},{14,12},{16,14},{18,16},{20... | collective-permute-start | bytes 98312 | tf_op jit(solution)/shard_map/ppermute | solution.py:641
  11.4 1.2 %collective-permute-start = (f32[8,128]{1,0:T(8,128)S(1)}, f32[8,128]{1,0:T(8,128)S(1)}, u32[]{:S(2)}, u32[]{:S(2)}) collective-permute-start(f32[8,128]{1,0:T(8,128)S(1)} %get-tuple-element.50.refs_2_), channel_id=1, source_target_pairs={{0,1},{1,0},{2,3},{3,2},{4,5},{5,4},{6,7},{7,6},{8,9},{9,8},{10,11... | collective-permute-start | bytes 12296 | tf_op jit(solution)/shard_map/ppermute | solution.py:603
  14.6 1.2 %collective-permute-start.5 = (f32[8,128]{1,0:T(8,128)S(1)}, f32[8,128]{1,0:T(8,128)S(1)}, u32[]{:S(2)}, u32[]{:S(2)}) collective-permute-start(f32[8,128]{1,0:T(8,128)S(1)} %get-tuple-element.66), channel_id=1, source_target_pairs={{0,1},{1,0},{2,3},{3,2},{4,5},{5,4},{6,7},{7,6},{8,9},{9,8},{10,11... | collective-permute-start | bytes 12296 | tf_op jit(solution)/shard_map/ppermute | solution.py:603
  15.9 7.5 %collective-permute-start.6 = (f32[3,16,128]{2,1,0:T(8,128)S(1)}, f32[3,16,128]{2,1,0:T(8,128)S(1)}, u32[]{:S(2)}, u32[]{:S(2)}) collective-permute-start(f32[3,16,128]{2,1,0:T(8,128)S(1)} %get-tuple-element.67.refs_3_), channel_id=1, source_target_pairs={{0,2},{2,4},{4,6},{6,8},{8,10},{10,12},{12,14},{14,16},{16,18},{18... | collective-permute-start | bytes 73736 | tf_op jit(solution)/shard_map/ppermute | solution.py:641
  16.3 7.1 %collective-permute-start.7 = (f32[3,16,128]{2,1,0:T(8,128)S(1)}, f32[3,16,128]{2,1,0:T(8,128)S(1)}, u32[]{:S(2)}, u32[]{:S(2)}) collective-permute-start(f32[3,16,128]{2,1,0:T(8,128)S(1)} %get-tuple-element.68.refs_4_), channel_id=1, source_target_pairs={{2,0},{4,2},{6,4},{8,6},{10,8},{12,10},{14,12},{16,14},{18,16},{20... | collective-permute-start | bytes 73736 | tf_op jit(solution)/shard_map/ppermute | solution.py:641
  21.7 1.2 %collective-permute-start.4 = (f32[8,128]{1,0:T(8,128)S(1)}, f32[8,128]{1,0:T(8,128)S(1)}, u32[]{:S(2)}, u32[]{:S(2)}) collective-permute-start(f32[8,128]{1,0:T(8,128)S(1)} %get-tuple-element.64.refs_2_), channel_id=1, source_target_pairs={{0,1},{1,0},{2,3},{3,2},{4,5},{5,4},{6,7},{7,6},{8,9},{9,8},{10,11... | collective-permute-start | bytes 12296 | tf_op jit(solution)/shard_map/ppermute | solution.py:603

commit v7 on v6

--- a/solution.py
+++ b/solution.py
@@ -399,28 +399,43 @@
     ]
 
 
+def one_wall_neighbour():
+    return len(wall_pairings(lax.axis_size("col"))) == 1
+
+
 def pack_edges(sum_ref, edge_ref):
     lane = lax.broadcasted_iota(jnp.int32, (8, LANES), 1)
     packed = jnp.zeros((8, LANES), F32)
+    alone = one_wall_neighbour()
+    col_odd, _, _ = positions()
     for slot, x, e, at in places(sum_ref):
         tile = sum_ref[slot, x, 8 * e : 8 * (e + 1), :]
-        packed = jnp.where(lane == 2 * at, pltpu.roll(tile, 2 * at, 1) if at else tile, packed)
-        packed = jnp.where(lane == 2 * at + 1, pltpu.roll(tile, (2 * at + 2) % LANES, 1), packed)
+        if alone:
+            packed = jnp.where(lane == at + 1, pltpu.roll(tile, at + 2 - col_odd, 1), packed)
+        else:
+            packed = jnp.where(lane == 2 * at, pltpu.roll(tile, 2 * at, 1) if at else tile, packed)
+            last = pltpu.roll(tile, (2 * at + 2) % LANES, 1)
+            packed = jnp.where(lane == 2 * at + 1, last, packed)
     edge_ref[...] = packed
 
 
 def with_edges(sum_ref, edge_refs):
     col_odd, _, _ = positions()
     lane = lax.broadcasted_iota(jnp.int32, (8, LANES), 1)
-    edges = jnp.zeros((8, LANES), F32)
-    for k, ref in enumerate(edge_refs):
-        edges = edges + jnp.where(lane % 2 == (col_odd + k) % 2, ref[...], 0.0)
-    meets = (lane == LANES - 1) | (lane == 0)
-    return {
-        (slot, x, e): sum_ref[slot, x, 8 * e : 8 * (e + 1), :]
-        + jnp.where(meets, pltpu.roll(edges, LANES - 1 - 2 * at, 1), 0.0)
-        for slot, x, e, at in places(sum_ref)
-    }
+    if one_wall_neighbour():
+        edges = edge_refs[0][...]
+        meets = lane == (LANES - 1) * (1 - col_odd)
+    else:
+        edges = jnp.zeros((8, LANES), F32)
+        for k, ref in enumerate(edge_refs):
+            edges = edges + jnp.where(lane % 2 == (col_odd + k) % 2, ref[...], 0.0)
+        meets = (lane == LANES - 1) | (lane == 0)
+    tiles = {}
+    for slot, x, e, at in places(sum_ref):
+        shift = LANES - 2 - at + col_odd if one_wall_neighbour() else LANES - 1 - 2 * at
+        add = jnp.where(meets, pltpu.roll(edges, shift, 1), 0.0)
+        tiles[slot, x, e] = sum_ref[slot, x, 8 * e : 8 * (e + 1), :] + add
+    return tiles
 
 
 def planes_kernel(count, *refs):

time: 24.2 us -> 24.2 us (level)
  no operation moved by 1% of the time
where the time goes in v7:
time: 24.2 us; the launch traced here: 24.1 us
  starting transfers between devices  13.2 us (55%)
  Pallas kernels  7.68 us (32%)
  waiting for transfers between devices  3.1 us (13%)
    ppermute x2, starting transfers between devices, exchange(): lax.ppermute(down, 'span', back_way)  9.37 us
    pallas_call x9, Pallas kernels, call(): pl.pallas_call(kernel, name=name, out_shape=[out_space(shape, dtype) for...  7.68 us
    ppermute x2, starting transfers between devices, exchange(): lax.ppermute(up, 'span', ahead)  3.19 us
    ppermute x4, waiting for transfers between devices, swap_edges(): lax.ppermute(edge, 'col', way)  2.41 us
    ppermute x2, waiting for transfers between devices, exchange(): lax.ppermute(up, 'span', ahead)  0.68 us
    ppermute x4, starting transfers between devices, swap_edges(): lax.ppermute(edge, 'col', way)  0.67 us
  transfers between devices with their start and end apart: 8, of which 5 were waited for; matrix products, arithmetic and copies ran while one was open for 0% of the time, Pallas kernels for 10%

profile of v7, /device:TPU:0, one launch (start us, length us, event | category | flops | bytes accessed | tf_op | source)
XLA Modules:
  0.0 24.1 jit_solution(17646101839621374709)
XLA Ops:
  0.0 3.0 %first_operator.1 = (f32[3,8,16,128]{3,2,1,0:T(8,128)S(1)}, bf16[864,128]{1,0:T(8,128)(2,1)S(1)}, bf16[960,128]{1,0:T(8,128)(2,1)S(1)}, bf16[6,256,128]{2,1,0:T(...) custom-call(f32[168,128]{1,0:T(8,128)} %constant.8.clone.refs_0_, ...), custom_call_target="tpu_custom_call" | custom-call | tf_op jit(solution)/shard_map/first_operator/pallas_call | solution.py:600
  3.0 0.5 %collective-permute-start.1 = (f32[8,128]{1,0:T(8,128)S(1)}, f32[8,128]{1,0:T(8,128)S(1)}, u32[]{:S(2)}, u32[]{:S(2)}) collective-permute-start(f32[8,128]{1,0:T(8,128)S(1)} %get-tuple-element.55), channel_id=1, source_target_pairs={{0,1},{1,0},{2,3},{3,2},{4,5},{5,4},{6,7},{7,6},{8,9},{9,8},{10,11... | collective-permute-start | bytes 12296 | tf_op jit(solution)/shard_map/ppermute | solution.py:618
  3.5 0.9 %inner_planes.2 = (f32[4,6,16,128]{3,2,1,0:T(8,128)S(1)}, f32[8,128]{1,0:T(8,128)S(1)}) custom-call(bf16[9,864,128]{2,1,0:T(8,128)(2,1)S(1)} %get-tuple-element.43.refs_0_, bf16[6,256,128]{2,1,0:T(8,128)(2,1)S(1)} %get-tuple-element.44.refs_1_, f32[6,64,128]{2,1,0:T(8,128)S(1)} %get-tuple-element.45.refs_2_, ...), custom_call_target="tpu_custom_call" | custom-call | tf_op jit(solution)/shard_map/inner_planes/pallas_call | solution.py:600
  4.5 0.0 collective-permute-done.1.refs_1_
  4.5 0.1 planes.2
  4.6 2.7 %collective-permute-start.2 = (f32[4,16,128]{2,1,0:T(8,128)S(1)}, f32[4,16,128]{2,1,0:T(8,128)S(1)}, u32[]{:S(2)}, u32[]{:S(2)}) collective-permute-start(f32[4,16,128]{2,1,0:T(8,128)S(1)} %get-tuple-element.56.refs_9_), channel_id=1, source_target_pairs={{0,2},{2,4},{4,6},{6,8},{8,10},{10,12},{12,14},{14,16},{16,18},{18... | collective-permute-start | bytes 98312 | tf_op jit(solution)/shard_map/ppermute | solution.py:656
  7.3 4.0 %collective-permute-start.3 = (f32[4,16,128]{2,1,0:T(8,128)S(1)}, f32[4,16,128]{2,1,0:T(8,128)S(1)}, u32[]{:S(2)}, u32[]{:S(2)}) collective-permute-start(f32[4,16,128]{2,1,0:T(8,128)S(1)} %get-tuple-element.57.refs_10_), channel_id=1, source_target_pairs={{2,0},{4,2},{6,4},{8,6},{10,8},{12,10},{14,12},{16,14},{18,16},{20... | collective-permute-start | bytes 98312 | tf_op jit(solution)/shard_map/ppermute | solution.py:656
  11.4 0.1 collective-permute-start
  11.4 1.1 %collective-permute-done.refs_3_ = f32[8,128]{1,0:T(8,128)S(1)} collective-permute-done((f32[8,128]{1,0:T(8,128)S(1)}, f32[8,128]{1,0:T(8,128)S(1)}, u32[]{:S(2)}, u32[]{:S(2)}) %collective-permute-start) | collective-permute-done | bytes 4128 | tf_op jit(solution)/shard_map/ppermute | solution.py:618
  12.5 0.4 %prepare.1 = (f32[6,16,128]{2,1,0:T(8,128)S(1)}, bf16[9,144,128]{2,1,0:T(8,128)(2,1)S(1)}, bf16[6,144,128]{2,1,0:T(8,128)(2,1)S(1)}, f32[6,48,128]{2,1,0:T(8,128)S(1)}) custom-call(f32[3,8,16,128]{3,2,1,0:T(8,128)S(1)} %get-tuple-element.37.refs_0_, bf16[6,256,128]{2,1,0:T(8,128)(2,1)S(1)} %get-tuple-element.38.refs_1_, ...), custom_call_target="tpu_custom_call" | custom-call | tf_op jit(solution)/shard_map/prepare/pallas_call | solution.py:600
  13.0 0.2 collective-permute-done.2.refs_11_
  13.2 0.0 collective-permute-done.3.refs_12_
  13.2 1.4 %second_operator.1 = (f32[2,16,128]{2,1,0:T(8,128)S(1)}, bf16[9,864,128]{2,1,0:T(8,128)(2,1)S(1)}, bf16[6,256,128]{2,1,0:T(8,128)(2,1)S(1)}, f32[6,64,128]{2,1,0...) custom-call(f32[3,8,16,128]{3,2,1,0:T(8,128)S(1)} %get-tuple-element.37.refs_0_, ...), custom_call_target="tpu_custom_call" | custom-call | tf_op jit(solution)/shard_map/second_operator/pallas_call | solution.py:600
  14.6 0.0 collective-permute-start.5
  14.6 1.0 %inner_planes.3 = (f32[3,6,16,128]{3,2,1,0:T(8,128)S(1)}, f32[8,128]{1,0:T(8,128)S(1)}) custom-call(bf16[9,864,128]{2,1,0:T(8,128)(2,1)S(1)} %get-tuple-element.60.refs_0_, bf16[6,256,128]{2,1,0:T(8,128)(2,1)S(1)} %get-tuple-element.61.refs_1_, f32[6,64,128]{2,1,0:T(8,128)S(1)} %get-tuple-element.62.refs_2_, ...), custom_call_target="tpu_custom_call" | custom-call | tf_op jit(solution)/shard_map/inner_planes/pallas_call | solution.py:600
  15.6 0.2 collective-permute-done.5.refs_1_
  15.8 0.1 planes.3
  15.8 0.5 %collective-permute-start.6 = (f32[3,16,128]{2,1,0:T(8,128)S(1)}, f32[3,16,128]{2,1,0:T(8,128)S(1)}, u32[]{:S(2)}, u32[]{:S(2)}) collective-permute-start(f32[3,16,128]{2,1,0:T(8,128)S(1)} %get-tuple-element.67.refs_3_), channel_id=1, source_target_pairs={{0,2},{2,4},{4,6},{6,8},{8,10},{10,12},{12,14},{14,16},{16,18},{18... | collective-permute-start | bytes 73736 | tf_op jit(solution)/shard_map/ppermute | solution.py:656
  16.3 5.3 %collective-permute-start.7 = (f32[3,16,128]{2,1,0:T(8,128)S(1)}, f32[3,16,128]{2,1,0:T(8,128)S(1)}, u32[]{:S(2)}, u32[]{:S(2)}) collective-permute-start(f32[3,16,128]{2,1,0:T(8,128)S(1)} %get-tuple-element.68.refs_4_), channel_id=1, source_target_pairs={{2,0},{4,2},{6,4},{8,6},{10,8},{12,10},{14,12},{16,14},{18,16},{20... | collective-permute-start | bytes 73736 | tf_op jit(solution)/shard_map/ppermute | solution.py:656
  21.6 0.0 collective-permute-start.4
  21.7 1.1 %collective-permute-done.4.refs_3_ = f32[8,128]{1,0:T(8,128)S(1)} collective-permute-done((f32[8,128]{1,0:T(8,128)S(1)}, f32[8,128]{1,0:T(8,128)S(1)}, u32[]{:S(2)}, u32[]{:S(2)}) %collective-permute-start.4) | collective-permute-done | bytes 4128 | tf_op jit(solution)/shard_map/ppermute | solution.py:618
  22.8 0.1 advance_inner.1.refs_2_
  22.9 0.5 %collective-permute-done.6.refs_5_ = f32[3,16,128]{2,1,0:T(8,128)S(1)} collective-permute-done((f32[3,16,128]{2,1,0:T(8,128)S(1)}, f32[3,16,128]{2,1,0:T(8,128)S(1)}, u32[]{:S(2)}, u32[]{:S(2)}) %collective-permute-start.6) | collective-permute-done | bytes 24608 | tf_op jit(solution)/shard_map/ppermute | solution.py:656
  23.4 0.7 %advance.1 = f32[3,8,16,128]{3,2,1,0:T(8,128)} custom-call(f32[3,8,16,128]{3,2,1,0:T(8,128)S(1)} %get-tuple-element.37.refs_0_, f32[2,16,128]{2,1,0:T(8,128)S(1)} %get-tuple-element.58.refs_1_, f32[3,6,16,128]{3,2,1,0:T(8,128)S(1)} %advance_inner.1.refs_2_, f32[3,16,128]{2,1,0:T(8,128)S(1)} %get-tuple-element.67.refs_3_, ...), custom_call_target="tpu_custom_call" | custom-call | tf_op jit(solution)/shard_map/advance/pallas_call | solution.py:600
  (1 shorter events, 0.0 us)
Async XLA Ops:
  3.0 1.5 %collective-permute-start.1 = (f32[8,128]{1,0:T(8,128)S(1)}, f32[8,128]{1,0:T(8,128)S(1)}, u32[]{:S(2)}, u32[]{:S(2)}) collective-permute-start(f32[8,128]{1,0:T(8,128)S(1)} %get-tuple-element.55), channel_id=1, source_target_pairs={{0,1},{1,0},{2,3},{3,2},{4,5},{5,4},{6,7},{7,6},{8,9},{9,8},{10,11... | collective-permute-start | bytes 12296 | tf_op jit(solution)/shard_map/ppermute | solution.py:618
  4.6 8.6 %collective-permute-start.2 = (f32[4,16,128]{2,1,0:T(8,128)S(1)}, f32[4,16,128]{2,1,0:T(8,128)S(1)}, u32[]{:S(2)}, u32[]{:S(2)}) collective-permute-start(f32[4,16,128]{2,1,0:T(8,128)S(1)} %get-tuple-element.56.refs_9_), channel_id=1, source_target_pairs={{0,2},{2,4},{4,6},{6,8},{8,10},{10,12},{12,14},{14,16},{16,18},{18... | collective-permute-start | bytes 98312 | tf_op jit(solution)/shard_map/ppermute | solution.py:656
  7.3 5.9 %collective-permute-start.3 = (f32[4,16,128]{2,1,0:T(8,128)S(1)}, f32[4,16,128]{2,1,0:T(8,128)S(1)}, u32[]{:S(2)}, u32[]{:S(2)}) collective-permute-start(f32[4,16,128]{2,1,0:T(8,128)S(1)} %get-tuple-element.57.refs_10_), channel_id=1, source_target_pairs={{2,0},{4,2},{6,4},{8,6},{10,8},{12,10},{14,12},{16,14},{18,16},{20... | collective-permute-start | bytes 98312 | tf_op jit(solution)/shard_map/ppermute | solution.py:656
  11.4 1.2 %collective-permute-start = (f32[8,128]{1,0:T(8,128)S(1)}, f32[8,128]{1,0:T(8,128)S(1)}, u32[]{:S(2)}, u32[]{:S(2)}) collective-permute-start(f32[8,128]{1,0:T(8,128)S(1)} %get-tuple-element.50.refs_2_), channel_id=1, source_target_pairs={{0,1},{1,0},{2,3},{3,2},{4,5},{5,4},{6,7},{7,6},{8,9},{9,8},{10,11... | collective-permute-start | bytes 12296 | tf_op jit(solution)/shard_map/ppermute | solution.py:618
  14.6 1.2 %collective-permute-start.5 = (f32[8,128]{1,0:T(8,128)S(1)}, f32[8,128]{1,0:T(8,128)S(1)}, u32[]{:S(2)}, u32[]{:S(2)}) collective-permute-start(f32[8,128]{1,0:T(8,128)S(1)} %get-tuple-element.66), channel_id=1, source_target_pairs={{0,1},{1,0},{2,3},{3,2},{4,5},{5,4},{6,7},{7,6},{8,9},{9,8},{10,11... | collective-permute-start | bytes 12296 | tf_op jit(solution)/shard_map/ppermute | solution.py:618
  15.8 7.5 %collective-permute-start.6 = (f32[3,16,128]{2,1,0:T(8,128)S(1)}, f32[3,16,128]{2,1,0:T(8,128)S(1)}, u32[]{:S(2)}, u32[]{:S(2)}) collective-permute-start(f32[3,16,128]{2,1,0:T(8,128)S(1)} %get-tuple-element.67.refs_3_), channel_id=1, source_target_pairs={{0,2},{2,4},{4,6},{6,8},{8,10},{10,12},{12,14},{14,16},{16,18},{18... | collective-permute-start | bytes 73736 | tf_op jit(solution)/shard_map/ppermute | solution.py:656
  16.3 7.1 %collective-permute-start.7 = (f32[3,16,128]{2,1,0:T(8,128)S(1)}, f32[3,16,128]{2,1,0:T(8,128)S(1)}, u32[]{:S(2)}, u32[]{:S(2)}) collective-permute-start(f32[3,16,128]{2,1,0:T(8,128)S(1)} %get-tuple-element.68.refs_4_), channel_id=1, source_target_pairs={{2,0},{4,2},{6,4},{8,6},{10,8},{12,10},{14,12},{16,14},{18,16},{20... | collective-permute-start | bytes 73736 | tf_op jit(solution)/shard_map/ppermute | solution.py:656
  21.6 1.2 %collective-permute-start.4 = (f32[8,128]{1,0:T(8,128)S(1)}, f32[8,128]{1,0:T(8,128)S(1)}, u32[]{:S(2)}, u32[]{:S(2)}) collective-permute-start(f32[8,128]{1,0:T(8,128)S(1)} %get-tuple-element.64.refs_2_), channel_id=1, source_target_pairs={{0,1},{1,0},{2,3},{3,2},{4,5},{5,4},{6,7},{7,6},{8,9},{9,8},{10,11... | collective-permute-start | bytes 12296 | tf_op jit(solution)/shard_map/ppermute | solution.py:618
